TPU v7x, 32 devices: a whole 2x2x4 slice. The times are simulated.
32 devices in a mesh: lane: 4 (over y, x), section: 2 (over core), tp: 4 (over z).
Axes of the slice: x: 2, y: 2, z: 4, core: 2. Of those that a mesh axis runs over, the one named last changes fastest.
Arguments:
- merge_hidden: bfloat16 [2048, 5120], P('lane', 'section'), may hold values from -6 to 6
- merge_weight: bfloat16 [5120, 8192], P('section', 'tp'), may hold values from -0.25 to 0.25
- merge_bias: float32 [8192], P('tp'), may hold values from -3 to 3
- row_dest: int32 [2048], P(('lane', 'section')), may hold values from -1 to 3, as said below
- image_pos: int32 [4, 2, 4, 4], P('lane', 'section'), may hold values from -1 to 255, as said below
- text_embed: bfloat16 [2048, 8192], P(('lane', 'section'), 'tp'), may hold values from -8 to 8
- norm_gain: float32 [8192], P('tp'), may hold values from 0.25 to 1.75
- kv_weight: bfloat16 [8192, 2048], P('tp'), may hold values from -0.0625 to 0.0625
- kv_grad: bfloat16 [2048, 2048], P(('lane', 'section')), may hold values from -6 to 6
Outputs:
- key_value: bfloat16 [2048, 2048], P(('lane', 'section'), 'tp')
- embed_grad: bfloat16 [2048, 8192], P(('lane', 'section'), 'tp')
- image_grad: bfloat16 [2048, 8192], P(('lane', 'section'), 'tp')
Inputs may be any that keep to these rules, and one draw needn't show every extreme that they name: `row_dest`: rows come in blocks of 256: block s of lane j is rows j * 512 + s * 256 onward. Rows of one block that go to one lane number at most 4; every block sends 4 rows to some lane, and for every s some lane receives 4 rows from block s of every lane. image_pos[l, s, j, k] is the position, among the 256 tokens of block s of lane l (tokens l * 512 + s * 256 onward), of the k-th row (in row order) that block s of lane j sends to lane l, and -1 where that block sends fewer than k + 1 rows to lane l; the positions taken in one block are distinct.
All inputs are finite; a program needn't handle non-finite values.
Results may differ from a plain program's by a relative error of at most 0.007.
Values may be sent and summed in bfloat16 or wider, within the bound.
No kernel may reach another device: no remote copies, remote signals or barrier semaphores. Data moves between devices by JAX's collectives and lax.ppermute only.
A program may use at most 64 MiB of HBM per device.

v0:
```python
import jax
import jax.numpy as jnp
from jax import lax
from jax.sharding import PartitionSpec as P

D = 8192


EPSILON = 1e-06


def on_device(
    merge_hidden,
    merge_weight,
    merge_bias,
    row_dest,
    image_pos,
    text_embed,
    norm_gain,
    kv_weight,
    kv_grad,
):
    lane_count = lax.axis_size("lane")
    tp_count = lax.axis_size("tp")
    slot_count = image_pos.shape[3]
    tokens = text_embed.shape[0]
    activated = jax.nn.gelu(merge_hidden.astype(jnp.float32), approximate=False).astype(
        jnp.bfloat16
    )
    merged = lax.psum_scatter(
        jnp.dot(activated, merge_weight, preferred_element_type=jnp.float32).astype(jnp.bfloat16),
        "section",
        scatter_dimension=0,
        tiled=True,
    ).astype(jnp.float32)
    image_block = (merged + merge_bias).astype(jnp.bfloat16)
    lane_ids = jnp.arange(lane_count, dtype=jnp.int32)
    matches = (row_dest[:, None] == lane_ids[None, :]).astype(jnp.int32)
    before = jnp.cumsum(matches, axis=0) - matches
    row_rank = jnp.sum(before * matches, axis=1)
    slot_ids = jnp.where(row_dest >= 0, row_dest * slot_count + row_rank, -1)
    send_table = (
        slot_ids[:, None] == jnp.arange(lane_count * slot_count, dtype=jnp.int32)[None, :]
    ).astype(jnp.bfloat16)
    outgoing = jnp.dot(send_table.T, image_block, preferred_element_type=jnp.float32).astype(
        jnp.bfloat16
    )
    arrived = lax.all_to_all(
        outgoing.reshape(lane_count, slot_count, -1),
        "lane",
        split_axis=0,
        concat_axis=0,
        tiled=True,
    )
    positions = image_pos.reshape(-1)
    place_match = positions[None, :] == jnp.arange(tokens, dtype=jnp.int32)[:, None]
    is_image = jnp.any(place_match, axis=1)
    place_table = place_match.astype(jnp.bfloat16)
    image_part = jnp.dot(
        place_table,
        arrived.reshape(lane_count * slot_count, -1),
        preferred_element_type=jnp.float32,
    ).astype(jnp.bfloat16)
    stream = jnp.where(is_image[:, None], image_part, text_embed)
    widened = stream.astype(jnp.float32)
    squares = jnp.sum(widened * widened, axis=1)
    normed_grad = lax.dot_general(
        kv_grad, kv_weight, (((1,), (1,)), ((), ())), preferred_element_type=jnp.float32
    )
    dot_terms = jnp.sum(widened * norm_gain * normed_grad, axis=1)
    total_squares, total_dots = lax.psum((squares, dot_terms), "tp")
    inv_rms = lax.rsqrt(total_squares / D + EPSILON)[:, None]
    normed = (widened * inv_rms * norm_gain).astype(jnp.bfloat16)
    col_size = kv_weight.shape[1] // tp_count
    product = jnp.dot(normed, kv_weight, preferred_element_type=jnp.float32)
    kv_block = lax.psum_scatter(
        jnp.transpose(product.reshape(tokens, 1 * lax.axis_size("tp"), col_size), (1, 0, 2)),
        "tp",
        scatter_dimension=0,
        tiled=True,
    )[0]
    key_value = kv_block.astype(jnp.bfloat16)
    embed_wide = inv_rms * norm_gain * normed_grad - widened * inv_rms**3 * total_dots[:, None] / D
    embed_grad = embed_wide.astype(jnp.bfloat16)
    returning = jnp.dot(place_table.T, embed_grad, preferred_element_type=jnp.float32).astype(
        jnp.bfloat16
    )
    returned = lax.all_to_all(
        returning.reshape(lane_count, slot_count, -1),
        "lane",
        split_axis=0,
        concat_axis=0,
        tiled=True,
    )
    image_grad = jnp.dot(
        send_table,
        returned.reshape(lane_count * slot_count, -1),
        preferred_element_type=jnp.float32,
    ).astype(jnp.bfloat16)
    return (key_value, embed_grad, image_grad)


def solution(mesh):
    in_specs = (
        P("lane", "section"),
        P("section", "tp"),
        P("tp"),
        P(("lane", "section")),
        P("lane", "section", None, None),
        P(("lane", "section"), "tp"),
        P("tp"),
        P("tp", None),
        P(("lane", "section"), None),
    )
    out_specs = (
        P(("lane", "section"), "tp"),
        P(("lane", "section"), "tp"),
        P(("lane", "section"), "tp"),
    )
    return jax.shard_map(
        on_device, mesh=mesh, in_specs=in_specs, out_specs=out_specs, check_vma=False
    )
```

profile of v0, /device:TPU:0, one launch (start us, length us, event | category | flops | bytes accessed | tf_op | source)
XLA Modules:
  0.0 128.4 jit_solution(10511445072433306503)
XLA Ops:
  7.2 0.0 copy-start
  7.2 0.0 reduce-scatter.3.cloned.1.call-start
  7.3 21.5 %convolution_convert_fusion = bf16[512,2048]{1,0:T(8,128)(2,1)} fusion(bf16[2560,2048]{1,0:T(8,128)(2,1)} %param.10, bf16[512,2560]{1,0:T(8,128)(2,1)} %param.9), kind=kOutput, calls=%fused_computation.38 | convolution fusion | flops 5456265216 | bytes 15204352 | tf_op jit(solution)/shard_map/dot_general | solution.py:31
  28.8 0.0 reduce-scatter.3.cloned.1.call-update
  28.8 0.0 copy-done.6
  28.8 0.1 eq.51
  28.9 1.2 reduce-window.6
  30.1 0.1 slice.8
  30.2 0.1 copy.15
  30.3 0.1 copy.16
  30.4 0.1 add_bitcast_fusion
  30.6 10.7 %reduce-scatter.3.cloned.1.call-done = bf16[256,2048]{1,0:T(8,128)(2,1)} async-done(((bf16[512,2048]{1,0:T(8,128)(2,1)}), bf16[256,2048]{1,0:T(8,128)(2,1)}) %reduce-scatter.3.cloned.1.call-update) | async-done | bytes 1048592 | tf_op jit(solution)/shard_map/reduce_scatter | solution.py:30
  41.3 0.0 copy-done.4
  41.3 1.6 %convolution_convert_fusion.4 = bf16[16,2048]{1,0:T(8,128)(2,1)S(1)} fusion(bf16[256,2048]{1,0:T(8,128)(2,1)} %reduce-scatter.3.cloned.1.call-done, f32[2048]{0:T(1024)S(1)} %copy-done.4, s32[256]{0:T(256)S(1)} %compare_select_fusion), kind=kOutput, calls=%fused_computation.73 | convolution fusion | flops 18386944 | bytes 1123328 | tf_op jit(solution)/shard_map/dot_general | solution.py:45
  42.8 0.7 reshape.49
  43.5 3.9 %all-to-all-start = ((bf16[4,4,2048]{2,1,0:T(4,128)(2,1)}), bf16[4,4,2048]{2,1,0:T(4,128)(2,1)S(1)}, u32[]{:S(2)}, u32[]{:S(2)}) async-start(bf16[4,4,2048]{2,1,0:T(4,128)(2,1)} %reshape.49), calls=%async_computation.1 | async-start | bytes 131072 | tf_op jit(solution)/shard_map/all_to_all | solution.py:48
  47.4 0.0 reduce-scatter.5.cloned.1.call-start
  47.4 0.1 fusion.79
  47.5 4.8 %all-to-all-done = bf16[4,4,2048]{2,1,0:T(4,128)(2,1)S(1)} async-done(((bf16[4,4,2048]{2,1,0:T(4,128)(2,1)}), bf16[4,4,2048]{2,1,0:T(4,128)(2,1)S(1)}, u32[]{:S(2)}, u32[]{:S(2)}) %all-to-all-start) | async-done | bytes 65568 | tf_op jit(solution)/shard_map/all_to_all | solution.py:48
  52.3 0.5 fusion.62
  52.9 7.1 %fusion.71 = (f32[256]{0:T(256)S(1)}, f32[256]{0:T(256)S(1)}, f32[256,2048]{1,0:T(8,128)}) fusion(bf16[256,2048]{1,0:T(8,128)(2,1)S(1)} %fusion.62, f32[2048]{0:T(1024)S(1)} %copy-done.5, bf16[256,2048]{1,0:T(8,128)(2,1)S(1)} %copy-done, bf16[2048,2048]{1,0:T(8,128)(2,1)} %param.16), kind=kOutput, calls=%fused_computation.82 | convolution fusion | flops 2150628864 | bytes 12593152 | tf_op jit(solution)/shard_map/dot_general | solution.py:67
  60.0 11.9 %all-reduce = (f32[256]{0:T(256)S(1)}, f32[256]{0:T(256)S(1)}) all-reduce(f32[256]{0:T(256)S(1)} %get-tuple-element.4, f32[256]{0:T(256)S(1)} %get-tuple-element.3), channel_id=1, replica_groups=mesh['lane'=4,'section'=2,'tp'=4] {'tp'}, use_global_device_ids=true, to_apply=%region_6.7 | all-reduce | flops 512 | bytes 4096 | tf_op jit(solution)/shard_map/psum | solution.py:71
  71.9 5.8 %fusion.72 = f32[256,2048]{1,0:T(8,128)S(1)} fusion(bf16[2048,2048]{1,0:T(8,128)(2,1)} %param.16, bf16[256,2048]{1,0:T(8,128)(2,1)S(1)} %fusion.62, f32[2048]{0:T(1024)S(1)} %copy-done.5, f32[256]{0:T(256)S(1)} %get-tuple-element.8), kind=kOutput, calls=%fused_computation.85 | convolution fusion | flops 2149580800 | bytes 11543552 | tf_op jit(solution)/shard_map/dot_general | solution.py:75
  77.6 1.5 %copy.22 = f32[32,4,8,512]{3,2,0,1:T(8,128)} copy(f32[32,4,8,512]{3,2,1,0:T(8,128)S(1)} %bitcast.37) | data formatting | bytes 4194304 | tf_op jit(solution)/shard_map/reshape | solution.py:77
  79.1 0.0 reduce-scatter.5.cloned.1.call-update
  79.1 2.2 %fusion.69 = bf16[256,2048]{1,0:T(8,128)(2,1)S(1)} fusion(bf16[256,2048]{1,0:T(8,128)(2,1)S(1)} %fusion.62, f32[256,2048]{1,0:T(8,128)} %get-tuple-element.9, f32[256]{0:T(256)S(1)} %get-tuple-element.6, f32[256]{0:T(256)S(1)} %get-tuple-element.7, f32[2048]{0:T(1024)S(1)} %copy-done.5, f32[256]{0:T(256)S(1)} %get-tuple-element.8), kind=kLoop, calls=%fused_computation.80 | loop fusion | flops 4194304 | bytes 4205568 | tf_op jit(solution)/shard_map/convert_element_type | solution.py:84
  81.3 0.0 copy-start.1
  81.4 0.3 convolution_convert_fusion.3
  81.7 7.2 %all_to_all.10 = bf16[4,4,2048]{2,1,0:T(4,128)(2,1)S(1)} all-to-all(bf16[4,4,2048]{2,1,0:T(4,128)(2,1)S(1)} %reshape.52), channel_id=1, replica_groups=mesh['lane'=4,'section'=2,'tp'=4] {'lane'}, dimensions={0} | all-to-all | bytes 131072 | tf_op jit(solution)/shard_map/all_to_all | solution.py:88
  88.9 1.4 %convolution_convert_fusion.2 = bf16[256,2048]{1,0:T(8,128)(2,1)} fusion(bf16[16,2048]{1,0:T(8,128)(2,1)S(1)} %reshape.53, s32[256]{0:T(256)S(1)} %compare_select_fusion), kind=kOutput, calls=%fused_computation.70 | convolution fusion | flops 17305600 | bytes 1115136 | tf_op jit(solution)/shard_map/dot_general | solution.py:95
  90.4 29.4 %reduce-scatter.5.cloned.1.call-done = f32[1,256,512]{2,1,0:T(8,128)} async-done(((f32[4,256,512]{2,1,0:T(8,128)}), f32[1,256,512]{2,1,0:T(8,128)}) %reduce-scatter.5.cloned.1.call-update) | async-done | bytes 524304 | tf_op jit(solution)/shard_map/reduce_scatter | solution.py:76
  119.7 1.8 %convert_bitcast_fusion = bf16[256,512]{1,0:T(8,128)(2,1)} fusion(f32[1,256,512]{2,1,0:T(8,128)} %reduce-scatter.5.cloned.1.call-done), kind=kLoop, calls=%fused_computation.89 | loop fusion | flops 131072 | bytes 786432 | tf_op jit(solution)/shard_map/convert_element_type | solution.py:82
  (19 shorter events, 0.2 us)
Async XLA Ops:
  7.2 45.7 %copy-start = (bf16[256,2048]{1,0:T(8,128)(2,1)S(1)}, bf16[256,2048]{1,0:T(8,128)(2,1)}, u32[]{:S(2)}) copy-start(bf16[256,2048]{1,0:T(8,128)(2,1)} %param.17) | copy-start | bytes 3145732
  7.2 21.6 %copy-start.6 = (s32[1,1,4,4]{3,2,1,0:T(4,128)S(1)}, s32[1,1,4,4]{3,2,1,0:T(4,128)}, u32[]{:S(2)}) copy-start(s32[1,1,4,4]{3,2,1,0:T(4,128)} %param.13) | copy-start | bytes 196
  7.2 21.7 %copy-start.3 = (s32[256]{0:T(256)S(1)}, s32[256]{0:T(256)}, u32[]{:S(2)}) copy-start(s32[256]{0:T(256)} %param.12) | copy-start | bytes 3076
  7.2 34.1 %copy-start.4 = (f32[2048]{0:T(1024)S(1)}, f32[2048]{0:T(1024)}, u32[]{:S(2)}) copy-start(f32[2048]{0:T(1024)} %param.11) | copy-start | bytes 24580
  7.2 45.1 %copy-start.2 = (bf16[256,2048]{1,0:T(8,128)(2,1)S(1)}, bf16[256,2048]{1,0:T(8,128)(2,1)}, u32[]{:S(2)}) copy-start(bf16[256,2048]{1,0:T(8,128)(2,1)} %param.14) | copy-start | bytes 3145732
  7.2 34.0 %reduce-scatter.3.cloned.1.call-start = ((), (), s32[]{:S(2)}) async-start(), calls=%async_computation.4 | async-start | bytes 3145728 | tf_op jit(solution)/shard_map/reduce_scatter | solution.py:30
  28.8 24.1 %copy-start.5 = (f32[2048]{0:T(1024)S(1)}, f32[2048]{0:T(1024)}, u32[]{:S(2)}) copy-start(f32[2048]{0:T(1024)} %param.15) | copy-start | bytes 24580
  43.5 8.7 %all-to-all-start = ((bf16[4,4,2048]{2,1,0:T(4,128)(2,1)}), bf16[4,4,2048]{2,1,0:T(4,128)(2,1)S(1)}, u32[]{:S(2)}, u32[]{:S(2)}) async-start(bf16[4,4,2048]{2,1,0:T(4,128)(2,1)} %reshape.49), calls=%async_computation.1 | async-start | bytes 131072 | tf_op jit(solution)/shard_map/all_to_all | solution.py:48
  47.4 72.3 %reduce-scatter.5.cloned.1.call-start = ((), (), s32[]{:S(2)}) async-start(), calls=%async_computation.5 | async-start | bytes 2621440 | tf_op jit(solution)/shard_map/reduce_scatter | solution.py:76
  81.3 40.2 %copy-start.1 = (bf16[256,2048]{1,0:T(8,128)(2,1)}, bf16[256,2048]{1,0:T(8,128)(2,1)S(1)}, u32[]{:S(2)}) copy-start(bf16[256,2048]{1,0:T(8,128)(2,1)S(1)} %fusion.69) | copy-start | bytes 3145732
Sparse Core Ops, SparseCore 0:
  28.9 12.2 reduce-scatter.2
  79.3 40.4 reduce-scatter.4
where the time goes:
time: 129 us; the launch traced here: 128 us
  waiting for transfers between devices  44.9 us (35%)
  matrix products  38.2 us (30%)
  blocking collectives  19.1 us (15%)
  between operations  14.2 us (11%)
  other arithmetic  5.44 us (4%)
  starting transfers between devices  3.94 us (3%)
  local copies, waits for them, and re-layouts  2.65 us (2%)
    reduce_scatter x1, waiting for transfers between devices, on_device(): lax.psum_scatter(jnp.transpose(product.reshape(tokens, 1 * lax.axis_size(...  29.4 us
    dot_general x1, matrix products, on_device(): jnp.dot(activated, merge_weight, preferred_element_type=jnp.float32)  21.5 us
    psum x1, blocking collectives, on_device(): total_squares, total_dots = lax.psum((squares, dot_terms), 'tp')  11.9 us
    reduce_scatter x1, waiting for transfers between devices, on_device(): lax.psum_scatter(jnp.dot(activated, merge_weight, preferred_element_type=...  10.7 us
    all_to_all x1, blocking collectives, on_device(): lax.all_to_all(returning.reshape(lane_count, slot_count, -1), 'lane', spl...  7.21 us
    dot_general x1, matrix products, on_device(): lax.dot_general(kv_grad, kv_weight, (((1,), (1,)), ((), ())), preferred_e...  7.13 us
    dot_general x1, matrix products, on_device(): product = jnp.dot(normed, kv_weight, preferred_element_type=jnp.float32)  5.76 us
    all_to_all x1, waiting for transfers between devices, on_device(): lax.all_to_all(outgoing.reshape(lane_count, slot_count, -1), 'lane', spli...  4.75 us
  transfers between devices with their start and end apart: 3, of which 3 were waited for; matrix products, arithmetic and copies ran while one was open for 5% of the time, Pallas kernels for 0%

commit v1 on v0

v1 whole, which is shorter than its diff:
```python
import math

import jax
import jax.numpy as jnp
import numpy as np
from jax import lax
from jax.experimental import pallas as pl
from jax.experimental.pallas import tpu as pltpu
from jax.sharding import PartitionSpec as P

EPSILON = 1e-06
F32 = jnp.float32
BF16 = jnp.bfloat16
MIB = 1 << 20
VMEM = pl.BlockSpec(memory_space=pltpu.VMEM)
ANY = pl.BlockSpec(memory_space=pl.ANY)
SMEM = pl.BlockSpec(memory_space=pltpu.SMEM)


def round_up(value, step):
    return -(-value // step) * step


def dot(a, b):
    return jnp.dot(a, b, preferred_element_type=F32)


def dot_dims(a, b, dim_a, dim_b):
    return lax.dot_general(a, b, (((dim_a,), (dim_b,)), ((), ())), preferred_element_type=F32)


def iota(shape, dim):
    return lax.broadcasted_iota(jnp.int32, shape, dim)


def one_hot(column, width):
    return (column == iota((column.shape[0], width), 1)).astype(F32).astype(BF16)


def text_kernel(tp_count, order_ref, text_hbm, gain_ref, grad_hbm, weight_hbm, *refs):
    parts = refs[:tp_count]
    weight, sums, text, grad, weight_sem, row_sem = refs[tp_count:]
    cols = weight.shape[1] // tp_count
    text_copy = pltpu.make_async_copy(text_hbm, text, row_sem.at[0])
    grad_copy = pltpu.make_async_copy(grad_hbm, grad, row_sem.at[1])
    text_copy.start()
    copies = []
    for k in range(tp_count):
        span = pl.ds(pl.multiple_of(order_ref[k] * cols, cols), cols)
        copy = pltpu.make_async_copy(weight_hbm.at[:, span], weight.at[:, span], weight_sem.at[k])
        copy.start()
        copies.append(copy)
        if k == 0:
            grad_copy.start()
    text_copy.wait()
    wide = text[...].astype(F32)
    squares = jnp.sum(wide * wide, axis=1, keepdims=True)
    scaled = (wide * gain_ref[...]).astype(BF16)
    dots = jnp.zeros_like(squares)
    grad_copy.wait()
    for k in range(tp_count):
        span = pl.ds(pl.multiple_of(order_ref[k] * cols, cols), cols)
        copies[k].wait()
        part = dot(scaled, weight[:, span])
        parts[k][...] = part.astype(parts[k].dtype)
        dots = dots + jnp.sum(part * grad[:, span].astype(F32), axis=1, keepdims=True)
    lane = iota((text.shape[0], 128), 1)
    sums[...] = jnp.where(lane == 0, squares, jnp.where(lane == 1, dots, 0.0)).T[:8]


def gather_kernel(group, cap, section_ref, own_ref, other_ref, pos_ref, slot_ref, hidden, grad, payload, send_table):
    rows = payload.shape[0]
    block = own_ref.shape[1]
    row_id = iota((rows, block), 0)
    shift = int(math.log2(group))
    lane_id = row_id >> shift
    place = row_id & (group - 1)
    earlier = (iota((block, block), 0) < iota((block, block), 1)).astype(F32).astype(BF16)

    def select(dest, first):
        match = dest == lane_id
        rank = dot(match.astype(F32).astype(BF16), earlier)
        return (match & (rank == (place - first).astype(F32))).astype(F32).astype(BF16)

    own = select(own_ref[...], 0)
    other = select(other_ref[...], cap)
    section = section_ref[0]
    own_rows = pl.ds(pl.multiple_of(section * block, block), block)
    other_rows = pl.ds(pl.multiple_of((1 - section) * block, block), block)
    picked = dot(own, hidden[own_rows, :]) + dot(other, hidden[other_rows, :])
    active = 0.5 * picked * (1.0 + lax.erf(picked * np.float32(math.sqrt(0.5))))
    grad_rows = dot(one_hot(pos_ref[...], block), grad[...])
    width = grad_rows.shape[1]
    payload[:, :width] = (active[:, :width] + grad_rows).astype(BF16)
    if width < payload.shape[1]:
        payload[:, width:] = active[:, width:].astype(BF16)
    send_table[...] = dot(one_hot(slot_ref[...], rows), own).astype(BF16)


def merge_kernel(cap, slot_ref, got, sent, weight, own, other, grad_rows):
    rows = got.shape[0]
    width = grad_rows.shape[1]
    slots = slot_ref.shape[0]
    first = one_hot(slot_ref[...], rows)
    second = one_hot(slot_ref[...] + cap, rows)
    third = one_hot(slot_ref[...] + 2 * cap, rows)
    picked = jnp.concatenate(
        [dot(first, got[...]), dot(first, sent[...]), dot(second, got[...]), dot(second, sent[...])], axis=0
    ).astype(BF16)
    grad_rows[:slots] = dot(third, sent[:, :width]).astype(BF16)
    grad_rows[slots:] = dot(third, got[:, :width]).astype(BF16)
    cols = weight.shape[1]
    step = min(512, cols)
    for c in range(0, cols, step):
        total = dot(picked, weight[:, c : c + step])
        own[:, c : c + step] = total[: 2 * slots]
        other[:, c : c + step] = total[2 * slots :].astype(BF16)


def slot_kernel(tp_count, sum_rows, own, other, bias, gain, weight, grad_rows, text_sums, rows, payload):
    slots2 = own.shape[0]
    slots = slots2 // 2
    placed = (own[...] + other[...].astype(F32) + bias[...]).astype(BF16)
    rows[...] = placed
    wide = placed.astype(F32)
    squares = jnp.sum(wide * wide, axis=1, keepdims=True)
    scaled = (wide * gain[...]).astype(BF16)
    cols = payload.shape[1]
    height = slots + sum_rows
    dots = jnp.zeros_like(squares)
    for d in range(tp_count):
        part = dot(scaled, weight[:, d * cols : (d + 1) * cols])
        dots = dots + jnp.sum(part * grad_rows[:, d * cols : (d + 1) * cols].astype(F32), axis=1, keepdims=True)
        payload[d * height : d * height + slots] = part[:slots].astype(BF16)
    lane = iota((slots2, 128), 1)
    columns = jnp.where(lane == 0, squares, jnp.where(lane == 1, dots, 0.0))
    padded = round_up(slots2, 128)
    if padded > slots2:
        columns = jnp.concatenate([columns, jnp.zeros((padded - slots2, 128), F32)], axis=0)
    turned = columns.T
    pieces = []
    for i in range(2):
        total = jnp.concatenate([text_sums[i : i + 1], turned[i : i + 1]], axis=1)
        high = total.astype(BF16).astype(F32)
        pieces += [high, total - high]
    line = jnp.concatenate(pieces, axis=1)
    message = jnp.zeros((sum_rows, cols), F32)
    sublane = iota((sum_rows, cols), 0)
    for i in range(line.shape[1] // cols):
        message = jnp.where(sublane == i, line[:, i * cols : (i + 1) * cols], message)
    message = message.astype(BF16)
    for d in range(tp_count):
        payload[d * height + slots : (d + 1) * height] = message


def grad_kernel(grad, grad_rows, weight, out):
    tokens = grad.shape[0]
    step = min(512, weight.shape[0])
    for c in range(0, weight.shape[0], step):
        piece = weight[c : c + step, :]
        out[:tokens, c : c + step] = dot_dims(grad[...], piece, 1, 1)
        out[tokens:, c : c + step] = dot_dims(grad_rows[...], piece, 1, 1)


def final_kernel(
    tp_count, features, got, rows, normed_grad, text, gain, place_table, send_table, embed_grad, image_grad, kv_rows, inv_out
):
    slots2 = rows.shape[0]
    slots = slots2 // 2
    tokens, cols = text.shape[0], got.shape[1]
    height = got.shape[0] // tp_count
    total = got[:height].astype(F32)
    for d in range(1, tp_count):
        total = total + got[d * height : (d + 1) * height].astype(F32)
    span = tokens + round_up(slots2, 128)
    line = jnp.concatenate([total[slots + i : slots + i + 1] for i in range(4 * span // cols)], axis=1)
    squares = line[:, :span] + line[:, span : 2 * span]
    dots = line[:, 2 * span : 3 * span] + line[:, 3 * span :]
    inv = lax.rsqrt(squares / features + EPSILON)
    slope = inv * inv * inv * dots / features
    sublane = iota((128, span), 0)
    turned = jnp.where(sublane == 0, inv, jnp.where(sublane == 1, slope, 0.0)).T
    inv_col, slope_col = turned[:, 0:1], turned[:, 1:2]
    inv_out[...] = jnp.broadcast_to(inv_col[:tokens], inv_out.shape)
    kv_rows[...] = (total[:slots] * inv_col[tokens : tokens + slots]).astype(BF16)
    is_image = jnp.sum(place_table[...].astype(F32), axis=1, keepdims=True) > 0.0
    step = min(512, text.shape[1])
    for c in range(0, text.shape[1], step):
        cut = slice(c, c + step)
        row_grad = (
            inv_col[tokens : tokens + slots2] * gain[:, cut] * normed_grad[tokens:, cut]
            - rows[:, cut].astype(F32) * slope_col[tokens : tokens + slots2]
        ).astype(BF16)
        token_grad = inv_col[:tokens] * gain[:, cut] * normed_grad[:tokens, cut] - text[:, cut].astype(F32) * slope_col[:tokens]
        embed_grad[:, cut] = jnp.where(is_image, dot(place_table[...], row_grad[:slots]), token_grad).astype(BF16)
        image_grad[:, cut] = dot_dims(send_table[...], row_grad[slots:], 0, 0).astype(BF16)


def key_value_kernel(count, *refs):
    parts, (inv, place_table, kv_rows, out) = refs[:count], refs[count:]
    total = parts[0][...].astype(F32)
    for part in parts[1:]:
        total = total + part[...].astype(F32)
    is_image = jnp.sum(place_table[...].astype(F32), axis=1, keepdims=True) > 0.0
    out[...] = jnp.where(is_image, dot(place_table[...], kv_rows[...]), total * inv[:, 0:1]).astype(BF16)


def params(mib):
    return pltpu.CompilerParams(vmem_limit_bytes=mib * MIB)


def shape(dims, dtype):
    return jax.ShapeDtypeStruct(dims, dtype)


def on_device(
    merge_hidden, merge_weight, merge_bias, row_dest, image_pos, text_embed, norm_gain, kv_weight, kv_grad
):
    lane_count, tp_count = lax.axis_size("lane"), lax.axis_size("tp")
    tp_id = lax.axis_index("tp")
    section_id = lax.axis_index("section")
    tokens, features = text_embed.shape
    kv_cols = kv_weight.shape[1]
    cols = kv_cols // tp_count
    cap = image_pos.shape[3]
    slots = lane_count * cap
    slots2 = 2 * slots
    group = max(16, 1 << (3 * cap - 1).bit_length())
    rows = lane_count * group
    width = max(merge_hidden.shape[1], kv_cols)
    block = row_dest.shape[0]
    gain = norm_gain.reshape(1, features)
    bias = merge_bias.reshape(1, features)

    own_dest = row_dest.reshape(1, block)
    other_dest = lax.ppermute(own_dest, "section", [(0, 1), (1, 0)])

    steps = sorted(range(tp_count), key=lambda k: -k)
    order = jnp.stack([tp_id ^ k for k in steps]).astype(jnp.int32)
    *parts, weight, text_sums = pl.pallas_call(
        lambda *refs: text_kernel(tp_count, *refs),
        out_shape=[shape((tokens, cols), F32 if k == 0 else BF16) for k in steps]
        + [pltpu.VMEM(kv_weight.shape, BF16), shape((8, tokens), F32)],
        in_specs=[SMEM, ANY, VMEM, ANY, ANY],
        out_specs=[VMEM] * (tp_count + 2),
        scratch_shapes=[
            pltpu.VMEM(text_embed.shape, BF16),
            pltpu.VMEM(kv_grad.shape, BF16),
            pltpu.SemaphoreType.DMA((tp_count,)),
            pltpu.SemaphoreType.DMA((2,)),
        ],
        compiler_params=params(24),
        name="text_kv",
    )(order, text_embed, gain, kv_grad, kv_weight)
    arrived = [parts[-1]]
    for k, part in zip(steps[:-1], parts[:-1]):
        arrived.append(lax.ppermute(part, "tp", [(i, i ^ k) for i in range(tp_count)]))

    slot_rows = np.arange(slots, dtype=np.int32)
    slot_rows = jnp.asarray((slot_rows // cap * group + slot_rows % cap)[:, None])
    positions = image_pos.reshape(lane_count, cap)
    pos_column = jnp.pad(positions, ((0, 0), (2 * cap, group - 3 * cap)), constant_values=-1).reshape(rows, 1)
    place_table = (positions.reshape(1, slots) == jnp.arange(tokens, dtype=jnp.int32)[:, None]).astype(BF16)
    sent, send_table = pl.pallas_call(
        lambda *refs: gather_kernel(group, cap, *refs),
        out_shape=[shape((rows, width), BF16), shape((slots, block), BF16)],
        in_specs=[SMEM] + [VMEM] * 6,
        out_specs=[VMEM] * 2,
        compiler_params=params(24),
        name="gather_rows",
    )(section_id.astype(jnp.int32).reshape(1), own_dest, other_dest, pos_column, slot_rows, merge_hidden, kv_grad)
    got = lax.all_to_all(sent, "lane", 0, 0, tiled=True)

    own, other, grad_rows = pl.pallas_call(
        lambda *refs: merge_kernel(cap, *refs),
        out_shape=[shape((slots2, features), F32), shape((slots2, features), BF16), shape((slots2, kv_cols), BF16)],
        in_specs=[VMEM] * 4,
        out_specs=[VMEM] * 3,
        compiler_params=params(32),
        name="merge_rows",
    )(slot_rows, got, sent, merge_weight)
    other = lax.ppermute(other, "section", [(0, 1), (1, 0)])

    span = tokens + round_up(slots2, 128)
    sum_rows = round_up(-(-4 * span // cols), 16)
    placed, message = pl.pallas_call(
        lambda *refs: slot_kernel(tp_count, sum_rows, *refs),
        out_shape=[shape((slots2, features), BF16), shape((tp_count * (slots + sum_rows), cols), BF16)],
        in_specs=[VMEM] * 7,
        out_specs=[VMEM] * 2,
        compiler_params=params(24),
        name="slot_kv",
    )(own, other, bias, gain, weight, grad_rows, text_sums)
    messages = lax.all_to_all(message, "tp", 0, 0, tiled=True)

    normed_grad = pl.pallas_call(
        grad_kernel,
        out_shape=shape((tokens + slots2, features), F32),
        in_specs=[VMEM] * 3,
        out_specs=VMEM,
        compiler_params=params(24),
        name="normed_grad",
    )(kv_grad, grad_rows, weight)

    embed_grad, image_grad, kv_rows, inv = pl.pallas_call(
        lambda *refs: final_kernel(tp_count, features * tp_count, *refs),
        out_shape=[
            shape((tokens, features), BF16),
            shape((block, features), BF16),
            shape((slots, cols), BF16),
            shape((tokens, 128), F32),
        ],
        in_specs=[VMEM] * 7,
        out_specs=[VMEM] * 4,
        compiler_params=params(24),
        name="input_grads",
    )(messages, placed, normed_grad, text_embed, gain, place_table, send_table)

    key_value = pl.pallas_call(
        lambda *refs: key_value_kernel(tp_count, *refs),
        out_shape=shape((tokens, cols), BF16),
        in_specs=[VMEM] * (tp_count + 3),
        out_specs=VMEM,
        compiler_params=params(16),
        name="key_value",
    )(*arrived, inv, place_table, kv_rows)
    return (key_value, embed_grad, image_grad)


def solution(mesh):
    in_specs = (
        P("lane", "section"),
        P("section", "tp"),
        P("tp"),
        P(("lane", "section")),
        P("lane", "section", None, None),
        P(("lane", "section"), "tp"),
        P("tp"),
        P("tp", None),
        P(("lane", "section"), None),
    )
    out_specs = (
        P(("lane", "section"), "tp"),
        P(("lane", "section"), "tp"),
        P(("lane", "section"), "tp"),
    )
    return jax.shard_map(
        on_device, mesh=mesh, in_specs=in_specs, out_specs=out_specs, check_vma=False
    )
```

time: 129 us -> 76.9 us (0.60)
  matrix products: 38.2 us -> 0 us
  waiting for transfers between devices: 44.9 us -> 11.3 us
  Pallas kernels: 0 us -> 23.6 us
  local copies, waits for them, and re-layouts: 2.65 us -> 25.5 us
  blocking collectives: 19.1 us -> 0 us
  between operations: 14.2 us -> 0.75 us
  starting transfers between devices: 3.94 us -> 14.9 us
  other arithmetic: 5.44 us -> 0.1 us
    reduce_scatter x2 -> x0, waiting for transfers between devices: 40.1 us -> none  [the longest x1 29.4 us: on_device(): lax.psum_scatter(jnp.transpose(product.reshape(tokens, 1 * lax.axis_size(...]
    dot_general x7 -> x0, matrix products: 38.2 us -> none  [the longest x1 21.5 us: on_device(): jnp.dot(activated, merge_weight, preferred_element_type=jnp.float32)]
    unnamed x14 -> x44, local copies, waits for them, and re-layouts: 0.04 us -> 24.6 us
    pallas_call x0 -> x7, Pallas kernels: none -> 23.6 us  [the longest x1 6.21 us: on_device(): pl.pallas_call(lambda *refs: text_kernel(tp_count, *refs), out_shape=[sha...]
    psum x1 -> x0, blocking collectives: 11.9 us -> none  [on_device(): total_squares, total_dots = lax.psum((squares, dot_terms), 'tp')]
    all_to_all x1 -> x0, blocking collectives: 7.21 us -> none  [on_device(): lax.all_to_all(returning.reshape(lane_count, slot_count, -1), 'lane', spl...]
    all_to_all x1 -> x2, waiting for transfers between devices: 4.75 us -> 11.1 us  [the longest x1 6.24 us: on_device(): got = lax.all_to_all(sent, 'lane', 0, 0, tiled=True)]
    all_to_all x1 -> x2, starting transfers between devices: 3.9 us -> 9.89 us  [the longest x1 5.03 us: on_device(): got = lax.all_to_all(sent, 'lane', 0, 0, tiled=True)]
  transfers between devices with their start and end apart: 3 -> 7, of which waited for: 3 -> 3; matrix products, arithmetic and copies ran while one was open for 5% -> 1% of each run, Pallas kernels for 0% -> 22%
where the time goes in v1:
time: 76.9 us; the launch traced here: 76.2 us
  local copies, waits for them, and re-layouts  25.5 us (33%)
  Pallas kernels  23.6 us (31%)
  starting transfers between devices  14.9 us (19%)
  waiting for transfers between devices  11.3 us (15%)
    unnamed x44, local copies, waits for them, and re-layouts  24.6 us
    all_to_all x1, waiting for transfers between devices, on_device(): got = lax.all_to_all(sent, 'lane', 0, 0, tiled=True)  6.24 us
    pallas_call x1, Pallas kernels, on_device(): pl.pallas_call(lambda *refs: text_kernel(tp_count, *refs), out_shape=[sha...  6.21 us
    all_to_all x1, starting transfers between devices, on_device(): got = lax.all_to_all(sent, 'lane', 0, 0, tiled=True)  5.03 us
    all_to_all x1, waiting for transfers between devices, on_device(): messages = lax.all_to_all(message, 'tp', 0, 0, tiled=True)  4.87 us
    all_to_all x1, starting transfers between devices, on_device(): messages = lax.all_to_all(message, 'tp', 0, 0, tiled=True)  4.87 us
    pallas_call x1, Pallas kernels, on_device(): pl.pallas_call(grad_kernel, out_shape=shape((tokens + slots2, features),...  4.75 us
    ppermute x3, starting transfers between devices, on_device(): lax.ppermute(part, 'tp', [(i, i ^ k) for i in range(tp_count)])  4.39 us
  transfers between devices with their start and end apart: 7, of which 3 were waited for; matrix products, arithmetic and copies ran while one was open for 1% of the time, Pallas kernels for 22%

profile of v1, /device:TPU:0, one launch (start us, length us, event | category | flops | bytes accessed | tf_op | source)
XLA Modules:
  0.0 76.2 jit_solution(18198458400226059987)
XLA Ops:
  0.6 0.5 collective-permute-start.3
  1.2 0.8 pad.4
  1.9 0.1 reshape.35.refs_3_
  2.0 0.2 collective-permute-done.3.refs_2_
  2.2 1.2 %copy-done.4 = bf16[256,2048]{1,0:T(8,128)(2,1)S(1)} copy-done((bf16[256,2048]{1,0:T(8,128)(2,1)S(1)}, bf16[256,2048]{1,0:T(8,128)(2,1)}, u32[]{:S(2)}) %copy-start.4) | copy-done | bytes 1048600
  3.4 1.7 %copy-done.9 = bf16[512,2560]{1,0:T(8,128)(2,1)S(1)} copy-done((bf16[512,2560]{1,0:T(8,128)(2,1)S(1)}, bf16[512,2560]{1,0:T(8,128)(2,1)}, u32[]{:S(2)}) %copy-start.9) | copy-done | bytes 2621464
  5.2 0.7 copy-done.17
  5.9 0.7 copy-done.20
  6.5 1.6 %gather_rows.1 = (bf16[64,2560]{1,0:T(8,128)(2,1)}, bf16[16,256]{1,0:T(8,128)(2,1)S(1)}) custom-call(s32[1]{0:T(128)} %bitcast.5.refs_0_, s32[1,256]{1,0:T(1,128)S(1)} %bitcast.19, s32[1,256]{1,0:T(1,128)S(1)} %collective-permute-done.3.refs_2_, s32[64,1]{1,0:T(8,128)S(1)} %reshape.35.refs_3_, s32[16,1]{1,0:T(8,128)S(1)} %copy-done.17, ...), custom_call_target="tpu_custom_call" | custom-call | tf_op jit(solution)/shard_map/gather_rows/pallas_call | solution.py:264
  8.2 5.0 %all-to-all-start = ((bf16[4,16,2560]{2,1,0:T(8,128)(2,1)}), bf16[4,16,2560]{2,1,0:T(8,128)(2,1)S(1)}, u32[]{:S(2)}, u32[]{:S(2)}) async-start(bf16[4,16,2560]{2,1,0:T(8,128)(2,1)} %bitcast.8), calls=%async_computation | async-start | bytes 655360 | tf_op jit(solution)/shard_map/all_to_all | solution.py:272
  13.2 6.2 %all-to-all-done = bf16[4,16,2560]{2,1,0:T(8,128)(2,1)S(1)} async-done(((bf16[4,16,2560]{2,1,0:T(8,128)(2,1)}), bf16[4,16,2560]{2,1,0:T(8,128)(2,1)S(1)}, u32[]{:S(2)}, u32[]{:S(2)}) %all-to-all-start) | async-done | bytes 327712 | tf_op jit(solution)/shard_map/all_to_all | solution.py:272
  19.4 4.0 %copy-done.3 = bf16[2560,2048]{1,0:T(8,128)(2,1)S(1)} copy-done((bf16[2560,2048]{1,0:T(8,128)(2,1)S(1)}, bf16[2560,2048]{1,0:T(8,128)(2,1)}, u32[]{:S(2)}) %copy-start.3) | copy-done | bytes 10485784
  23.4 0.7 copy-done.18
  24.1 3.4 %merge_rows.1 = (f32[32,2048]{1,0:T(8,128)S(1)}, bf16[32,2048]{1,0:T(8,128)(2,1)S(1)}, bf16[32,2048]{1,0:T(8,128)(2,1)S(1)}) custom-call(s32[16,1]{1,0:T(8,128)S(1)} %copy-done.18, bf16[64,2560]{1,0:T(8,128)(2,1)S(1)} %bitcast.13, bf16[64,2560]{1,0:T(8,128)(2,1)} %get-tuple-element.24.refs_2_, bf16[2560,2048]{1,0:T(8,128)(2,1)S(1)} %copy-done.3), custom_call_target="tpu_custom_call" | custom-call | tf_op jit(solution)/shard_map/merge_rows/pallas_call | solution.py:274
  27.7 6.2 %text_kv.1 = (bf16[256,512]{1,0:T(8,128)(2,1)}, bf16[256,512]{1,0:T(8,128)(2,1)}, bf16[256,512]{1,0:T(8,128)(2,1)}, f32[256,512]{1,0:T(8,128)S(1)}, bf16[2048,20...) custom-call(s32[4]{0:T(128)S(1)} %pad_add_fusion.refs_0_, bf16[256,2048]{1,0:T(8,128)(2,1)S(1)} %copy-done.7, ...), custom_call_target="tpu_custom_call" | custom-call | tf_op jit(solution)/shard_map/text_kv/pallas_call | solution.py:240
  33.9 3.3 %copy-done = bf16[2048,2048]{1,0:T(8,128)(2,1)} copy-done((bf16[2048,2048]{1,0:T(8,128)(2,1)}, bf16[2048,2048]{1,0:T(8,128)(2,1)S(1)}, u32[]{:S(2)}) %copy-start) | copy-done | bytes 8388632
  37.2 0.8 %copy-done.12 = f32[256,512]{1,0:T(8,128)} copy-done((f32[256,512]{1,0:T(8,128)}, f32[256,512]{1,0:T(8,128)S(1)}, u32[]{:S(2)}) %copy-start.12) | copy-done | bytes 524312
  38.0 3.6 %collective-permute-start = (bf16[256,512]{1,0:T(8,128)(2,1)}, bf16[256,512]{1,0:T(8,128)(2,1)}, u32[]{:S(2)}, u32[]{:S(2)}) collective-permute-start(bf16[256,512]{1,0:T(8,128)(2,1)} %get-tuple-element.21), channel_id=1, source_target_pairs={{0,3},{1,2},{2,1},{3,0},{4,7},{5,6},{6,5},{7,4},{8,11},{9,10},{10,... | collective-permute-start | bytes 786440 | tf_op jit(solution)/shard_map/ppermute | solution.py:257
  41.6 0.8 %collective-permute-start.2 = (bf16[256,512]{1,0:T(8,128)(2,1)}, bf16[256,512]{1,0:T(8,128)(2,1)}, u32[]{:S(2)}, u32[]{:S(2)}) collective-permute-start(bf16[256,512]{1,0:T(8,128)(2,1)} %get-tuple-element.23), channel_id=1, source_target_pairs={{0,1},{1,0},{2,3},{3,2},{4,5},{5,4},{6,7},{7,6},{8,9},{9,8},{10,11... | collective-permute-start | bytes 786440 | tf_op jit(solution)/shard_map/ppermute | solution.py:257
  42.5 3.4 %copy-done.1 = bf16[2048,2048]{1,0:T(8,128)(2,1)S(1)} copy-done((bf16[2048,2048]{1,0:T(8,128)(2,1)S(1)}, bf16[2048,2048]{1,0:T(8,128)(2,1)}, u32[]{:S(2)}) %copy-start.1) | copy-done | bytes 8388632
  45.9 2.4 %slot_kv.1 = (bf16[32,2048]{1,0:T(8,128)(2,1)S(1)}, bf16[128,512]{1,0:T(8,128)(2,1)}) custom-call(f32[32,2048]{1,0:T(8,128)S(1)} %get-tuple-element.25.refs_0_, bf16[32,2048]{1,0:T(8,128)(2,1)S(1)} %collective-permute-done.4.refs_1_, f32[1,2048]{1,0:T(1,128)S(1)} %bitcast.17, f32[1,2048]{1,0:T(1,128)S(1)} %bitcast.15, bf16[2048,2048]{1,0:T(8,128)(2,1)S(1)} %copy-done.1, ...), custom_call_target="tpu_custom_call" | custom-call | tf_op jit(solution)/shard_map/slot_kv/pallas_call | solution.py:286
  48.3 0.7 copy-done.14
  48.9 4.9 %all-to-all-start.1 = ((bf16[4,32,512]{2,1,0:T(8,128)(2,1)}), bf16[4,32,512]{2,1,0:T(8,128)(2,1)}, u32[]{:S(2)}, u32[]{:S(2)}) async-start(bf16[4,32,512]{2,1,0:T(8,128)(2,1)} %bitcast.11), calls=%async_computation.1 | async-start | bytes 262144 | tf_op jit(solution)/shard_map/all_to_all | solution.py:294
  53.8 3.4 %copy-done.2 = bf16[2048,2048]{1,0:T(8,128)(2,1)S(1)} copy-done((bf16[2048,2048]{1,0:T(8,128)(2,1)S(1)}, bf16[2048,2048]{1,0:T(8,128)(2,1)}, u32[]{:S(2)}) %copy-start.2) | copy-done | bytes 8388632
  57.2 0.9 %copy-done.11 = bf16[32,2048]{1,0:T(8,128)(2,1)S(1)} copy-done((bf16[32,2048]{1,0:T(8,128)(2,1)S(1)}, bf16[32,2048]{1,0:T(8,128)(2,1)}, u32[]{:S(2)}) %copy-start.11) | copy-done | bytes 131096
  58.1 4.7 %normed_grad.1.refs_2_ = f32[288,2048]{1,0:T(8,128)S(1)} custom-call(bf16[256,2048]{1,0:T(8,128)(2,1)S(1)} %copy-done.5, bf16[32,2048]{1,0:T(8,128)(2,1)S(1)} %copy-done.11, bf16[2048,2048]{1,0:T(8,128)(2,1)S(1)} %copy-done.2), custom_call_target="tpu_custom_call" | custom-call | tf_op jit(solution)/shard_map/normed_grad/pallas_call | solution.py:296
  62.8 4.9 %all-to-all-done.1 = bf16[4,32,512]{2,1,0:T(8,128)(2,1)} async-done(((bf16[4,32,512]{2,1,0:T(8,128)(2,1)}), bf16[4,32,512]{2,1,0:T(8,128)(2,1)}, u32[]{:S(2)}, u32[]{:S(2)}) %all-to-all-start.1) | async-done | bytes 131104 | tf_op jit(solution)/shard_map/all_to_all | solution.py:294
  67.7 1.2 %copy-done.8 = bf16[256,2048]{1,0:T(8,128)(2,1)S(1)} copy-done((bf16[256,2048]{1,0:T(8,128)(2,1)S(1)}, bf16[256,2048]{1,0:T(8,128)(2,1)}, u32[]{:S(2)}) %copy-start.8) | copy-done | bytes 1048600
  68.9 0.9 %copy-done.15 = bf16[32,2048]{1,0:T(8,128)(2,1)S(1)} copy-done((bf16[32,2048]{1,0:T(8,128)(2,1)S(1)}, bf16[32,2048]{1,0:T(8,128)(2,1)}, u32[]{:S(2)}) %copy-start.15) | copy-done | bytes 131096
  69.8 3.2 %input_grads.1 = (bf16[256,2048]{1,0:T(8,128)(2,1)}, bf16[256,2048]{1,0:T(8,128)(2,1)}, bf16[16,512]{1,0:T(8,128)(2,1)S(1)}, f32[256,128]{1,0:T(8,128)S(1)}) custom-call(bf16[128,512]{1,0:T(8,128)(2,1)} %bitcast.12.refs_0_, bf16[32,2048]{1,0:T(8,128)(2,1)S(1)} %copy-done.15, f32[288,2048]{1,0:T(8,128)S(1)} %normed_grad.1.refs_2_, ...), custom_call_target="tpu_custom_call" | custom-call | tf_op jit(solution)/shard_map/input_grads/pallas_call | solution.py:305
  73.1 1.0 %copy-done.13 = f32[256,512]{1,0:T(8,128)S(1)} copy-done((f32[256,512]{1,0:T(8,128)S(1)}, f32[256,512]{1,0:T(8,128)}, u32[]{:S(2)}) %copy-start.13) | copy-done | bytes 524312
  74.1 2.1 %key_value.1 = bf16[256,512]{1,0:T(8,128)(2,1)} custom-call(f32[256,512]{1,0:T(8,128)S(1)} %copy-done.13, bf16[256,512]{1,0:T(8,128)(2,1)} %collective-permute-done.refs_1_, bf16[256,512]{1,0:T(8,128)(2,1)} %collective-permute-done.1.refs_2_, bf16[256,512]{1,0:T(8,128)(2,1)} %collective-permute-done.2.refs_3_, f32[256,128]{1,0:T(8,128)S(1)} %get-tuple-element.33.refs_4_, ...), custom_call_target="tpu_custom_call" | custom-call | tf_op jit(solution)/shard_map/key_value/pallas_call | solution.py:319
  (38 shorter events, 0.3 us)
Async XLA Ops:
  0.6 27.0 %copy-start.16 = (f32[2048]{0:T(1024)S(1)}, f32[2048]{0:T(1024)}, u32[]{:S(2)}) copy-start(f32[2048]{0:T(1024)} %param.16) | copy-start | bytes 24580
  0.6 1.5 %collective-permute-start.3 = (s32[1,256]{1,0:T(1,128)}, s32[1,256]{1,0:T(1,128)S(1)}, u32[]{:S(2)}, u32[]{:S(2)}) collective-permute-start(s32[1,256]{1,0:T(1,128)} %bitcast.18), channel_id=1, source_target_pairs={{0,4},{4,0},{1,5},{5,1},{2,6},{6,2},{3,7},{7,3},{8,12},{12,8},{9,1... | collective-permute-start | bytes 3080 | tf_op jit(solution)/shard_map/ppermute | solution.py:236
  2.2 1.2 %copy-start.4 = (bf16[256,2048]{1,0:T(8,128)(2,1)S(1)}, bf16[256,2048]{1,0:T(8,128)(2,1)}, u32[]{:S(2)}) copy-start(bf16[256,2048]{1,0:T(8,128)(2,1)} %grad.1) | copy-start | bytes 3145732
  3.4 1.7 %copy-start.9 = (bf16[512,2560]{1,0:T(8,128)(2,1)S(1)}, bf16[512,2560]{1,0:T(8,128)(2,1)}, u32[]{:S(2)}) copy-start(bf16[512,2560]{1,0:T(8,128)(2,1)} %refs_5_.1) | copy-start | bytes 7864324
  5.2 0.7 copy-start.17
  5.9 0.7 copy-start.20
  6.5 21.1 %copy-start.5 = (bf16[256,2048]{1,0:T(8,128)(2,1)S(1)}, bf16[256,2048]{1,0:T(8,128)(2,1)}, u32[]{:S(2)}) copy-start(bf16[256,2048]{1,0:T(8,128)(2,1)} %grad.1) | copy-start | bytes 3145732
  6.5 21.1 %copy-start.7 = (bf16[256,2048]{1,0:T(8,128)(2,1)S(1)}, bf16[256,2048]{1,0:T(8,128)(2,1)}, u32[]{:S(2)}) copy-start(bf16[256,2048]{1,0:T(8,128)(2,1)} %refs_3_.5) | copy-start | bytes 3145732
  8.2 11.3 %all-to-all-start = ((bf16[4,16,2560]{2,1,0:T(8,128)(2,1)}), bf16[4,16,2560]{2,1,0:T(8,128)(2,1)S(1)}, u32[]{:S(2)}, u32[]{:S(2)}) async-start(bf16[4,16,2560]{2,1,0:T(8,128)(2,1)} %bitcast.8), calls=%async_computation | async-start | bytes 655360 | tf_op jit(solution)/shard_map/all_to_all | solution.py:272
  19.4 4.0 %copy-start.3 = (bf16[2560,2048]{1,0:T(8,128)(2,1)S(1)}, bf16[2560,2048]{1,0:T(8,128)(2,1)}, u32[]{:S(2)}) copy-start(bf16[2560,2048]{1,0:T(8,128)(2,1)} %refs_3_.4) | copy-start | bytes 31457284
  23.4 0.7 copy-start.18
  24.1 3.6 %copy-start.6 = (bf16[2048,2048]{1,0:T(8,128)(2,1)S(1)}, bf16[2048,2048]{1,0:T(8,128)(2,1)}, u32[]{:S(2)}) copy-start(bf16[2048,2048]{1,0:T(8,128)(2,1)} %refs_4_.2) | copy-start | bytes 25165828
  24.1 18.3 %copy-start.21 = (s32[1,1,4,4]{3,2,1,0:T(4,128)S(1)}, s32[1,1,4,4]{3,2,1,0:T(4,128)}, u32[]{:S(2)}) copy-start(s32[1,1,4,4]{3,2,1,0:T(4,128)} %param.14) | copy-start | bytes 196
  24.1 18.4 %copy-start.19 = (f32[2048]{0:T(1024)S(1)}, f32[2048]{0:T(1024)}, u32[]{:S(2)}) copy-start(f32[2048]{0:T(1024)} %param.12) | copy-start | bytes 24580
  27.5 20.8 %copy-start.10 = (bf16[32,2048]{1,0:T(8,128)(2,1)}, bf16[32,2048]{1,0:T(8,128)(2,1)S(1)}, u32[]{:S(2)}) copy-start(bf16[32,2048]{1,0:T(8,128)(2,1)S(1)} %get-tuple-element.28.refs_5_.grad_rows) | copy-start | bytes 393220
  27.5 15.0 %collective-permute-start.4 = (bf16[32,2048]{1,0:T(8,128)(2,1)S(1)}, bf16[32,2048]{1,0:T(8,128)(2,1)S(1)}, u32[]{:S(2)}, u32[]{:S(2)}) collective-permute-start(bf16[32,2048]{1,0:T(8,128)(2,1)S(1)} %get-tuple-element.26), channel_id=1, source_target_pairs={{0,4},{4,0},{1,5},{5,1},{2,6},{6,2},{3,7},{7,3},{8,12},{12,8},{9,1... | collective-permute-start | bytes 393224 | tf_op jit(solution)/shard_map/ppermute | solution.py:282
  33.9 3.3 %copy-start = (bf16[2048,2048]{1,0:T(8,128)(2,1)}, bf16[2048,2048]{1,0:T(8,128)(2,1)S(1)}, u32[]{:S(2)}) copy-start(bf16[2048,2048]{1,0:T(8,128)(2,1)S(1)} %get-tuple-element.27.refs_4_.weight) | copy-start | bytes 25165828
  37.2 0.8 %copy-start.12 = (f32[256,512]{1,0:T(8,128)}, f32[256,512]{1,0:T(8,128)S(1)}, u32[]{:S(2)}) copy-start(f32[256,512]{1,0:T(8,128)S(1)} %get-tuple-element.20.refs_0_) | copy-start | bytes 1572868
  38.0 35.0 %collective-permute-start = (bf16[256,512]{1,0:T(8,128)(2,1)}, bf16[256,512]{1,0:T(8,128)(2,1)}, u32[]{:S(2)}, u32[]{:S(2)}) collective-permute-start(bf16[256,512]{1,0:T(8,128)(2,1)} %get-tuple-element.21), channel_id=1, source_target_pairs={{0,3},{1,2},{2,1},{3,0},{4,7},{5,6},{6,5},{7,4},{8,11},{9,10},{10,... | collective-permute-start | bytes 786440 | tf_op jit(solution)/shard_map/ppermute | solution.py:257
  41.6 31.4 %collective-permute-start.1 = (bf16[256,512]{1,0:T(8,128)(2,1)}, bf16[256,512]{1,0:T(8,128)(2,1)}, u32[]{:S(2)}, u32[]{:S(2)}) collective-permute-start(bf16[256,512]{1,0:T(8,128)(2,1)} %get-tuple-element.22), channel_id=1, source_target_pairs={{0,2},{1,3},{2,0},{3,1},{4,6},{5,7},{6,4},{7,5},{8,10},{9,11},{10,... | collective-permute-start | bytes 786440 | tf_op jit(solution)/shard_map/ppermute | solution.py:257
  41.6 31.4 %collective-permute-start.2 = (bf16[256,512]{1,0:T(8,128)(2,1)}, bf16[256,512]{1,0:T(8,128)(2,1)}, u32[]{:S(2)}, u32[]{:S(2)}) collective-permute-start(bf16[256,512]{1,0:T(8,128)(2,1)} %get-tuple-element.23), channel_id=1, source_target_pairs={{0,1},{1,0},{2,3},{3,2},{4,5},{5,4},{6,7},{7,6},{8,9},{9,8},{10,11... | collective-permute-start | bytes 786440 | tf_op jit(solution)/shard_map/ppermute | solution.py:257
  42.5 3.4 %copy-start.1 = (bf16[2048,2048]{1,0:T(8,128)(2,1)S(1)}, bf16[2048,2048]{1,0:T(8,128)(2,1)}, u32[]{:S(2)}) copy-start(bf16[2048,2048]{1,0:T(8,128)(2,1)} %copy-done) | copy-start | bytes 25165828
  48.3 0.7 copy-start.14
  48.9 18.8 %all-to-all-start.1 = ((bf16[4,32,512]{2,1,0:T(8,128)(2,1)}), bf16[4,32,512]{2,1,0:T(8,128)(2,1)}, u32[]{:S(2)}, u32[]{:S(2)}) async-start(bf16[4,32,512]{2,1,0:T(8,128)(2,1)} %bitcast.11), calls=%async_computation.1 | async-start | bytes 262144 | tf_op jit(solution)/shard_map/all_to_all | solution.py:294
  53.8 3.4 %copy-start.2 = (bf16[2048,2048]{1,0:T(8,128)(2,1)S(1)}, bf16[2048,2048]{1,0:T(8,128)(2,1)}, u32[]{:S(2)}) copy-start(bf16[2048,2048]{1,0:T(8,128)(2,1)} %copy-done) | copy-start | bytes 25165828
  57.2 0.9 %copy-start.11 = (bf16[32,2048]{1,0:T(8,128)(2,1)S(1)}, bf16[32,2048]{1,0:T(8,128)(2,1)}, u32[]{:S(2)}) copy-start(bf16[32,2048]{1,0:T(8,128)(2,1)} %copy-done.10) | copy-start | bytes 393220
  67.7 1.2 %copy-start.8 = (bf16[256,2048]{1,0:T(8,128)(2,1)S(1)}, bf16[256,2048]{1,0:T(8,128)(2,1)}, u32[]{:S(2)}) copy-start(bf16[256,2048]{1,0:T(8,128)(2,1)} %refs_3_.5) | copy-start | bytes 3145732
  68.9 0.9 %copy-start.15 = (bf16[32,2048]{1,0:T(8,128)(2,1)S(1)}, bf16[32,2048]{1,0:T(8,128)(2,1)}, u32[]{:S(2)}) copy-start(bf16[32,2048]{1,0:T(8,128)(2,1)} %copy-done.14) | copy-start | bytes 393220
  73.1 1.0 %copy-start.13 = (f32[256,512]{1,0:T(8,128)S(1)}, f32[256,512]{1,0:T(8,128)}, u32[]{:S(2)}) copy-start(f32[256,512]{1,0:T(8,128)} %copy-done.12) | copy-start | bytes 1572868

commit v2 on v0

v2 whole, which is shorter than its diff:
```python
import math

import jax
import jax.numpy as jnp
import numpy as np
from jax import lax
from jax.experimental import pallas as pl
from jax.experimental.pallas import tpu as pltpu
from jax.sharding import PartitionSpec as P

EPSILON = 1e-06
F32 = jnp.float32
BF16 = jnp.bfloat16
MIB = 1 << 20
VMEM = pl.BlockSpec(memory_space=pltpu.VMEM)
ANY = pl.BlockSpec(memory_space=pl.ANY)


def round_up(value, step):
    return -(-value // step) * step


def dot(a, b):
    return jnp.dot(a, b, preferred_element_type=F32)


def dot_dims(a, b, dim_a, dim_b):
    return lax.dot_general(a, b, (((dim_a,), (dim_b,)), ((), ())), preferred_element_type=F32)


def iota(shape, dim):
    return lax.broadcasted_iota(jnp.int32, shape, dim)


def one_hot(column, width):
    return (column == iota((column.shape[0], width), 1)).astype(F32).astype(BF16)


def peer_columns(axis, k, cols):
    return pl.ds(pl.multiple_of((lax.axis_index(axis) ^ k) * cols, cols), cols)


def picker(slots, rows, group, cap, first):
    row = iota((slots, rows), 1)
    place = (row & (group - 1)) - first
    slot = (row >> int(math.log2(group))) * cap + place
    return ((slot == iota((slots, rows), 0)) & (place >= 0) & (place < cap)).astype(F32).astype(BF16)


def mask(match):
    return match.astype(F32).astype(BF16)


def first_text_kernel(step, *refs):
    sources, (part, scaled, sums), kept, (gain, weight, sem) = refs[:7], refs[7:10], refs[10:15], refs[15:]
    text, grad = kept[:2]
    span = peer_columns("tp", step, part.shape[1])
    text_hbm, grad_hbm, dest_hbm, pos_hbm, hidden_hbm, gain_hbm, weight_hbm = sources
    pairs = [
        (text_hbm, text),
        (gain_hbm, gain),
        (weight_hbm.at[:, span], weight),
        (grad_hbm, grad),
        (dest_hbm, kept[2]),
        (pos_hbm, kept[3]),
        (hidden_hbm, kept[4]),
    ]
    copies = [pltpu.make_async_copy(source, target, sem.at[i]) for i, (source, target) in enumerate(pairs)]
    for copy in copies:
        copy.start()
    copies[0].wait()
    copies[1].wait()
    wide = text[...].astype(F32)
    squares = jnp.sum(wide * wide, axis=1, keepdims=True)
    scaled[...] = (wide * gain[...]).astype(BF16)
    copies[2].wait()
    product = dot(scaled[...], weight[...])
    part[...] = product.astype(BF16)
    copies[3].wait()
    dots = jnp.sum(product * grad[:, span].astype(F32), axis=1, keepdims=True)
    lane = iota(sums.shape, 1)
    sums[...] = jnp.where(lane == 0, squares, jnp.where(lane == 1, dots, 0.0))
    for copy in copies[4:]:
        copy.wait()


def text_kernel(steps, scaled, weight, grad, sums, *refs):
    parts, sums_out = refs[:-1], refs[-1]
    dots = jnp.zeros((scaled.shape[0], 1), F32)
    for step, part in zip(steps, parts):
        span = peer_columns("tp", step, part.shape[1])
        product = dot(scaled[...], weight[:, span])
        part[...] = product.astype(part.dtype)
        dots = dots + jnp.sum(product * grad[:, span].astype(F32), axis=1, keepdims=True)
    lane = iota(sums.shape, 1)
    sums_out[...] = (sums[...] + jnp.where(lane == 1, dots, 0.0)).T[:8]


def gather_kernel(lane_count, group, cap, own_ref, other_ref, pos_ref, hidden, grad, *refs):
    payloads, (send_table, place_table) = refs[:lane_count], refs[lane_count:]
    rows = lane_count * group
    slots = lane_count * cap
    block, tokens = own_ref.shape[1], grad.shape[0]
    lane = lax.axis_index("lane")
    row_id = iota((rows, block), 0)
    lane_id = (row_id >> int(math.log2(group))) ^ lane
    place = row_id & (group - 1)
    entry = place & (2 * cap - 1)
    earlier = mask(iota((block, block), 0) < iota((block, block), 1))

    def select(dest, first):
        match = dest == lane_id
        rank = dot(mask(match), earlier)
        return match & (rank == (entry - first).astype(F32))

    own = select(own_ref[...], 0)
    other = select(other_ref[...], cap)
    section = lax.axis_index("section")
    own_rows = pl.ds(pl.multiple_of(section * block, block), block)
    other_rows = pl.ds(pl.multiple_of((1 - section) * block, block), block)
    folds = group // (2 * cap)
    width = hidden.shape[1] // folds
    picked = jnp.zeros((rows, width), F32)
    for i in range(folds):
        here = (place >= 2 * cap * i) & (place < 2 * cap * (i + 1))
        cut = slice(i * width, (i + 1) * width)
        picked = picked + dot(mask(own & here), hidden[own_rows, cut]) + dot(mask(other & here), hidden[other_rows, cut])
    active = 0.5 * picked * (1.0 + lax.erf(picked * np.float32(math.sqrt(0.5))))

    lane_pick = mask((iota((rows, lane_count), 0) >> int(math.log2(group))) ^ lane == iota((rows, lane_count), 1))
    high, low = pos_ref[...] >> 7, pos_ref[...] & 127
    spread = dot(lane_pick, high.astype(F32).astype(BF16)) * 128.0 + dot(lane_pick, low.astype(F32).astype(BF16))
    chosen = (iota((rows, cap), 0) & (cap - 1)) == iota((rows, cap), 1)
    row_pos = jnp.sum(jnp.where(chosen, spread, 0.0), axis=1, keepdims=True)
    taken = row_pos == iota((rows, tokens), 1).astype(F32)
    taken_place = iota((rows, tokens), 0) & (group - 1)
    grad_folds = group // cap
    grad_width = grad.shape[1] // grad_folds
    grad_rows = jnp.zeros((rows, grad_width), F32)
    for i in range(grad_folds):
        here = (taken_place >= cap * i) & (taken_place < cap * (i + 1))
        grad_rows = grad_rows + dot(mask(taken & here), grad[:, i * grad_width : (i + 1) * grad_width])
    for k in range(lane_count):
        cut = slice(k * group, (k + 1) * group)
        payloads[k][:, :width] = active[cut].astype(BF16)
        payloads[k][:, width:] = grad_rows[cut].astype(BF16)
    first = picker(slots, rows, group, cap, 0)
    send_table[...] = dot(first, mask(own)).astype(BF16)
    place_table[...] = dot(first, mask(taken)).astype(BF16)


def merge_kernel(lane_count, cap, *refs):
    got_refs, sent_refs = (refs[0],) + refs[lane_count : 2 * lane_count - 1], refs[:lane_count]
    weight, text_part, first_part, own, other, grad_rows, text_total = refs[2 * lane_count - 1 :]
    text_total[...] = text_part[...] + first_part[...].astype(F32)
    group = refs[0].shape[0]
    rows = lane_count * group
    slots = lane_count * cap
    grad_width = grad_rows.shape[1] // (group // cap)
    width = refs[0].shape[1] - grad_width
    got = jnp.concatenate([ref[...] for ref in got_refs], axis=0)
    sent = jnp.concatenate([ref[...] for ref in sent_refs], axis=0)

    def unfold(table, first, step, cols):
        pieces = [dot(picker(slots, rows, group, cap, i), table[:, cols]) for i in range(first, group, step)]
        return jnp.concatenate(pieces, axis=1).astype(BF16)

    merged = slice(0, width)
    picked = jnp.concatenate(
        [unfold(table, first, 2 * cap, merged) for first in (0, cap) for table in (got, sent)], axis=0
    )
    grad_rows[:slots] = unfold(sent, 0, cap, slice(width, width + grad_width))
    grad_rows[slots:] = unfold(got, 0, cap, slice(width, width + grad_width))
    cols = weight.shape[1]
    step = min(512, cols)
    for c in range(0, cols, step):
        total = dot(picked, weight[:, c : c + step])
        own[:, c : c + step] = total[: 2 * slots]
        other[:, c : c + step] = total[2 * slots :].astype(BF16)


def slot_kernel(tp_count, sum_rows, own, other, bias, gain, weight, grad_rows, text_sums, rows, *messages):
    slots2 = own.shape[0]
    slots = slots2 // 2
    placed = (own[...] + other[...].astype(F32) + bias[...]).astype(BF16)
    rows[...] = placed
    wide = placed.astype(F32)
    squares = jnp.sum(wide * wide, axis=1, keepdims=True)
    scaled = (wide * gain[...]).astype(BF16)
    cols = messages[0].shape[1]
    dots = jnp.zeros_like(squares)
    for k in range(tp_count):
        span = peer_columns("tp", k, cols)
        part = dot(scaled, weight[:, span])
        dots = dots + jnp.sum(part * grad_rows[:, span].astype(F32), axis=1, keepdims=True)
        messages[k][:slots] = part[:slots].astype(BF16)
    lane = iota((slots2, 128), 1)
    columns = jnp.where(lane == 0, squares, jnp.where(lane == 1, dots, 0.0))
    padded = round_up(slots2, 128)
    if padded > slots2:
        columns = jnp.concatenate([columns, jnp.zeros((padded - slots2, 128), F32)], axis=0)
    turned = columns.T
    pieces = []
    for i in range(2):
        total = jnp.concatenate([text_sums[i : i + 1], turned[i : i + 1]], axis=1)
        high = total.astype(BF16).astype(F32)
        pieces += [high, total - high]
    line = jnp.concatenate(pieces, axis=1)
    message = jnp.zeros((sum_rows, cols), F32)
    sublane = iota((sum_rows, cols), 0)
    for i in range(line.shape[1] // cols):
        message = jnp.where(sublane == i, line[:, i * cols : (i + 1) * cols], message)
    for k in range(tp_count):
        messages[k][slots:] = message.astype(BF16)


def grad_kernel(grad, grad_rows, weight, gain, text, rows, place_table, out, stream):
    slots = grad_rows.shape[0] // 2
    joined = jnp.concatenate([grad[...], grad_rows[slots:]], axis=0)
    taken = dot_dims(place_table[...], jnp.ones((slots, 128), BF16), 0, 0)[:, 0:1] > 0.0
    step = min(512, weight.shape[0])
    for c in range(0, weight.shape[0], step):
        cut = slice(c, c + step)
        out[:, cut] = gain[:, cut] * dot_dims(joined, weight[cut, :], 1, 1)
        placed = dot_dims(place_table[...], rows[:slots, cut], 0, 0)
        stream[:, cut] = jnp.where(taken, placed, text[:, cut].astype(F32)).astype(BF16)


def final_kernel(tp_count, arrived_count, features, rows, scaled_grad, stream, place_table, send_table, *refs):
    messages, parts = refs[:tp_count], refs[tp_count : tp_count + arrived_count]
    key_value, embed_grad, image_grad, kv_buffer, embed_buffer, image_buffer, sem = refs[tp_count + arrived_count :]
    slots2 = rows.shape[0]
    slots = slots2 // 2
    tokens, cols = kv_buffer.shape
    total = messages[0][...].astype(F32)
    for message in messages[1:]:
        total = total + message[...].astype(F32)
    span = tokens + round_up(slots2, 128)
    line = jnp.concatenate([total[slots + i : slots + i + 1] for i in range(4 * span // cols)], axis=1)
    squares = line[:, :span] + line[:, span : 2 * span]
    dots = line[:, 2 * span : 3 * span] + line[:, 3 * span :]
    inv = lax.rsqrt(squares / features + EPSILON)
    slope = inv * inv * inv * dots / features
    sublane = iota((128, span), 0)
    turned = jnp.where(sublane == 0, inv, jnp.where(sublane == 1, slope, 0.0)).T
    slot_inv, slot_slope = turned[tokens : tokens + slots2, 0:1], turned[tokens : tokens + slots2, 1:2]
    table = place_table[...].astype(F32)
    taken = jnp.sum(table, axis=0, keepdims=True) > 0.0
    token_inv = jnp.where(taken, jnp.sum(table * slot_inv[:slots], axis=0, keepdims=True), inv[:, :tokens])
    token_slope = jnp.where(taken, jnp.sum(table * slot_slope[:slots], axis=0, keepdims=True), slope[:, :tokens])
    sublane = iota((128, tokens), 0)
    lines = jnp.where(sublane == 0, token_inv, jnp.where(sublane == 1, token_slope, 0.0))
    turned = jnp.where(sublane == 2, taken.astype(F32), lines).T
    inv_col, slope_col, taken_col = turned[:, 0:1], turned[:, 1:2], turned[:, 2:3] > 0.0

    copies = []

    def send(source, target):
        copy = pltpu.make_async_copy(source, target, sem.at[len(copies)])
        copy.start()
        copies.append(copy)

    step = stream.shape[1] // 2
    for c in range(0, stream.shape[1], step):
        cut = slice(c, c + step)
        embed_buffer[:, cut] = (inv_col * scaled_grad[:tokens, cut] - stream[:, cut].astype(F32) * slope_col).astype(BF16)
        send(embed_buffer.at[:, cut], embed_grad.at[:, cut])
        row_grad = slot_inv[slots:] * scaled_grad[tokens:, cut] - rows[slots:, cut].astype(F32) * slot_slope[slots:]
        image_buffer[:, cut] = dot_dims(send_table[...], row_grad.astype(BF16), 0, 0).astype(BF16)
        send(image_buffer.at[:, cut], image_grad.at[:, cut])
    kv_rows = (total[:slots] * slot_inv[:slots]).astype(BF16)
    kv_total = parts[0][...]
    for part in parts[1:]:
        kv_total = kv_total + part[...].astype(F32)
    kv_buffer[...] = jnp.where(taken_col, dot_dims(place_table[...], kv_rows, 0, 0), kv_total * inv_col).astype(BF16)
    send(kv_buffer, key_value)
    for copy in copies:
        copy.wait()


def params(mib=16):
    return pltpu.CompilerParams(vmem_limit_bytes=mib * MIB)


COST = pl.CostEstimate(flops=1024, bytes_accessed=1024, transcendentals=0)


def shape(dims, dtype):
    return jax.ShapeDtypeStruct(dims, dtype)


def call(kernel, name, operands, in_specs, outs, out_specs=None, scratch=(), cost=COST):
    return pl.pallas_call(
        kernel,
        out_shape=outs,
        in_specs=in_specs,
        out_specs=out_specs or [VMEM] * len(outs),
        scratch_shapes=scratch,
        compiler_params=params(),
        cost_estimate=cost,
        name=name,
    )(*operands)


def in_hbm(array):
    return pltpu.with_memory_space_constraint(array, pltpu.HBM)


def swap(array, axis, k):
    return lax.ppermute(array, axis, [(i, i ^ k) for i in range(lax.axis_size(axis))])


def on_device(
    merge_hidden, merge_weight, merge_bias, row_dest, image_pos, text_embed, norm_gain, kv_weight, kv_grad
):
    lane_count, tp_count = lax.axis_size("lane"), lax.axis_size("tp")
    tokens, features = text_embed.shape
    kv_cols = kv_weight.shape[1]
    cols = kv_cols // tp_count
    cap = image_pos.shape[3]
    slots = lane_count * cap
    slots2 = 2 * slots
    group = max(16, 2 * cap)
    width = merge_hidden.shape[1] // (group // (2 * cap)) + kv_cols // (group // cap)
    block = row_dest.shape[0]
    gain = norm_gain.reshape(1, features)
    bias = merge_bias.reshape(1, features)
    own_dest = row_dest.reshape(1, block)
    positions = image_pos.reshape(lane_count, cap)

    other_dest = swap(own_dest, "section", 1)
    half = tp_count // 2
    kept = (text_embed, kv_grad, own_dest, positions, merge_hidden)
    first_part, scaled, first_sums, text, grad, own_dest, positions, hidden = call(
        lambda *refs: first_text_kernel(half, *refs),
        "first_text_kv",
        [in_hbm(array) for array in kept + (gain, kv_weight)],
        [ANY] * 7,
        [shape((tokens, cols), BF16), shape((tokens, features), BF16), shape((tokens, 128), F32)]
        + [pltpu.VMEM(array.shape, array.dtype) for array in kept],
        scratch=[
            pltpu.VMEM((1, features), F32),
            pltpu.VMEM((features, cols), BF16),
            pltpu.SemaphoreType.DMA((7,)),
        ],
    )
    first_part, other_dest = lax.optimization_barrier((first_part, other_dest))
    first_part = swap(first_part, "tp", half)

    *sent, send_table, place_table = call(
        lambda *refs: gather_kernel(lane_count, group, cap, *refs),
        "gather_rows",
        [own_dest, other_dest, positions, hidden, grad],
        [VMEM] * 5,
        [shape((group, width), BF16)] * lane_count + [shape((slots, block), BF16), shape((slots, tokens), BF16)],
    )
    got = [swap(sent[k], "lane", k) for k in range(1, lane_count)]

    steps = [k for k in range(1, tp_count) if k != half] + [0]
    *parts, text_sums = call(
        lambda *refs: text_kernel(steps, *refs),
        "text_kv",
        [scaled, kv_weight, grad, first_sums],
        [VMEM] * 4,
        [shape((tokens, cols), BF16)] * (tp_count - 2) + [shape((tokens, cols), F32), shape((8, tokens), F32)],
    )
    arrived = [swap(part, "tp", k) for part, k in zip(parts, steps[:-1])]

    own, other, grad_rows, text_total = call(
        lambda *refs: merge_kernel(lane_count, cap, *refs),
        "merge_rows",
        [*sent, *got, merge_weight, parts[-1], first_part],
        [VMEM] * (2 * lane_count + 2),
        [
            shape((slots2, features), F32),
            shape((slots2, features), BF16),
            shape((slots2, kv_cols), BF16),
            shape((tokens, cols), F32),
        ],
    )
    other = swap(other, "section", 1)

    span = tokens + round_up(slots2, 128)
    sum_rows = round_up(-(-4 * span // cols), 16)
    placed, *messages = call(
        lambda *refs: slot_kernel(tp_count, sum_rows, *refs),
        "slot_kv",
        [own, other, bias, gain, kv_weight, grad_rows, text_sums],
        [VMEM] * 7,
        [shape((slots2, features), BF16)] + [shape((slots + sum_rows, cols), BF16)] * tp_count,
    )
    messages = [messages[0]] + [swap(messages[k], "tp", k) for k in range(1, tp_count)]

    scaled_grad, stream = call(
        grad_kernel,
        "normed_grad",
        [grad, grad_rows, kv_weight, gain, text, placed, place_table],
        [VMEM] * 7,
        [shape((tokens + slots, features), F32), shape((tokens, features), BF16)],
    )

    key_value, embed_grad, image_grad = call(
        lambda *refs: final_kernel(tp_count, tp_count - 1, features * tp_count, *refs),
        "outputs",
        [placed, scaled_grad, stream, place_table, send_table, *messages, text_total, *arrived],
        [VMEM] * (4 + 2 * tp_count),
        [shape((tokens, cols), BF16), shape((tokens, features), BF16), shape((block, features), BF16)],
        out_specs=[ANY] * 3,
        scratch=[
            pltpu.VMEM((tokens, cols), BF16),
            pltpu.VMEM((tokens, features), BF16),
            pltpu.VMEM((block, features), BF16),
            pltpu.SemaphoreType.DMA((5,)),
        ],
    )
    return (key_value, embed_grad, image_grad)


def solution(mesh):
    in_specs = (
        P("lane", "section"),
        P("section", "tp"),
        P("tp"),
        P(("lane", "section")),
        P("lane", "section", None, None),
        P(("lane", "section"), "tp"),
        P("tp"),
        P("tp", None),
        P(("lane", "section"), None),
    )
    out_specs = (
        P(("lane", "section"), "tp"),
        P(("lane", "section"), "tp"),
        P(("lane", "section"), "tp"),
    )
    return jax.shard_map(
        on_device, mesh=mesh, in_specs=in_specs, out_specs=out_specs, check_vma=False
    )
```

time: 129 us -> 39.3 us (0.30)
  matrix products: 38.2 us -> 0 us
  waiting for transfers between devices: 44.9 us -> 8.9 us
  blocking collectives: 19.1 us -> 0 us
  Pallas kernels: 0 us -> 15.5 us
  between operations: 14.2 us -> 0.76 us
  starting transfers between devices: 3.94 us -> 14 us
  other arithmetic: 5.44 us -> 0.01 us
  local copies, waits for them, and re-layouts: 2.65 us -> 0.03 us
    reduce_scatter x2 -> x0, waiting for transfers between devices: 40.1 us -> none  [the longest x1 29.4 us: on_device(): lax.psum_scatter(jnp.transpose(product.reshape(tokens, 1 * lax.axis_size(...]
    dot_general x7 -> x0, matrix products: 38.2 us -> none  [the longest x1 21.5 us: on_device(): jnp.dot(activated, merge_weight, preferred_element_type=jnp.float32)]
    pallas_call x0 -> x7, Pallas kernels: none -> 15.5 us  [call(): pl.pallas_call(kernel, out_shape=outs, in_specs=in_specs, out_specs=out_s...]
    ppermute x0 -> x11, starting transfers between devices: none -> 14 us  [swap(): lax.ppermute(array, axis, [(i, i ^ k) for i in range(lax.axis_size(axis))])]
    psum x1 -> x0, blocking collectives: 11.9 us -> none  [on_device(): total_squares, total_dots = lax.psum((squares, dot_terms), 'tp')]
    ppermute x0 -> x11, waiting for transfers between devices: none -> 8.9 us  [swap(): lax.ppermute(array, axis, [(i, i ^ k) for i in range(lax.axis_size(axis))])]
    all_to_all x1 -> x0, blocking collectives: 7.21 us -> none  [on_device(): lax.all_to_all(returning.reshape(lane_count, slot_count, -1), 'lane', spl...]
    all_to_all x1 -> x0, waiting for transfers between devices: 4.75 us -> none  [on_device(): lax.all_to_all(outgoing.reshape(lane_count, slot_count, -1), 'lane', spli...]
  transfers between devices with their start and end apart: 3 -> 11, of which waited for: 3 -> 4; matrix products, arithmetic and copies ran while one was open for 5% -> 0% of each run, Pallas kernels for 0% -> 34%
where the time goes in v2:
time: 39.3 us; the launch traced here: 39.2 us
  Pallas kernels  15.5 us (39%)
  starting transfers between devices  14 us (36%)
  waiting for transfers between devices  8.9 us (23%)
  between operations  0.76 us (2%)
    pallas_call x7, Pallas kernels, call(): pl.pallas_call(kernel, out_shape=outs, in_specs=in_specs, out_specs=out_s...  15.5 us
    ppermute x11, starting transfers between devices, swap(): lax.ppermute(array, axis, [(i, i ^ k) for i in range(lax.axis_size(axis))])  14 us
    ppermute x11, waiting for transfers between devices, swap(): lax.ppermute(array, axis, [(i, i ^ k) for i in range(lax.axis_size(axis))])  8.9 us
  transfers between devices with their start and end apart: 11, of which 4 were waited for; matrix products, arithmetic and copies ran while one was open for 0% of the time, Pallas kernels for 34%

profile of v2, /device:TPU:0, one launch (start us, length us, event | category | flops | bytes accessed | tf_op | source)
XLA Modules:
  0.0 39.2 jit_solution(11005887218033796346)
XLA Ops:
  0.6 0.5 %collective-permute-start = (s32[1,256]{1,0:T(1,128)}, s32[1,256]{1,0:T(1,128)S(1)}, u32[]{:S(2)}, u32[]{:S(2)}) collective-permute-start(s32[1,256]{1,0:T(1,128)} %bitcast.13), channel_id=1, source_target_pairs={{0,4},{4,0},{1,5},{5,1},{2,6},{6,2},{3,7},{7,3},{8,12},{12,8},{9,1... | collective-permute-start | bytes 3080 | tf_op jit(solution)/shard_map/ppermute | solution.py:310
  1.2 3.3 %first_text_kv.1 = (bf16[256,512]{1,0:T(8,128)(2,1)S(1)}, bf16[256,2048]{1,0:T(8,128)(2,1)S(1)}, f32[256,128]{1,0:T(8,128)S(1)}, bf16[256,2048]{1,0:T(8,128)(2,1...) custom-call(bf16[256,2048]{1,0:T(8,128)(2,1)} %refs_0_.1, ...), custom_call_target="tpu_custom_call" | custom-call | flops 1024 | bytes 1024 | tf_op jit(solution)/shard_map/first_text_kv/pallas_call | solution.py:293
  4.4 0.0 collective-permute-done.refs_1_
  4.4 3.7 %collective-permute-start.4 = (bf16[256,512]{1,0:T(8,128)(2,1)S(1)}, bf16[256,512]{1,0:T(8,128)(2,1)S(1)}, u32[]{:S(2)}, u32[]{:S(2)}) collective-permute-start(bf16[256,512]{1,0:T(8,128)(2,1)S(1)} %get-tuple-element.47), channel_id=1, source_target_pairs={{0,2},{1,3},{2,0},{3,1},{4,6},{5,7},{6,4},{7,5},{8,10},{9,11},{10,... | collective-permute-start | bytes 786440 | tf_op jit(solution)/shard_map/ppermute | solution.py:310
  8.1 1.3 %gather_rows.1 = (bf16[16,1792]{1,0:T(8,128)(2,1)S(1)}, bf16[16,1792]{1,0:T(8,128)(2,1)S(1)}, bf16[16,1792]{1,0:T(8,128)(2,1)S(1)}, bf16[16,1792]{1,0:T(8,128)(2...) custom-call(s32[1,256]{1,0:T(1,128)S(1)} %get-tuple-element.34.refs_0_, ...), custom_call_target="tpu_custom_call" | custom-call | flops 1024 | bytes 1024 | tf_op jit(solution)/shard_map/gather_rows/pallas_call | solution.py:293
  9.4 1.6 %collective-permute-start.1 = (bf16[16,1792]{1,0:T(8,128)(2,1)S(1)}, bf16[16,1792]{1,0:T(8,128)(2,1)S(1)}, u32[]{:S(2)}, u32[]{:S(2)}) collective-permute-start(bf16[16,1792]{1,0:T(8,128)(2,1)S(1)} %get-tuple-element.41.refs_1_), channel_id=1, source_target_pairs={{0,8},{8,0},{16,24},{24,16},{1,9},{9,1},{17,25},{25,17},{2,10},{10... | collective-permute-start | bytes 172040 | tf_op jit(solution)/shard_map/ppermute | solution.py:310
  11.0 0.0 slice-done
  11.0 1.9 %text_kv.1 = (bf16[256,512]{1,0:T(8,128)(2,1)S(1)}, bf16[256,512]{1,0:T(8,128)(2,1)S(1)}, f32[256,512]{1,0:T(8,128)S(1)}, f32[8,256]{1,0:T(8,128)S(1)}) custom-call(bf16[256,2048]{1,0:T(8,128)(2,1)S(1)} %get-tuple-element.44.refs_0_, bf16[2048,2048]{1,0:T(8,128)(2,1)S(1)} %bitcast.5, bf16[256,2048]{1,0:T(8,128)(2,1)S(1)} %get-tuple-element.39.refs_4_.refs_2_.grad, ...), custom_call_target="tpu_custom_call" | custom-call | flops 1024 | bytes 1024 | tf_op jit(solution)/shard_map/text_kv/pallas_call | solution.py:293
  12.9 1.6 %collective-permute-start.9 = (bf16[256,512]{1,0:T(8,128)(2,1)S(1)}, bf16[256,512]{1,0:T(8,128)(2,1)S(1)}, u32[]{:S(2)}, u32[]{:S(2)}) collective-permute-start(bf16[256,512]{1,0:T(8,128)(2,1)S(1)} %get-tuple-element.63), channel_id=1, source_target_pairs={{0,1},{1,0},{2,3},{3,2},{4,5},{5,4},{6,7},{7,6},{8,9},{9,8},{10,11... | collective-permute-start | bytes 786440 | tf_op jit(solution)/shard_map/ppermute | solution.py:310
  14.6 0.2 collective-permute-start.10
  14.8 1.5 %collective-permute-start.2 = (bf16[16,1792]{1,0:T(8,128)(2,1)S(1)}, bf16[16,1792]{1,0:T(8,128)(2,1)S(1)}, u32[]{:S(2)}, u32[]{:S(2)}) collective-permute-start(bf16[16,1792]{1,0:T(8,128)(2,1)S(1)} %get-tuple-element.42.refs_2_), channel_id=1, source_target_pairs={{0,16},{8,24},{16,0},{24,8},{1,17},{9,25},{17,1},{25,9},{2,18},{10... | collective-permute-start | bytes 172040 | tf_op jit(solution)/shard_map/ppermute | solution.py:310
  16.3 0.0 collective-permute-done.1.refs_4_
  16.3 0.3 collective-permute-start.3
  16.7 2.3 %collective-permute-done.2.refs_5_ = bf16[16,1792]{1,0:T(8,128)(2,1)S(1)} collective-permute-done((bf16[16,1792]{1,0:T(8,128)(2,1)S(1)}, bf16[16,1792]{1,0:T(8,128)(2,1)S(1)}, u32[]{:S(2)}, u32[]{:S(2)}) %collective-permute-start.2) | collective-permute-done | bytes 57376 | tf_op jit(solution)/shard_map/ppermute | solution.py:310
  19.0 2.4 %collective-permute-done.3.refs_6_ = bf16[16,1792]{1,0:T(8,128)(2,1)S(1)} collective-permute-done((bf16[16,1792]{1,0:T(8,128)(2,1)S(1)}, bf16[16,1792]{1,0:T(8,128)(2,1)S(1)}, u32[]{:S(2)}, u32[]{:S(2)}) %collective-permute-start.3) | collective-permute-done | bytes 57376 | tf_op jit(solution)/shard_map/ppermute | solution.py:310
  21.4 0.0 collective-permute-done.4.refs_9_
  21.4 0.0 copy-start
  21.4 0.0 copy-start.1
  21.4 2.2 %merge_rows.1 = (f32[32,2048]{1,0:T(8,128)S(1)}, bf16[32,2048]{1,0:T(8,128)(2,1)S(1)}, bf16[32,2048]{1,0:T(8,128)(2,1)S(1)}, f32[256,512]{1,0:T(8,128)S(1)}) custom-call(bf16[16,1792]{1,0:T(8,128)(2,1)S(1)} %get-tuple-element.40.refs_0_, bf16[16,1792]{1,0:T(8,128)(2,1)S(1)} %get-tuple-element.41.refs_1_, bf16[16,1792]{1,0:T(8,128)(2,1)S(1)} %get-tuple-element.42.refs_2_, ...), custom_call_target="tpu_custom_call" | custom-call | flops 1024 | bytes 1024 | tf_op jit(solution)/shard_map/merge_rows/pallas_call | solution.py:293
  23.7 0.1 collective-permute-start.5
  23.8 1.3 %collective-permute-done.5.refs_1_ = bf16[32,2048]{1,0:T(8,128)(2,1)S(1)} collective-permute-done((bf16[32,2048]{1,0:T(8,128)(2,1)S(1)}, bf16[32,2048]{1,0:T(8,128)(2,1)S(1)}, u32[]{:S(2)}, u32[]{:S(2)}) %collective-permute-start.5) | collective-permute-done | bytes 131104 | tf_op jit(solution)/shard_map/ppermute | solution.py:310
  25.1 1.7 %slot_kv.1 = (bf16[32,2048]{1,0:T(8,128)(2,1)S(1)}, bf16[32,512]{1,0:T(8,128)(2,1)S(1)}, bf16[32,512]{1,0:T(8,128)(2,1)S(1)}, bf16[32,512]{1,0:T(8,128)(2,1)S(1)}, bf16[32,512]{1,0:T(8,128)(2,1)S(1)}) custom-call(f32[32,2048]{1,0:T(8,128)S(1)} %get-tuple-element.48.refs_0_, bf16[32,2048]{1,0:T(8,128)(2,1)S(1)} %collective-permute-done.5.refs_1_, ...), custom_call_target="tpu_custom_call" | custom-call | flops 1024 | bytes 1024 | tf_op jit(solution)/shard_map/slot_kv/pallas_call | solution.py:293
  26.8 0.8 %collective-permute-start.6 = (bf16[32,512]{1,0:T(8,128)(2,1)S(1)}, bf16[32,512]{1,0:T(8,128)(2,1)S(1)}, u32[]{:S(2)}, u32[]{:S(2)}) collective-permute-start(bf16[32,512]{1,0:T(8,128)(2,1)S(1)} %get-tuple-element.59), channel_id=1, source_target_pairs={{0,1},{1,0},{2,3},{3,2},{4,5},{5,4},{6,7},{7,6},{8,9},{9,8},{10,11... | collective-permute-start | bytes 98312 | tf_op jit(solution)/shard_map/ppermute | solution.py:310
  27.6 3.6 %collective-permute-start.7 = (bf16[32,512]{1,0:T(8,128)(2,1)S(1)}, bf16[32,512]{1,0:T(8,128)(2,1)S(1)}, u32[]{:S(2)}, u32[]{:S(2)}) collective-permute-start(bf16[32,512]{1,0:T(8,128)(2,1)S(1)} %get-tuple-element.60), channel_id=1, source_target_pairs={{0,2},{1,3},{2,0},{3,1},{4,6},{5,7},{6,4},{7,5},{8,10},{9,11},{10,... | collective-permute-start | bytes 98312 | tf_op jit(solution)/shard_map/ppermute | solution.py:310
  31.2 0.0 collective-permute-start.8
  31.2 2.8 %normed_grad.1 = (f32[272,2048]{1,0:T(8,128)S(1)}, bf16[256,2048]{1,0:T(8,128)(2,1)S(1)}) custom-call(bf16[256,2048]{1,0:T(8,128)(2,1)S(1)} %get-tuple-element.39.refs_4_.refs_2_.grad, bf16[32,2048]{1,0:T(8,128)(2,1)S(1)} %get-tuple-element.50.refs_5_.grad_rows, bf16[2048,2048]{1,0:T(8,128)(2,1)S(1)} %bitcast.5, f32[1,2048]{1,0:T(1,128)S(1)} %bitcast.10, ...), custom_call_target="tpu_custom_call" | custom-call | flops 1024 | bytes 1024 | tf_op jit(solution)/shard_map/normed_grad/pallas_call | solution.py:293
  34.1 0.0 collective-permute-done.9.refs_10_
  34.1 0.0 collective-permute-done.10.refs_11_
  34.1 0.0 collective-permute-done.6.refs_6_
  34.1 0.0 collective-permute-done.7.refs_7_
  34.1 2.8 %collective-permute-done.8.refs_8_ = bf16[32,512]{1,0:T(8,128)(2,1)S(1)} collective-permute-done((bf16[32,512]{1,0:T(8,128)(2,1)S(1)}, bf16[32,512]{1,0:T(8,128)(2,1)S(1)}, u32[]{:S(2)}, u32[]{:S(2)}) %collective-permute-start.8) | collective-permute-done | bytes 32800 | tf_op jit(solution)/shard_map/ppermute | solution.py:310
  36.9 2.2 %outputs.1 = (bf16[256,512]{1,0:T(8,128)(2,1)}, bf16[256,2048]{1,0:T(8,128)(2,1)}, bf16[256,2048]{1,0:T(8,128)(2,1)}) custom-call(bf16[32,2048]{1,0:T(8,128)(2,1)S(1)} %get-tuple-element.52.rows.refs_0_, f32[272,2048]{1,0:T(8,128)S(1)} %get-tuple-element.55.refs_1_, bf16[256,2048]{1,0:T(8,128)(2,1)S(1)} %get-tuple-element.56.refs_2_, ...), custom_call_target="tpu_custom_call" | custom-call | flops 1024 | bytes 1024 | tf_op jit(solution)/shard_map/outputs/pallas_call | solution.py:293
  (13 shorter events, 0.0 us)
Async XLA Ops:
  0.6 3.8 %collective-permute-start = (s32[1,256]{1,0:T(1,128)}, s32[1,256]{1,0:T(1,128)S(1)}, u32[]{:S(2)}, u32[]{:S(2)}) collective-permute-start(s32[1,256]{1,0:T(1,128)} %bitcast.13), channel_id=1, source_target_pairs={{0,4},{4,0},{1,5},{5,1},{2,6},{6,2},{3,7},{7,3},{8,12},{12,8},{9,1... | collective-permute-start | bytes 3080 | tf_op jit(solution)/shard_map/ppermute | solution.py:310
  1.1 9.8 %slice-start = ((s8[8388608]{0:T(1024)(128)(4,1)}), s8[4194304]{0:T(1024)(128)(4,1)S(1)}, s32[]{:S(2)}) async-start(s8[8388608]{0:T(1024)(128)(4,1)} %bitcast.4), calls=%async_computation | async-start | bytes 8388608
  1.2 9.8 %slice-start.1 = ((s8[8388608]{0:T(1024)(128)(4,1)}), s8[4194304]{0:T(1024)(128)(4,1)S(1)}, s32[]{:S(2)}) async-start(s8[8388608]{0:T(1024)(128)(4,1)} %bitcast.4), calls=%async_computation.1 | async-start | bytes 8388608
  1.2 20.2 %slice-start.2 = ((s8[10485760]{0:T(1024)(128)(4,1)}), s8[4194304]{0:T(1024)(128)(4,1)S(1)}, s32[]{:S(2)}) async-start(s8[10485760]{0:T(1024)(128)(4,1)} %bitcast.6), calls=%async_computation.2 | async-start | bytes 8388608
  1.2 20.2 %slice-start.3 = ((s8[10485760]{0:T(1024)(128)(4,1)}), s8[4194304]{0:T(1024)(128)(4,1)S(1)}, s32[]{:S(2)}) async-start(s8[10485760]{0:T(1024)(128)(4,1)} %bitcast.6), calls=%async_computation.3 | async-start | bytes 8388608
  4.4 17.0 %collective-permute-start.4 = (bf16[256,512]{1,0:T(8,128)(2,1)S(1)}, bf16[256,512]{1,0:T(8,128)(2,1)S(1)}, u32[]{:S(2)}, u32[]{:S(2)}) collective-permute-start(bf16[256,512]{1,0:T(8,128)(2,1)S(1)} %get-tuple-element.47), channel_id=1, source_target_pairs={{0,2},{1,3},{2,0},{3,1},{4,6},{5,7},{6,4},{7,5},{8,10},{9,11},{10,... | collective-permute-start | bytes 786440 | tf_op jit(solution)/shard_map/ppermute | solution.py:310
  9.4 6.9 %collective-permute-start.1 = (bf16[16,1792]{1,0:T(8,128)(2,1)S(1)}, bf16[16,1792]{1,0:T(8,128)(2,1)S(1)}, u32[]{:S(2)}, u32[]{:S(2)}) collective-permute-start(bf16[16,1792]{1,0:T(8,128)(2,1)S(1)} %get-tuple-element.41.refs_1_), channel_id=1, source_target_pairs={{0,8},{8,0},{16,24},{24,16},{1,9},{9,1},{17,25},{25,17},{2,10},{10... | collective-permute-start | bytes 172040 | tf_op jit(solution)/shard_map/ppermute | solution.py:310
  11.0 10.4 %slice-start.4 = ((s8[10485760]{0:T(1024)(128)(4,1)}), s8[2097152]{0:T(1024)(128)(4,1)S(1)}, s32[]{:S(2)}) async-start(s8[10485760]{0:T(1024)(128)(4,1)} %bitcast.6), calls=%async_computation.4 | async-start | bytes 4194304
  12.9 21.1 %collective-permute-start.9 = (bf16[256,512]{1,0:T(8,128)(2,1)S(1)}, bf16[256,512]{1,0:T(8,128)(2,1)S(1)}, u32[]{:S(2)}, u32[]{:S(2)}) collective-permute-start(bf16[256,512]{1,0:T(8,128)(2,1)S(1)} %get-tuple-element.63), channel_id=1, source_target_pairs={{0,1},{1,0},{2,3},{3,2},{4,5},{5,4},{6,7},{7,6},{8,9},{9,8},{10,11... | collective-permute-start | bytes 786440 | tf_op jit(solution)/shard_map/ppermute | solution.py:310
  14.6 19.5 %collective-permute-start.10 = (bf16[256,512]{1,0:T(8,128)(2,1)S(1)}, bf16[256,512]{1,0:T(8,128)(2,1)S(1)}, u32[]{:S(2)}, u32[]{:S(2)}) collective-permute-start(bf16[256,512]{1,0:T(8,128)(2,1)S(1)} %get-tuple-element.64), channel_id=1, source_target_pairs={{0,3},{1,2},{2,1},{3,0},{4,7},{5,6},{6,5},{7,4},{8,11},{9,10},{10,... | collective-permute-start | bytes 786440 | tf_op jit(solution)/shard_map/ppermute | solution.py:310
  14.8 4.2 %collective-permute-start.2 = (bf16[16,1792]{1,0:T(8,128)(2,1)S(1)}, bf16[16,1792]{1,0:T(8,128)(2,1)S(1)}, u32[]{:S(2)}, u32[]{:S(2)}) collective-permute-start(bf16[16,1792]{1,0:T(8,128)(2,1)S(1)} %get-tuple-element.42.refs_2_), channel_id=1, source_target_pairs={{0,16},{8,24},{16,0},{24,8},{1,17},{9,25},{17,1},{25,9},{2,18},{10... | collective-permute-start | bytes 172040 | tf_op jit(solution)/shard_map/ppermute | solution.py:310
  16.3 5.1 %collective-permute-start.3 = (bf16[16,1792]{1,0:T(8,128)(2,1)S(1)}, bf16[16,1792]{1,0:T(8,128)(2,1)S(1)}, u32[]{:S(2)}, u32[]{:S(2)}) collective-permute-start(bf16[16,1792]{1,0:T(8,128)(2,1)S(1)} %get-tuple-element.43.refs_3_), channel_id=1, source_target_pairs={{0,24},{8,16},{16,8},{24,0},{1,25},{9,17},{17,9},{25,1},{2,26},{10... | collective-permute-start | bytes 172040 | tf_op jit(solution)/shard_map/ppermute | solution.py:310
  21.4 3.7 %copy-start = (f32[2048]{0:T(1024)S(1)}, f32[2048]{0:T(1024)}, u32[]{:S(2)}) copy-start(f32[2048]{0:T(1024)} %param.15) | copy-start | bytes 24580
  21.4 3.7 %copy-start.1 = (f32[2048]{0:T(1024)S(1)}, f32[2048]{0:T(1024)}, u32[]{:S(2)}) copy-start(f32[2048]{0:T(1024)} %param.11) | copy-start | bytes 24580
  23.7 1.4 %collective-permute-start.5 = (bf16[32,2048]{1,0:T(8,128)(2,1)S(1)}, bf16[32,2048]{1,0:T(8,128)(2,1)S(1)}, u32[]{:S(2)}, u32[]{:S(2)}) collective-permute-start(bf16[32,2048]{1,0:T(8,128)(2,1)S(1)} %get-tuple-element.49), channel_id=1, source_target_pairs={{0,4},{4,0},{1,5},{5,1},{2,6},{6,2},{3,7},{7,3},{8,12},{12,8},{9,1... | collective-permute-start | bytes 393224 | tf_op jit(solution)/shard_map/ppermute | solution.py:310
  26.8 7.3 %collective-permute-start.6 = (bf16[32,512]{1,0:T(8,128)(2,1)S(1)}, bf16[32,512]{1,0:T(8,128)(2,1)S(1)}, u32[]{:S(2)}, u32[]{:S(2)}) collective-permute-start(bf16[32,512]{1,0:T(8,128)(2,1)S(1)} %get-tuple-element.59), channel_id=1, source_target_pairs={{0,1},{1,0},{2,3},{3,2},{4,5},{5,4},{6,7},{7,6},{8,9},{9,8},{10,11... | collective-permute-start | bytes 98312 | tf_op jit(solution)/shard_map/ppermute | solution.py:310
  27.6 6.5 %collective-permute-start.7 = (bf16[32,512]{1,0:T(8,128)(2,1)S(1)}, bf16[32,512]{1,0:T(8,128)(2,1)S(1)}, u32[]{:S(2)}, u32[]{:S(2)}) collective-permute-start(bf16[32,512]{1,0:T(8,128)(2,1)S(1)} %get-tuple-element.60), channel_id=1, source_target_pairs={{0,2},{1,3},{2,0},{3,1},{4,6},{5,7},{6,4},{7,5},{8,10},{9,11},{10,... | collective-permute-start | bytes 98312 | tf_op jit(solution)/shard_map/ppermute | solution.py:310
  31.2 5.7 %collective-permute-start.8 = (bf16[32,512]{1,0:T(8,128)(2,1)S(1)}, bf16[32,512]{1,0:T(8,128)(2,1)S(1)}, u32[]{:S(2)}, u32[]{:S(2)}) collective-permute-start(bf16[32,512]{1,0:T(8,128)(2,1)S(1)} %get-tuple-element.61), channel_id=1, source_target_pairs={{0,3},{1,2},{2,1},{3,0},{4,7},{5,6},{6,5},{7,4},{8,11},{9,10},{10,... | collective-permute-start | bytes 98312 | tf_op jit(solution)/shard_map/ppermute | solution.py:310

commit v3 on v2

--- a/solution.py
+++ b/solution.py
@@ -51,53 +51,59 @@
     return match.astype(F32).astype(BF16)
 
 
-def first_text_kernel(step, *refs):
-    sources, (part, scaled, sums), kept, (gain, weight, sem) = refs[:7], refs[7:10], refs[10:15], refs[15:]
-    text, grad = kept[:2]
+def first_text_kernel(step, text_hbm, gain_hbm, weight_hbm, part, scaled, text, gain, weight, sem):
     span = peer_columns("tp", step, part.shape[1])
-    text_hbm, grad_hbm, dest_hbm, pos_hbm, hidden_hbm, gain_hbm, weight_hbm = sources
-    pairs = [
-        (text_hbm, text),
-        (gain_hbm, gain),
-        (weight_hbm.at[:, span], weight),
-        (grad_hbm, grad),
-        (dest_hbm, kept[2]),
-        (pos_hbm, kept[3]),
-        (hidden_hbm, kept[4]),
-    ]
+    gain_copy = pltpu.make_async_copy(gain_hbm, gain, sem.at[0])
+    gain_copy.start()
+    count = 4 if text.shape[1] % 512 == 0 else 1
+    size = text.shape[1] // count
+    cuts = [slice(i * size, (i + 1) * size) for i in range(count)]
+    copies = []
+    for i, cut in enumerate(cuts):
+        pair = (
+            pltpu.make_async_copy(text_hbm.at[:, cut], text.at[:, cut], sem.at[2 * i + 1]),
+            pltpu.make_async_copy(weight_hbm.at[cut, span], weight.at[cut], sem.at[2 * i + 2]),
+        )
+        for copy in pair:
+            copy.start()
+        copies.append(pair)
+    gain_copy.wait()
+    total = jnp.zeros(part.shape, F32)
+    for cut, pair in zip(cuts, copies):
+        pair[0].wait()
+        scaled[:, cut] = (text[:, cut].astype(F32) * gain[:, cut]).astype(BF16)
+        pair[1].wait()
+        total = total + dot(scaled[:, cut], weight[cut])
+    part[...] = total.astype(BF16)
+
+
+def text_kernel(first_step, steps, scaled, weight, grad, text, first_part, *refs):
+    parts, sums = refs[:-1], refs[-1]
+    cols = parts[0].shape[1]
+
+    def row_dots(product, span):
+        return jnp.sum(product * grad[:, span].astype(F32), axis=1, keepdims=True)
+
+    dots = row_dots(first_part[...].astype(F32), peer_columns("tp", first_step, cols))
+    for step, part in zip(steps, parts):
+        span = peer_columns("tp", step, cols)
+        product = dot(scaled[...], weight[:, span])
+        part[...] = product.astype(part.dtype)
+        dots = dots + row_dots(product, span)
+    wide = text[...].astype(F32)
+    squares = jnp.sum(wide * wide, axis=1, keepdims=True)
+    lane = iota((text.shape[0], 128), 1)
+    sums[...] = jnp.where(lane == 0, squares, jnp.where(lane == 1, dots, 0.0)).T[:8]
+
+
+def gather_kernel(lane_count, group, cap, other_ref, own_hbm, pos_hbm, grad, hidden, *refs):
+    payloads, (send_table, place_table, own_ref, pos_ref, sem) = refs[:lane_count], refs[lane_count:]
+    pairs = [(own_hbm, own_ref), (pos_hbm, pos_ref)]
     copies = [pltpu.make_async_copy(source, target, sem.at[i]) for i, (source, target) in enumerate(pairs)]
     for copy in copies:
         copy.start()
     copies[0].wait()
     copies[1].wait()
-    wide = text[...].astype(F32)
-    squares = jnp.sum(wide * wide, axis=1, keepdims=True)
-    scaled[...] = (wide * gain[...]).astype(BF16)
-    copies[2].wait()
-    product = dot(scaled[...], weight[...])
-    part[...] = product.astype(BF16)
-    copies[3].wait()
-    dots = jnp.sum(product * grad[:, span].astype(F32), axis=1, keepdims=True)
-    lane = iota(sums.shape, 1)
-    sums[...] = jnp.where(lane == 0, squares, jnp.where(lane == 1, dots, 0.0))
-    for copy in copies[4:]:
-        copy.wait()
-
-
-def text_kernel(steps, scaled, weight, grad, sums, *refs):
-    parts, sums_out = refs[:-1], refs[-1]
-    dots = jnp.zeros((scaled.shape[0], 1), F32)
-    for step, part in zip(steps, parts):
-        span = peer_columns("tp", step, part.shape[1])
-        product = dot(scaled[...], weight[:, span])
-        part[...] = product.astype(part.dtype)
-        dots = dots + jnp.sum(product * grad[:, span].astype(F32), axis=1, keepdims=True)
-    lane = iota(sums.shape, 1)
-    sums_out[...] = (sums[...] + jnp.where(lane == 1, dots, 0.0)).T[:8]
-
-
-def gather_kernel(lane_count, group, cap, own_ref, other_ref, pos_ref, hidden, grad, *refs):
-    payloads, (send_table, place_table) = refs[:lane_count], refs[lane_count:]
     rows = lane_count * group
     slots = lane_count * cap
     block, tokens = own_ref.shape[1], grad.shape[0]
@@ -115,18 +121,6 @@
 
     own = select(own_ref[...], 0)
     other = select(other_ref[...], cap)
-    section = lax.axis_index("section")
-    own_rows = pl.ds(pl.multiple_of(section * block, block), block)
-    other_rows = pl.ds(pl.multiple_of((1 - section) * block, block), block)
-    folds = group // (2 * cap)
-    width = hidden.shape[1] // folds
-    picked = jnp.zeros((rows, width), F32)
-    for i in range(folds):
-        here = (place >= 2 * cap * i) & (place < 2 * cap * (i + 1))
-        cut = slice(i * width, (i + 1) * width)
-        picked = picked + dot(mask(own & here), hidden[own_rows, cut]) + dot(mask(other & here), hidden[other_rows, cut])
-    active = 0.5 * picked * (1.0 + lax.erf(picked * np.float32(math.sqrt(0.5))))
-
     lane_pick = mask((iota((rows, lane_count), 0) >> int(math.log2(group))) ^ lane == iota((rows, lane_count), 1))
     high, low = pos_ref[...] >> 7, pos_ref[...] & 127
     spread = dot(lane_pick, high.astype(F32).astype(BF16)) * 128.0 + dot(lane_pick, low.astype(F32).astype(BF16))
@@ -140,6 +134,18 @@
     for i in range(grad_folds):
         here = (taken_place >= cap * i) & (taken_place < cap * (i + 1))
         grad_rows = grad_rows + dot(mask(taken & here), grad[:, i * grad_width : (i + 1) * grad_width])
+    section = lax.axis_index("section")
+    own_rows = pl.ds(pl.multiple_of(section * block, block), block)
+    other_rows = pl.ds(pl.multiple_of((1 - section) * block, block), block)
+    folds = group // (2 * cap)
+    width = hidden.shape[1] // folds
+    picked = jnp.zeros((rows, width), F32)
+    for i in range(folds):
+        here = (place >= 2 * cap * i) & (place < 2 * cap * (i + 1))
+        cut = slice(i * width, (i + 1) * width)
+        picked = picked + dot(mask(own & here), hidden[own_rows, cut]) + dot(mask(other & here), hidden[other_rows, cut])
+    active = 0.5 * picked * (1.0 + lax.erf(picked * np.float32(math.sqrt(0.5))))
+
     for k in range(lane_count):
         cut = slice(k * group, (k + 1) * group)
         payloads[k][:, :width] = active[cut].astype(BF16)
@@ -151,8 +157,7 @@
 
 def merge_kernel(lane_count, cap, *refs):
     got_refs, sent_refs = (refs[0],) + refs[lane_count : 2 * lane_count - 1], refs[:lane_count]
-    weight, text_part, first_part, own, other, grad_rows, text_total = refs[2 * lane_count - 1 :]
-    text_total[...] = text_part[...] + first_part[...].astype(F32)
+    weight, own, other, grad_rows = refs[2 * lane_count - 1 :]
     group = refs[0].shape[0]
     rows = lane_count * group
     slots = lane_count * cap
@@ -179,7 +184,10 @@
         other[:, c : c + step] = total[2 * slots :].astype(BF16)
 
 
-def slot_kernel(tp_count, sum_rows, own, other, bias, gain, weight, grad_rows, text_sums, rows, *messages):
+def slot_kernel(
+    tp_count, own, other, bias, gain, weight, grad_rows, text_sums, text_part, first_part, rows, text_total, *messages
+):
+    text_total[...] = text_part[...] + first_part[...].astype(F32)
     slots2 = own.shape[0]
     slots = slots2 // 2
     placed = (own[...] + other[...].astype(F32) + bias[...]).astype(BF16)
@@ -187,13 +195,13 @@
     wide = placed.astype(F32)
     squares = jnp.sum(wide * wide, axis=1, keepdims=True)
     scaled = (wide * gain[...]).astype(BF16)
-    cols = messages[0].shape[1]
+    cols = messages[0].shape[1] - 128
     dots = jnp.zeros_like(squares)
     for k in range(tp_count):
         span = peer_columns("tp", k, cols)
         part = dot(scaled, weight[:, span])
         dots = dots + jnp.sum(part * grad_rows[:, span].astype(F32), axis=1, keepdims=True)
-        messages[k][:slots] = part[:slots].astype(BF16)
+        messages[k][:, :cols] = part[:slots].astype(BF16)
     lane = iota((slots2, 128), 1)
     columns = jnp.where(lane == 0, squares, jnp.where(lane == 1, dots, 0.0))
     padded = round_up(slots2, 128)
@@ -206,12 +214,12 @@
         high = total.astype(BF16).astype(F32)
         pieces += [high, total - high]
     line = jnp.concatenate(pieces, axis=1)
-    message = jnp.zeros((sum_rows, cols), F32)
-    sublane = iota((sum_rows, cols), 0)
-    for i in range(line.shape[1] // cols):
-        message = jnp.where(sublane == i, line[:, i * cols : (i + 1) * cols], message)
+    message = jnp.zeros((slots, 128), F32)
+    sublane = iota((slots, 128), 0)
+    for i in range(line.shape[1] // 128):
+        message = jnp.where(sublane == i, line[:, i * 128 : (i + 1) * 128], message)
     for k in range(tp_count):
-        messages[k][slots:] = message.astype(BF16)
+        messages[k][:, cols:] = message.astype(BF16)
 
 
 def grad_kernel(grad, grad_rows, weight, gain, text, rows, place_table, out, stream):
@@ -236,7 +244,7 @@
     for message in messages[1:]:
         total = total + message[...].astype(F32)
     span = tokens + round_up(slots2, 128)
-    line = jnp.concatenate([total[slots + i : slots + i + 1] for i in range(4 * span // cols)], axis=1)
+    line = jnp.concatenate([total[i : i + 1, cols:] for i in range(4 * span // 128)], axis=1)
     squares = line[:, :span] + line[:, span : 2 * span]
     dots = line[:, 2 * span : 3 * span] + line[:, 3 * span :]
     inv = lax.rsqrt(squares / features + EPSILON)
@@ -268,7 +276,7 @@
         row_grad = slot_inv[slots:] * scaled_grad[tokens:, cut] - rows[slots:, cut].astype(F32) * slot_slope[slots:]
         image_buffer[:, cut] = dot_dims(send_table[...], row_grad.astype(BF16), 0, 0).astype(BF16)
         send(image_buffer.at[:, cut], image_grad.at[:, cut])
-    kv_rows = (total[:slots] * slot_inv[:slots]).astype(BF16)
+    kv_rows = (total[:, :cols] * slot_inv[:slots]).astype(BF16)
     kv_total = parts[0][...]
     for part in parts[1:]:
         kv_total = kv_total + part[...].astype(F32)
@@ -282,7 +290,15 @@
     return pltpu.CompilerParams(vmem_limit_bytes=mib * MIB)
 
 
-COST = pl.CostEstimate(flops=1024, bytes_accessed=1024, transcendentals=0)
+def cost_of(flops):
+    return pl.CostEstimate(flops=flops, bytes_accessed=1024, transcendentals=0)
+
+
+COST = cost_of(1024)
+MERGE_COST = cost_of(1024)
+GRAD_COST = cost_of(1000000000)
+TEXT_COST = cost_of(1024)
+GATHER_COST = cost_of(4000000000)
 
 
 def shape(dims, dtype):
@@ -330,73 +346,76 @@
 
     other_dest = swap(own_dest, "section", 1)
     half = tp_count // 2
-    kept = (text_embed, kv_grad, own_dest, positions, merge_hidden)
-    first_part, scaled, first_sums, text, grad, own_dest, positions, hidden = call(
+    first_part, scaled, text = call(
         lambda *refs: first_text_kernel(half, *refs),
         "first_text_kv",
-        [in_hbm(array) for array in kept + (gain, kv_weight)],
-        [ANY] * 7,
-        [shape((tokens, cols), BF16), shape((tokens, features), BF16), shape((tokens, 128), F32)]
-        + [pltpu.VMEM(array.shape, array.dtype) for array in kept],
+        [in_hbm(array) for array in (text_embed, gain, kv_weight)],
+        [ANY] * 3,
+        [shape((tokens, cols), BF16), shape((tokens, features), BF16), pltpu.VMEM(text_embed.shape, BF16)],
         scratch=[
             pltpu.VMEM((1, features), F32),
             pltpu.VMEM((features, cols), BF16),
-            pltpu.SemaphoreType.DMA((7,)),
+            pltpu.SemaphoreType.DMA((9,)),
         ],
     )
     first_part, other_dest = lax.optimization_barrier((first_part, other_dest))
-    first_part = swap(first_part, "tp", half)
+    first_arrived = swap(first_part, "tp", half)
 
     *sent, send_table, place_table = call(
         lambda *refs: gather_kernel(lane_count, group, cap, *refs),
         "gather_rows",
-        [own_dest, other_dest, positions, hidden, grad],
+        [other_dest, in_hbm(own_dest), in_hbm(positions), kv_grad, merge_hidden],
+        [VMEM, ANY, ANY, VMEM, VMEM],
+        [shape((group, width), BF16)] * lane_count
+        + [shape((slots, block), BF16), shape((slots, tokens), BF16)],
+        scratch=[
+            pltpu.VMEM(own_dest.shape, jnp.int32),
+            pltpu.VMEM(positions.shape, jnp.int32),
+            pltpu.SemaphoreType.DMA((2,)),
+        ],
+        cost=GATHER_COST,
+    )
+    send_table, kv_weight, merge_weight = lax.optimization_barrier((send_table, kv_weight, merge_weight))
+    got = [swap(sent[k], "lane", k) for k in range(1, lane_count)]
+
+    steps = [k for k in range(1, tp_count) if k != half] + [0]
+    *parts, text_own, text_sums = call(
+        lambda *refs: text_kernel(half, steps, *refs),
+        "text_kv",
+        [scaled, kv_weight, kv_grad, text, first_part],
         [VMEM] * 5,
-        [shape((group, width), BF16)] * lane_count + [shape((slots, block), BF16), shape((slots, tokens), BF16)],
-    )
-    got = [swap(sent[k], "lane", k) for k in range(1, lane_count)]
-
-    steps = [k for k in range(1, tp_count) if k != half] + [0]
-    *parts, text_sums = call(
-        lambda *refs: text_kernel(steps, *refs),
-        "text_kv",
-        [scaled, kv_weight, grad, first_sums],
-        [VMEM] * 4,
         [shape((tokens, cols), BF16)] * (tp_count - 2) + [shape((tokens, cols), F32), shape((8, tokens), F32)],
-    )
-    arrived = [swap(part, "tp", k) for part, k in zip(parts, steps[:-1])]
-
-    own, other, grad_rows, text_total = call(
+        cost=TEXT_COST,
+    )
+    arrived = [swap(part, "tp", k) for part, k in zip(parts, steps)]
+
+    own, other, grad_rows = call(
         lambda *refs: merge_kernel(lane_count, cap, *refs),
         "merge_rows",
-        [*sent, *got, merge_weight, parts[-1], first_part],
-        [VMEM] * (2 * lane_count + 2),
-        [
-            shape((slots2, features), F32),
-            shape((slots2, features), BF16),
-            shape((slots2, kv_cols), BF16),
-            shape((tokens, cols), F32),
-        ],
+        [*sent, *got, merge_weight],
+        [VMEM] * (2 * lane_count),
+        [shape((slots2, features), F32), shape((slots2, features), BF16), shape((slots2, kv_cols), BF16)],
+        cost=MERGE_COST,
     )
     other = swap(other, "section", 1)
 
-    span = tokens + round_up(slots2, 128)
-    sum_rows = round_up(-(-4 * span // cols), 16)
-    placed, *messages = call(
-        lambda *refs: slot_kernel(tp_count, sum_rows, *refs),
+    placed, text_total, *messages = call(
+        lambda *refs: slot_kernel(tp_count, *refs),
         "slot_kv",
-        [own, other, bias, gain, kv_weight, grad_rows, text_sums],
-        [VMEM] * 7,
-        [shape((slots2, features), BF16)] + [shape((slots + sum_rows, cols), BF16)] * tp_count,
+        [own, other, bias, gain, kv_weight, grad_rows, text_sums, text_own, first_arrived],
+        [VMEM] * 9,
+        [shape((slots2, features), BF16), shape((tokens, cols), F32)]
+        + [shape((slots, cols + 128), BF16)] * tp_count,
     )
     messages = [messages[0]] + [swap(messages[k], "tp", k) for k in range(1, tp_count)]
 
     scaled_grad, stream = call(
         grad_kernel,
         "normed_grad",
-        [grad, grad_rows, kv_weight, gain, text, placed, place_table],
+        [kv_grad, grad_rows, kv_weight, gain, text, placed, place_table],
         [VMEM] * 7,
         [shape((tokens + slots, features), F32), shape((tokens, features), BF16)],
+        cost=GRAD_COST,
     )
 
     key_value, embed_grad, image_grad = call(

time: 39.3 us -> 35.2 us (0.90)
  waiting for transfers between devices: 8.9 us -> 4.43 us
    ppermute x11, waiting for transfers between devices: 8.9 us -> 4.43 us  [swap(): lax.ppermute(array, axis, [(i, i ^ k) for i in range(lax.axis_size(axis))])]
  transfers between devices with their start and end apart: 11 -> 11, of which waited for: 4 -> 5; matrix products, arithmetic and copies ran while one was open for 0% -> 0% of each run, Pallas kernels for 34% -> 39%
where the time goes in v3:
time: 35.2 us; the launch traced here: 35 us
  Pallas kernels  15.8 us (45%)
  starting transfers between devices  14 us (40%)
  waiting for transfers between devices  4.43 us (13%)
  between operations  0.74 us (2%)
    pallas_call x7, Pallas kernels, call(): pl.pallas_call(kernel, out_shape=outs, in_specs=in_specs, out_specs=out_s...  15.8 us
    ppermute x11, starting transfers between devices, swap(): lax.ppermute(array, axis, [(i, i ^ k) for i in range(lax.axis_size(axis))])  14 us
    ppermute x11, waiting for transfers between devices, swap(): lax.ppermute(array, axis, [(i, i ^ k) for i in range(lax.axis_size(axis))])  4.43 us
  transfers between devices with their start and end apart: 11, of which 5 were waited for; matrix products, arithmetic and copies ran while one was open for 0% of the time, Pallas kernels for 39%

profile of v3, /device:TPU:0, one launch (start us, length us, event | category | flops | bytes accessed | tf_op | source)
XLA Modules:
  0.0 35.0 jit_solution(2135277488546011248)
XLA Ops:
  0.7 0.5 %collective-permute-start = (s32[1,256]{1,0:T(1,128)}, s32[1,256]{1,0:T(1,128)S(1)}, u32[]{:S(2)}, u32[]{:S(2)}) collective-permute-start(s32[1,256]{1,0:T(1,128)} %bitcast.13), channel_id=1, source_target_pairs={{0,4},{4,0},{1,5},{5,1},{2,6},{6,2},{3,7},{7,3},{8,12},{12,8},{9,1... | collective-permute-start | bytes 3080 | tf_op jit(solution)/shard_map/ppermute | solution.py:326
  1.2 2.6 %first_text_kv.1 = (bf16[256,512]{1,0:T(8,128)(2,1)S(1)}, bf16[256,2048]{1,0:T(8,128)(2,1)S(1)}, bf16[256,2048]{1,0:T(8,128)(2,1)S(1)}) custom-call(bf16[256,2048]{1,0:T(8,128)(2,1)} %refs_0_.1, f32[1,2048]{1,0:T(1,128)} %bitcast.8, bf16[2048,2048]{1,0:T(8,128)(2,1)} %weight), custom_call_target="tpu_custom_call" | custom-call | flops 1024 | bytes 1024 | tf_op jit(solution)/shard_map/first_text_kv/pallas_call | solution.py:309
  3.8 0.0 collective-permute-done.refs_0_
  3.8 3.6 %collective-permute-start.5 = (bf16[256,512]{1,0:T(8,128)(2,1)S(1)}, bf16[256,512]{1,0:T(8,128)(2,1)S(1)}, u32[]{:S(2)}, u32[]{:S(2)}) collective-permute-start(bf16[256,512]{1,0:T(8,128)(2,1)S(1)} %get-tuple-element.46.refs_4_), channel_id=1, source_target_pairs={{0,2},{1,3},{2,0},{3,1},{4,6},{5,7},{6,4},{7,5},{8,10},{9,11},{10,... | collective-permute-start | bytes 786440 | tf_op jit(solution)/shard_map/ppermute | solution.py:326
  7.4 0.0 copy-done
  7.4 0.0 slice-start.3
  7.4 1.9 %gather_rows.1 = (bf16[16,1792]{1,0:T(8,128)(2,1)S(1)}, bf16[16,1792]{1,0:T(8,128)(2,1)S(1)}, bf16[16,1792]{1,0:T(8,128)(2,1)S(1)}, bf16[16,1792]{1,0:T(8,128)(2...) custom-call(s32[1,256]{1,0:T(1,128)S(1)} %collective-permute-done.refs_0_, s32[1,256]{1,0:T(1,128)} %bitcast.14, ...), custom_call_target="tpu_custom_call" | custom-call | flops 4000000000 | bytes 1024 | tf_op jit(solution)/shard_map/gather_rows/pallas_call | solution.py:309
  9.4 1.6 %collective-permute-start.1 = (bf16[16,1792]{1,0:T(8,128)(2,1)S(1)}, bf16[16,1792]{1,0:T(8,128)(2,1)S(1)}, u32[]{:S(2)}, u32[]{:S(2)}) collective-permute-start(bf16[16,1792]{1,0:T(8,128)(2,1)S(1)} %get-tuple-element.35.refs_1_), channel_id=1, source_target_pairs={{0,8},{8,0},{16,24},{24,16},{1,9},{9,1},{17,25},{25,17},{2,10},{10... | collective-permute-start | bytes 172040 | tf_op jit(solution)/shard_map/ppermute | solution.py:326
  11.0 1.5 %collective-permute-start.2 = (bf16[16,1792]{1,0:T(8,128)(2,1)S(1)}, bf16[16,1792]{1,0:T(8,128)(2,1)S(1)}, u32[]{:S(2)}, u32[]{:S(2)}) collective-permute-start(bf16[16,1792]{1,0:T(8,128)(2,1)S(1)} %get-tuple-element.36.refs_2_), channel_id=1, source_target_pairs={{0,16},{8,24},{16,0},{24,8},{1,17},{9,25},{17,1},{25,9},{2,18},{10... | collective-permute-start | bytes 172040 | tf_op jit(solution)/shard_map/ppermute | solution.py:326
  12.5 0.5 %collective-permute-start.3 = (bf16[16,1792]{1,0:T(8,128)(2,1)S(1)}, bf16[16,1792]{1,0:T(8,128)(2,1)S(1)}, u32[]{:S(2)}, u32[]{:S(2)}) collective-permute-start(bf16[16,1792]{1,0:T(8,128)(2,1)S(1)} %get-tuple-element.37.refs_3_), channel_id=1, source_target_pairs={{0,24},{8,16},{16,8},{24,0},{1,25},{9,17},{17,9},{25,1},{2,26},{10... | collective-permute-start | bytes 172040 | tf_op jit(solution)/shard_map/ppermute | solution.py:326
  13.0 2.1 %text_kv.1 = (bf16[256,512]{1,0:T(8,128)(2,1)S(1)}, bf16[256,512]{1,0:T(8,128)(2,1)S(1)}, f32[256,512]{1,0:T(8,128)S(1)}, f32[8,256]{1,0:T(8,128)S(1)}) custom-call(bf16[256,2048]{1,0:T(8,128)(2,1)S(1)} %get-tuple-element.44.refs_0_, bf16[2048,2048]{1,0:T(8,128)(2,1)S(1)} %bitcast.5, bf16[256,2048]{1,0:T(8,128)(2,1)S(1)} %copy-done, ...), custom_call_target="tpu_custom_call" | custom-call | flops 1024 | bytes 1024 | tf_op jit(solution)/shard_map/text_kv/pallas_call | solution.py:309
  15.1 1.6 %collective-permute-start.9 = (bf16[256,512]{1,0:T(8,128)(2,1)S(1)}, bf16[256,512]{1,0:T(8,128)(2,1)S(1)}, u32[]{:S(2)}, u32[]{:S(2)}) collective-permute-start(bf16[256,512]{1,0:T(8,128)(2,1)S(1)} %get-tuple-element.59), channel_id=1, source_target_pairs={{0,1},{1,0},{2,3},{3,2},{4,5},{5,4},{6,7},{7,6},{8,9},{9,8},{10,11... | collective-permute-start | bytes 786440 | tf_op jit(solution)/shard_map/ppermute | solution.py:326
  16.7 0.0 collective-permute-done.1.refs_4_
  16.7 0.2 collective-permute-start.10
  17.0 0.0 collective-permute-done.2.refs_5_
  17.0 0.6 %collective-permute-done.3.refs_6_ = bf16[16,1792]{1,0:T(8,128)(2,1)S(1)} collective-permute-done((bf16[16,1792]{1,0:T(8,128)(2,1)S(1)}, bf16[16,1792]{1,0:T(8,128)(2,1)S(1)}, u32[]{:S(2)}, u32[]{:S(2)}) %collective-permute-start.3) | collective-permute-done | bytes 57376 | tf_op jit(solution)/shard_map/ppermute | solution.py:326
  17.6 0.0 slice-done.4
  17.6 2.2 %merge_rows.1 = (f32[32,2048]{1,0:T(8,128)S(1)}, bf16[32,2048]{1,0:T(8,128)(2,1)S(1)}, bf16[32,2048]{1,0:T(8,128)(2,1)S(1)}) custom-call(bf16[16,1792]{1,0:T(8,128)(2,1)S(1)} %get-tuple-element.34.refs_0_, bf16[16,1792]{1,0:T(8,128)(2,1)S(1)} %get-tuple-element.35.refs_1_, bf16[16,1792]{1,0:T(8,128)(2,1)S(1)} %get-tuple-element.36.refs_2_, ...), custom_call_target="tpu_custom_call" | custom-call | flops 1024 | bytes 1024 | tf_op jit(solution)/shard_map/merge_rows/pallas_call | solution.py:309
  19.8 0.1 collective-permute-start.4
  19.9 1.3 %collective-permute-done.4.refs_1_ = bf16[32,2048]{1,0:T(8,128)(2,1)S(1)} collective-permute-done((bf16[32,2048]{1,0:T(8,128)(2,1)S(1)}, bf16[32,2048]{1,0:T(8,128)(2,1)S(1)}, u32[]{:S(2)}, u32[]{:S(2)}) %collective-permute-start.4) | collective-permute-done | bytes 131104 | tf_op jit(solution)/shard_map/ppermute | solution.py:326
  21.2 0.0 collective-permute-done.5.refs_8_
  21.2 1.8 %slot_kv.1 = (bf16[32,2048]{1,0:T(8,128)(2,1)S(1)}, f32[256,512]{1,0:T(8,128)S(1)}, bf16[16,640]{1,0:T(8,128)(2,1)S(1)}, bf16[16,640]{1,0:T(8,128)(2,1)S(1)}, bf...) custom-call(f32[32,2048]{1,0:T(8,128)S(1)} %get-tuple-element.40.refs_0_, ...), custom_call_target="tpu_custom_call" | custom-call | flops 1024 | bytes 1024 | tf_op jit(solution)/shard_map/slot_kv/pallas_call | solution.py:309
  23.0 1.6 %collective-permute-start.6 = (bf16[16,640]{1,0:T(8,128)(2,1)S(1)}, bf16[16,640]{1,0:T(8,128)(2,1)S(1)}, u32[]{:S(2)}, u32[]{:S(2)}) collective-permute-start(bf16[16,640]{1,0:T(8,128)(2,1)S(1)} %get-tuple-element.55), channel_id=1, source_target_pairs={{0,1},{1,0},{2,3},{3,2},{4,5},{5,4},{6,7},{7,6},{8,9},{9,8},{10,11... | collective-permute-start | bytes 61448 | tf_op jit(solution)/shard_map/ppermute | solution.py:326
  24.5 2.0 %collective-permute-start.7 = (bf16[16,640]{1,0:T(8,128)(2,1)S(1)}, bf16[16,640]{1,0:T(8,128)(2,1)S(1)}, u32[]{:S(2)}, u32[]{:S(2)}) collective-permute-start(bf16[16,640]{1,0:T(8,128)(2,1)S(1)} %get-tuple-element.56), channel_id=1, source_target_pairs={{0,2},{1,3},{2,0},{3,1},{4,6},{5,7},{6,4},{7,5},{8,10},{9,11},{10,... | collective-permute-start | bytes 61448 | tf_op jit(solution)/shard_map/ppermute | solution.py:326
  26.6 0.8 %collective-permute-start.8 = (bf16[16,640]{1,0:T(8,128)(2,1)S(1)}, bf16[16,640]{1,0:T(8,128)(2,1)S(1)}, u32[]{:S(2)}, u32[]{:S(2)}) collective-permute-start(bf16[16,640]{1,0:T(8,128)(2,1)S(1)} %get-tuple-element.57), channel_id=1, source_target_pairs={{0,3},{1,2},{2,1},{3,0},{4,7},{5,6},{6,5},{7,4},{8,11},{9,10},{10,... | collective-permute-start | bytes 61448 | tf_op jit(solution)/shard_map/ppermute | solution.py:326
  27.4 2.9 %normed_grad.1 = (f32[272,2048]{1,0:T(8,128)S(1)}, bf16[256,2048]{1,0:T(8,128)(2,1)S(1)}) custom-call(bf16[256,2048]{1,0:T(8,128)(2,1)S(1)} %copy-done, bf16[32,2048]{1,0:T(8,128)(2,1)S(1)} %get-tuple-element.43.refs_5_.grad_rows, bf16[2048,2048]{1,0:T(8,128)(2,1)S(1)} %bitcast.5, f32[1,2048]{1,0:T(1,128)S(1)} %bitcast.10, ...), custom_call_target="tpu_custom_call" | custom-call | flops 1000000000 | bytes 1024 | tf_op jit(solution)/shard_map/normed_grad/pallas_call | solution.py:309
  30.2 1.5 %collective-permute-done.9.refs_10_ = bf16[256,512]{1,0:T(8,128)(2,1)S(1)} collective-permute-done((bf16[256,512]{1,0:T(8,128)(2,1)S(1)}, bf16[256,512]{1,0:T(8,128)(2,1)S(1)}, u32[]{:S(2)}, u32[]{:S(2)}) %collective-permute-start.9) | collective-permute-done | bytes 262176 | tf_op jit(solution)/shard_map/ppermute | solution.py:326
  31.7 0.0 collective-permute-done.10.refs_11_
  31.7 0.4 %collective-permute-done.6.refs_6_ = bf16[16,640]{1,0:T(8,128)(2,1)S(1)} collective-permute-done((bf16[16,640]{1,0:T(8,128)(2,1)S(1)}, bf16[16,640]{1,0:T(8,128)(2,1)S(1)}, u32[]{:S(2)}, u32[]{:S(2)}) %collective-permute-start.6) | collective-permute-done | bytes 20512 | tf_op jit(solution)/shard_map/ppermute | solution.py:326
  32.1 0.7 %collective-permute-done.7.refs_7_ = bf16[16,640]{1,0:T(8,128)(2,1)S(1)} collective-permute-done((bf16[16,640]{1,0:T(8,128)(2,1)S(1)}, bf16[16,640]{1,0:T(8,128)(2,1)S(1)}, u32[]{:S(2)}, u32[]{:S(2)}) %collective-permute-start.7) | collective-permute-done | bytes 20512 | tf_op jit(solution)/shard_map/ppermute | solution.py:326
  32.8 0.0 collective-permute-done.8.refs_8_
  32.8 2.3 %outputs.1 = (bf16[256,512]{1,0:T(8,128)(2,1)}, bf16[256,2048]{1,0:T(8,128)(2,1)}, bf16[256,2048]{1,0:T(8,128)(2,1)}) custom-call(bf16[32,2048]{1,0:T(8,128)(2,1)S(1)} %get-tuple-element.49.rows.refs_0_, f32[272,2048]{1,0:T(8,128)S(1)} %get-tuple-element.51.refs_1_, bf16[256,2048]{1,0:T(8,128)(2,1)S(1)} %get-tuple-element.52.refs_2_, ...), custom_call_target="tpu_custom_call" | custom-call | flops 1024 | bytes 1024 | tf_op jit(solution)/shard_map/outputs/pallas_call | solution.py:309
  (17 shorter events, 0.0 us)
Async XLA Ops:
  0.6 6.8 %copy-start = (bf16[256,2048]{1,0:T(8,128)(2,1)S(1)}, bf16[256,2048]{1,0:T(8,128)(2,1)}, u32[]{:S(2)}) copy-start(bf16[256,2048]{1,0:T(8,128)(2,1)} %grad.1) | copy-start | bytes 3145732
  0.6 6.8 %copy-start.3 = (bf16[512,2560]{1,0:T(8,128)(2,1)S(1)}, bf16[512,2560]{1,0:T(8,128)(2,1)}, u32[]{:S(2)}) copy-start(bf16[512,2560]{1,0:T(8,128)(2,1)} %refs_4_.1) | copy-start | bytes 7864324
  0.7 3.2 %collective-permute-start = (s32[1,256]{1,0:T(1,128)}, s32[1,256]{1,0:T(1,128)S(1)}, u32[]{:S(2)}, u32[]{:S(2)}) collective-permute-start(s32[1,256]{1,0:T(1,128)} %bitcast.13), channel_id=1, source_target_pairs={{0,4},{4,0},{1,5},{5,1},{2,6},{6,2},{3,7},{7,3},{8,12},{12,8},{9,1... | collective-permute-start | bytes 3080 | tf_op jit(solution)/shard_map/ppermute | solution.py:326
  1.2 11.8 %slice-start = ((s8[8388608]{0:T(1024)(128)(4,1)}), s8[4194304]{0:T(1024)(128)(4,1)S(1)}, s32[]{:S(2)}) async-start(s8[8388608]{0:T(1024)(128)(4,1)} %bitcast.4), calls=%async_computation | async-start | bytes 8388608
  3.8 17.4 %collective-permute-start.5 = (bf16[256,512]{1,0:T(8,128)(2,1)S(1)}, bf16[256,512]{1,0:T(8,128)(2,1)S(1)}, u32[]{:S(2)}, u32[]{:S(2)}) collective-permute-start(bf16[256,512]{1,0:T(8,128)(2,1)S(1)} %get-tuple-element.46.refs_4_), channel_id=1, source_target_pairs={{0,2},{1,3},{2,0},{3,1},{4,6},{5,7},{6,4},{7,5},{8,10},{9,11},{10,... | collective-permute-start | bytes 786440 | tf_op jit(solution)/shard_map/ppermute | solution.py:326
  7.4 5.6 %slice-start.1 = ((s8[8388608]{0:T(1024)(128)(4,1)}), s8[4194304]{0:T(1024)(128)(4,1)S(1)}, s32[]{:S(2)}) async-start(s8[8388608]{0:T(1024)(128)(4,1)} %bitcast.4), calls=%async_computation.1 | async-start | bytes 8388608
  7.4 10.2 %slice-start.2 = ((s8[10485760]{0:T(1024)(128)(4,1)}), s8[4194304]{0:T(1024)(128)(4,1)S(1)}, s32[]{:S(2)}) async-start(s8[10485760]{0:T(1024)(128)(4,1)} %bitcast.6), calls=%async_computation.2 | async-start | bytes 8388608
  7.4 10.2 %slice-start.3 = ((s8[10485760]{0:T(1024)(128)(4,1)}), s8[4194304]{0:T(1024)(128)(4,1)S(1)}, s32[]{:S(2)}) async-start(s8[10485760]{0:T(1024)(128)(4,1)} %bitcast.6), calls=%async_computation.3 | async-start | bytes 8388608
  9.4 7.4 %collective-permute-start.1 = (bf16[16,1792]{1,0:T(8,128)(2,1)S(1)}, bf16[16,1792]{1,0:T(8,128)(2,1)S(1)}, u32[]{:S(2)}, u32[]{:S(2)}) collective-permute-start(bf16[16,1792]{1,0:T(8,128)(2,1)S(1)} %get-tuple-element.35.refs_1_), channel_id=1, source_target_pairs={{0,8},{8,0},{16,24},{24,16},{1,9},{9,1},{17,25},{25,17},{2,10},{10... | collective-permute-start | bytes 172040 | tf_op jit(solution)/shard_map/ppermute | solution.py:326
  11.0 6.0 %collective-permute-start.2 = (bf16[16,1792]{1,0:T(8,128)(2,1)S(1)}, bf16[16,1792]{1,0:T(8,128)(2,1)S(1)}, u32[]{:S(2)}, u32[]{:S(2)}) collective-permute-start(bf16[16,1792]{1,0:T(8,128)(2,1)S(1)} %get-tuple-element.36.refs_2_), channel_id=1, source_target_pairs={{0,16},{8,24},{16,0},{24,8},{1,17},{9,25},{17,1},{25,9},{2,18},{10... | collective-permute-start | bytes 172040 | tf_op jit(solution)/shard_map/ppermute | solution.py:326
  12.5 5.1 %collective-permute-start.3 = (bf16[16,1792]{1,0:T(8,128)(2,1)S(1)}, bf16[16,1792]{1,0:T(8,128)(2,1)S(1)}, u32[]{:S(2)}, u32[]{:S(2)}) collective-permute-start(bf16[16,1792]{1,0:T(8,128)(2,1)S(1)} %get-tuple-element.37.refs_3_), channel_id=1, source_target_pairs={{0,24},{8,16},{16,8},{24,0},{1,25},{9,17},{17,9},{25,1},{2,26},{10... | collective-permute-start | bytes 172040 | tf_op jit(solution)/shard_map/ppermute | solution.py:326
  13.0 4.6 %slice-start.4 = ((s8[10485760]{0:T(1024)(128)(4,1)}), s8[2097152]{0:T(1024)(128)(4,1)S(1)}, s32[]{:S(2)}) async-start(s8[10485760]{0:T(1024)(128)(4,1)} %bitcast.6), calls=%async_computation.4 | async-start | bytes 4194304
  15.1 6.1 %copy-start.1 = (f32[2048]{0:T(1024)S(1)}, f32[2048]{0:T(1024)}, u32[]{:S(2)}) copy-start(f32[2048]{0:T(1024)} %param.15) | copy-start | bytes 24580
  15.1 6.1 %copy-start.2 = (f32[2048]{0:T(1024)S(1)}, f32[2048]{0:T(1024)}, u32[]{:S(2)}) copy-start(f32[2048]{0:T(1024)} %param.11) | copy-start | bytes 24580
  15.1 16.6 %collective-permute-start.9 = (bf16[256,512]{1,0:T(8,128)(2,1)S(1)}, bf16[256,512]{1,0:T(8,128)(2,1)S(1)}, u32[]{:S(2)}, u32[]{:S(2)}) collective-permute-start(bf16[256,512]{1,0:T(8,128)(2,1)S(1)} %get-tuple-element.59), channel_id=1, source_target_pairs={{0,1},{1,0},{2,3},{3,2},{4,5},{5,4},{6,7},{7,6},{8,9},{9,8},{10,11... | collective-permute-start | bytes 786440 | tf_op jit(solution)/shard_map/ppermute | solution.py:326
  16.7 15.0 %collective-permute-start.10 = (bf16[256,512]{1,0:T(8,128)(2,1)S(1)}, bf16[256,512]{1,0:T(8,128)(2,1)S(1)}, u32[]{:S(2)}, u32[]{:S(2)}) collective-permute-start(bf16[256,512]{1,0:T(8,128)(2,1)S(1)} %get-tuple-element.60), channel_id=1, source_target_pairs={{0,3},{1,2},{2,1},{3,0},{4,7},{5,6},{6,5},{7,4},{8,11},{9,10},{10,... | collective-permute-start | bytes 786440 | tf_op jit(solution)/shard_map/ppermute | solution.py:326
  19.8 1.4 %collective-permute-start.4 = (bf16[32,2048]{1,0:T(8,128)(2,1)S(1)}, bf16[32,2048]{1,0:T(8,128)(2,1)S(1)}, u32[]{:S(2)}, u32[]{:S(2)}) collective-permute-start(bf16[32,2048]{1,0:T(8,128)(2,1)S(1)} %get-tuple-element.41), channel_id=1, source_target_pairs={{0,4},{4,0},{1,5},{5,1},{2,6},{6,2},{3,7},{7,3},{8,12},{12,8},{9,1... | collective-permute-start | bytes 393224 | tf_op jit(solution)/shard_map/ppermute | solution.py:326
  23.0 9.1 %collective-permute-start.6 = (bf16[16,640]{1,0:T(8,128)(2,1)S(1)}, bf16[16,640]{1,0:T(8,128)(2,1)S(1)}, u32[]{:S(2)}, u32[]{:S(2)}) collective-permute-start(bf16[16,640]{1,0:T(8,128)(2,1)S(1)} %get-tuple-element.55), channel_id=1, source_target_pairs={{0,1},{1,0},{2,3},{3,2},{4,5},{5,4},{6,7},{7,6},{8,9},{9,8},{10,11... | collective-permute-start | bytes 61448 | tf_op jit(solution)/shard_map/ppermute | solution.py:326
  24.5 8.2 %collective-permute-start.7 = (bf16[16,640]{1,0:T(8,128)(2,1)S(1)}, bf16[16,640]{1,0:T(8,128)(2,1)S(1)}, u32[]{:S(2)}, u32[]{:S(2)}) collective-permute-start(bf16[16,640]{1,0:T(8,128)(2,1)S(1)} %get-tuple-element.56), channel_id=1, source_target_pairs={{0,2},{1,3},{2,0},{3,1},{4,6},{5,7},{6,4},{7,5},{8,10},{9,11},{10,... | collective-permute-start | bytes 61448 | tf_op jit(solution)/shard_map/ppermute | solution.py:326
  26.6 6.2 %collective-permute-start.8 = (bf16[16,640]{1,0:T(8,128)(2,1)S(1)}, bf16[16,640]{1,0:T(8,128)(2,1)S(1)}, u32[]{:S(2)}, u32[]{:S(2)}) collective-permute-start(bf16[16,640]{1,0:T(8,128)(2,1)S(1)} %get-tuple-element.57), channel_id=1, source_target_pairs={{0,3},{1,2},{2,1},{3,0},{4,7},{5,6},{6,5},{7,4},{8,11},{9,10},{10,... | collective-permute-start | bytes 61448 | tf_op jit(solution)/shard_map/ppermute | solution.py:326

commit v4 on v3

--- a/solution.py
+++ b/solution.py
@@ -40,6 +40,11 @@
     return pl.ds(pl.multiple_of((lax.axis_index(axis) ^ k) * cols, cols), cols)
 
 
+def in_middle(dims):
+    place = jnp.full(dims, lax.axis_index("tp"), jnp.int32)
+    return (place == 1) | (place == 2)
+
+
 def picker(slots, rows, group, cap, first):
     row = iota((slots, rows), 1)
     place = (row & (group - 1)) - first
@@ -51,11 +56,9 @@
     return match.astype(F32).astype(BF16)
 
 
-def first_text_kernel(step, text_hbm, gain_hbm, weight_hbm, part, scaled, text, gain, weight, sem):
+def first_text_kernel(step, text_hbm, gain_hbm, weight_hbm, dest_hbm, pos_hbm, part, scaled, text, dest, pos, gain, weight, sem):
     span = peer_columns("tp", step, part.shape[1])
-    gain_copy = pltpu.make_async_copy(gain_hbm, gain, sem.at[0])
-    gain_copy.start()
-    count = 4 if text.shape[1] % 512 == 0 else 1
+    count = CHUNKS if text.shape[1] % 512 == 0 else 1
     size = text.shape[1] // count
     cuts = [slice(i * size, (i + 1) * size) for i in range(count)]
     copies = []
@@ -67,6 +70,12 @@
         for copy in pair:
             copy.start()
         copies.append(pair)
+        if i == 0:
+            gain_copy = pltpu.make_async_copy(gain_hbm, gain, sem.at[0])
+            gain_copy.start()
+    small = [pltpu.make_async_copy(*pair, sem.at[2 * count + 1 + i]) for i, pair in enumerate([(dest_hbm, dest), (pos_hbm, pos)])]
+    for copy in small:
+        copy.start()
     gain_copy.wait()
     total = jnp.zeros(part.shape, F32)
     for cut, pair in zip(cuts, copies):
@@ -75,6 +84,8 @@
         pair[1].wait()
         total = total + dot(scaled[:, cut], weight[cut])
     part[...] = total.astype(BF16)
+    for copy in small:
+        copy.wait()
 
 
 def text_kernel(first_step, steps, scaled, weight, grad, text, first_part, *refs):
@@ -96,14 +107,13 @@
     sums[...] = jnp.where(lane == 0, squares, jnp.where(lane == 1, dots, 0.0)).T[:8]
 
 
-def gather_kernel(lane_count, group, cap, other_ref, own_hbm, pos_hbm, grad, hidden, *refs):
-    payloads, (send_table, place_table, own_ref, pos_ref, sem) = refs[:lane_count], refs[lane_count:]
-    pairs = [(own_hbm, own_ref), (pos_hbm, pos_ref)]
-    copies = [pltpu.make_async_copy(source, target, sem.at[i]) for i, (source, target) in enumerate(pairs)]
-    for copy in copies:
-        copy.start()
-    copies[0].wait()
-    copies[1].wait()
+def forward_kernel(turned, part, onward):
+    added = jnp.where(in_middle(part.shape), turned[...].astype(F32), 0.0)
+    onward[...] = (part[...].astype(F32) + added).astype(BF16)
+
+
+def gather_kernel(lane_count, group, cap, other_ref, own_ref, pos_ref, grad, hidden, *refs):
+    payloads, (send_table, place_table) = refs[:lane_count], refs[lane_count:]
     rows = lane_count * group
     slots = lane_count * cap
     block, tokens = own_ref.shape[1], grad.shape[0]
@@ -185,9 +195,12 @@
 
 
 def slot_kernel(
-    tp_count, own, other, bias, gain, weight, grad_rows, text_sums, text_part, first_part, rows, text_total, *messages
+    tp_count, own, other, bias, gain, weight, grad_rows, text_sums, text_part, first_arrived, rows, text_total, *messages
 ):
-    text_total[...] = text_part[...] + first_part[...].astype(F32)
+    arrived = first_arrived[...].astype(F32)
+    if tp_count == 4:
+        arrived = jnp.where(in_middle(arrived.shape), arrived, 0.0)
+    text_total[...] = text_part[...] + arrived
     slots2 = own.shape[0]
     slots = slots2 // 2
     placed = (own[...] + other[...].astype(F32) + bias[...]).astype(BF16)
@@ -268,7 +281,7 @@
         copy.start()
         copies.append(copy)
 
-    step = stream.shape[1] // 2
+    step = max(128, stream.shape[1] // PIECES)
     for c in range(0, stream.shape[1], step):
         cut = slice(c, c + step)
         embed_buffer[:, cut] = (inv_col * scaled_grad[:tokens, cut] - stream[:, cut].astype(F32) * slope_col).astype(BF16)
@@ -295,9 +308,12 @@
 
 
 COST = cost_of(1024)
+CHUNKS = 4
+PIECES = 2
 MERGE_COST = cost_of(1024)
 GRAD_COST = cost_of(1000000000)
 TEXT_COST = cost_of(1024)
+SLOT_COST = cost_of(1024)
 GATHER_COST = cost_of(4000000000)
 
 
@@ -344,49 +360,57 @@
     own_dest = row_dest.reshape(1, block)
     positions = image_pos.reshape(lane_count, cap)
 
-    other_dest = swap(own_dest, "section", 1)
-    half = tp_count // 2
-    first_part, scaled, text = call(
-        lambda *refs: first_text_kernel(half, *refs),
+    first = 3 if tp_count == 4 else tp_count // 2
+    first_part, scaled, text, own_dest, positions = call(
+        lambda *refs: first_text_kernel(first, *refs),
         "first_text_kv",
-        [in_hbm(array) for array in (text_embed, gain, kv_weight)],
-        [ANY] * 3,
-        [shape((tokens, cols), BF16), shape((tokens, features), BF16), pltpu.VMEM(text_embed.shape, BF16)],
+        [in_hbm(array) for array in (text_embed, gain, kv_weight, own_dest, positions)],
+        [ANY] * 5,
+        [shape((tokens, cols), BF16), shape((tokens, features), BF16)]
+        + [pltpu.VMEM(array.shape, array.dtype) for array in (text_embed, own_dest, positions)],
         scratch=[
             pltpu.VMEM((1, features), F32),
             pltpu.VMEM((features, cols), BF16),
-            pltpu.SemaphoreType.DMA((9,)),
+            pltpu.SemaphoreType.DMA((2 * CHUNKS + 3,)),
         ],
     )
-    first_part, other_dest = lax.optimization_barrier((first_part, other_dest))
-    first_arrived = swap(first_part, "tp", half)
-
+    if tp_count == 4:
+        turned = swap(first_part, "tp", 1)
+        sections = lax.axis_size("section")
+        pairs = [
+            (section * 4 + z, section * 4 + 3 - z if z in (1, 2) else (section + 1) % sections * 4 + z)
+            for section in range(sections)
+            for z in range(4)
+        ]
+        first_arrived = lax.ppermute(first_part, ("section", "tp"), pairs)
+    else:
+        first_arrived = swap(first_part, "tp", first)
+
+    other_dest = swap(own_dest, "section", 1)
     *sent, send_table, place_table = call(
         lambda *refs: gather_kernel(lane_count, group, cap, *refs),
         "gather_rows",
-        [other_dest, in_hbm(own_dest), in_hbm(positions), kv_grad, merge_hidden],
-        [VMEM, ANY, ANY, VMEM, VMEM],
+        [other_dest, own_dest, positions, kv_grad, merge_hidden],
+        [VMEM] * 5,
         [shape((group, width), BF16)] * lane_count
         + [shape((slots, block), BF16), shape((slots, tokens), BF16)],
-        scratch=[
-            pltpu.VMEM(own_dest.shape, jnp.int32),
-            pltpu.VMEM(positions.shape, jnp.int32),
-            pltpu.SemaphoreType.DMA((2,)),
-        ],
         cost=GATHER_COST,
     )
     send_table, kv_weight, merge_weight = lax.optimization_barrier((send_table, kv_weight, merge_weight))
     got = [swap(sent[k], "lane", k) for k in range(1, lane_count)]
 
-    steps = [k for k in range(1, tp_count) if k != half] + [0]
+    steps = [k for k in range(tp_count - 1, 0, -1) if k != first] + [0]
     *parts, text_own, text_sums = call(
-        lambda *refs: text_kernel(half, steps, *refs),
+        lambda *refs: text_kernel(first, steps, *refs),
         "text_kv",
         [scaled, kv_weight, kv_grad, text, first_part],
         [VMEM] * 5,
         [shape((tokens, cols), BF16)] * (tp_count - 2) + [shape((tokens, cols), F32), shape((8, tokens), F32)],
         cost=TEXT_COST,
     )
+    if tp_count == 4:
+        (parts[0],) = call(forward_kernel, "forward", [turned, parts[0]], [VMEM] * 2, [shape((tokens, cols), BF16)])
+        parts = list(lax.optimization_barrier(tuple(parts)))
     arrived = [swap(part, "tp", k) for part, k in zip(parts, steps)]
 
     own, other, grad_rows = call(
@@ -406,6 +430,7 @@
         [VMEM] * 9,
         [shape((slots2, features), BF16), shape((tokens, cols), F32)]
         + [shape((slots, cols + 128), BF16)] * tp_count,
+        cost=SLOT_COST,
     )
     messages = [messages[0]] + [swap(messages[k], "tp", k) for k in range(1, tp_count)]
 
@@ -429,7 +454,7 @@
             pltpu.VMEM((tokens, cols), BF16),
             pltpu.VMEM((tokens, features), BF16),
             pltpu.VMEM((block, features), BF16),
-            pltpu.SemaphoreType.DMA((5,)),
+            pltpu.SemaphoreType.DMA((2 * PIECES + 1,)),
         ],
     )
     return (key_value, embed_grad, image_grad)

time: 35.2 us -> 33.5 us (0.952)
  waiting for transfers between devices: 4.43 us -> 1.89 us
  starting transfers between devices: 14 us -> 15.7 us
  Pallas kernels: 15.8 us -> 15 us
    ppermute x11, waiting for transfers between devices: 4.43 us -> 1.89 us  [swap(): lax.ppermute(array, axis, [(i, i ^ k) for i in range(lax.axis_size(axis))])]
    ppermute x11, starting transfers between devices: 14 us -> 15.5 us  [swap(): lax.ppermute(array, axis, [(i, i ^ k) for i in range(lax.axis_size(axis))])]
    pallas_call x7 -> x8, Pallas kernels: 15.8 us -> 15 us  [call(): pl.pallas_call(kernel, out_shape=outs, in_specs=in_specs, out_specs=out_s...]
  transfers between devices with their start and end apart: 11 -> 12, of which waited for: 5 -> 2; matrix products, arithmetic and copies ran while one was open for 0% -> 0% of each run, Pallas kernels for 39% -> 30%
where the time goes in v4:
time: 33.5 us; the launch traced here: 33.4 us
  starting transfers between devices  15.7 us (47%)
  Pallas kernels  15 us (45%)
  waiting for transfers between devices  1.89 us (6%)
  between operations  0.79 us (2%)
    ppermute x11, starting transfers between devices, swap(): lax.ppermute(array, axis, [(i, i ^ k) for i in range(lax.axis_size(axis))])  15.5 us
    pallas_call x8, Pallas kernels, call(): pl.pallas_call(kernel, out_shape=outs, in_specs=in_specs, out_specs=out_s...  15 us
    ppermute x11, waiting for transfers between devices, swap(): lax.ppermute(array, axis, [(i, i ^ k) for i in range(lax.axis_size(axis))])  1.89 us
  transfers between devices with their start and end apart: 12, of which 2 were waited for; matrix products, arithmetic and copies ran while one was open for 0% of the time, Pallas kernels for 30%

profile of v4, /device:TPU:0, one launch (start us, length us, event | category | flops | bytes accessed | tf_op | source)
XLA Modules:
  0.0 33.4 jit_solution(15526331662763135643)
XLA Ops:
  0.7 0.0 slice-start
  0.7 2.5 %first_text_kv.1 = (bf16[256,512]{1,0:T(8,128)(2,1)S(1)}, bf16[256,2048]{1,0:T(8,128)(2,1)S(1)}, bf16[256,2048]{1,0:T(8,128)(2,1)S(1)}, s32[1,256]{1,0:T(1,128)S(1)}, s32[4,4]{1,0:T(4,128)S(1)}) custom-call(bf16[256,2048]{1,0:T(8,128)(2,1)} %refs_0_.1, f32[1,2048]{1,0:T(1,128)} %bitcast.8, bf16[2048,2048]{1,0:T(8,128)(2,1)} %weight, s32[1,256]{1,0:T(1,128)} %bitcast.13, ...), custom_call_target="tpu_custom_call" | custom-call | flops 1024 | bytes 1024 | tf_op jit(solution)/shard_map/first_text_kv/pallas_call | solution.py:325
  3.2 0.5 %collective-permute-start = (s32[1,256]{1,0:T(1,128)S(1)}, s32[1,256]{1,0:T(1,128)S(1)}, u32[]{:S(2)}, u32[]{:S(2)}) collective-permute-start(s32[1,256]{1,0:T(1,128)S(1)} %get-tuple-element.34.refs_1_), channel_id=1, source_target_pairs={{0,4},{4,0},{1,5},{5,1},{2,6},{6,2},{3,7},{7,3},{8,12},{12,8},{9,1... | collective-permute-start | bytes 3080 | tf_op jit(solution)/shard_map/ppermute | solution.py:342
  3.7 2.6 %collective-permute-start.9 = (bf16[256,512]{1,0:T(8,128)(2,1)S(1)}, bf16[256,512]{1,0:T(8,128)(2,1)S(1)}, u32[]{:S(2)}, u32[]{:S(2)}) collective-permute-start(bf16[256,512]{1,0:T(8,128)(2,1)S(1)} %get-tuple-element.48.refs_4_), channel_id=1, source_target_pairs={{0,1},{1,0},{2,3},{3,2},{4,5},{5,4},{6,7},{7,6},{8,9},{9,8},{10,11... | collective-permute-start | bytes 786440 | tf_op jit(solution)/shard_map/ppermute | solution.py:342
  6.4 0.2 collective-permute-start.5
  6.5 0.0 collective-permute-done.refs_0_
  6.6 0.0 slice-start.1
  6.6 0.0 slice-start.2
  6.6 0.0 slice-start.3
  6.6 1.1 %gather_rows.1 = (bf16[16,1792]{1,0:T(8,128)(2,1)S(1)}, bf16[16,1792]{1,0:T(8,128)(2,1)S(1)}, bf16[16,1792]{1,0:T(8,128)(2,1)S(1)}, bf16[16,1792]{1,0:T(8,128)(2...) custom-call(s32[1,256]{1,0:T(1,128)S(1)} %collective-permute-done.refs_0_, ...), custom_call_target="tpu_custom_call" | custom-call | flops 4000000000 | bytes 1024 | tf_op jit(solution)/shard_map/gather_rows/pallas_call | solution.py:325
  7.7 1.6 %collective-permute-start.1 = (bf16[16,1792]{1,0:T(8,128)(2,1)S(1)}, bf16[16,1792]{1,0:T(8,128)(2,1)S(1)}, u32[]{:S(2)}, u32[]{:S(2)}) collective-permute-start(bf16[16,1792]{1,0:T(8,128)(2,1)S(1)} %get-tuple-element.37.refs_1_), channel_id=1, source_target_pairs={{0,8},{8,0},{16,24},{24,16},{1,9},{9,1},{17,25},{25,17},{2,10},{10... | collective-permute-start | bytes 172040 | tf_op jit(solution)/shard_map/ppermute | solution.py:342
  9.2 1.5 %collective-permute-start.2 = (bf16[16,1792]{1,0:T(8,128)(2,1)S(1)}, bf16[16,1792]{1,0:T(8,128)(2,1)S(1)}, u32[]{:S(2)}, u32[]{:S(2)}) collective-permute-start(bf16[16,1792]{1,0:T(8,128)(2,1)S(1)} %get-tuple-element.38.refs_2_), channel_id=1, source_target_pairs={{0,16},{8,24},{16,0},{24,8},{1,17},{9,25},{17,1},{25,9},{2,18},{10... | collective-permute-start | bytes 172040 | tf_op jit(solution)/shard_map/ppermute | solution.py:342
  10.7 0.5 %collective-permute-start.3 = (bf16[16,1792]{1,0:T(8,128)(2,1)S(1)}, bf16[16,1792]{1,0:T(8,128)(2,1)S(1)}, u32[]{:S(2)}, u32[]{:S(2)}) collective-permute-start(bf16[16,1792]{1,0:T(8,128)(2,1)S(1)} %get-tuple-element.39.refs_3_), channel_id=1, source_target_pairs={{0,24},{8,16},{16,8},{24,0},{1,25},{9,17},{17,9},{25,1},{2,26},{10... | collective-permute-start | bytes 172040 | tf_op jit(solution)/shard_map/ppermute | solution.py:342
  11.2 2.1 %text_kv.1 = (bf16[256,512]{1,0:T(8,128)(2,1)S(1)}, bf16[256,512]{1,0:T(8,128)(2,1)S(1)}, f32[256,512]{1,0:T(8,128)S(1)}, f32[8,256]{1,0:T(8,128)S(1)}) custom-call(bf16[256,2048]{1,0:T(8,128)(2,1)S(1)} %get-tuple-element.46.refs_0_, bf16[2048,2048]{1,0:T(8,128)(2,1)S(1)} %bitcast.5, bf16[256,2048]{1,0:T(8,128)(2,1)S(1)} %copy-done, ...), custom_call_target="tpu_custom_call" | custom-call | flops 1024 | bytes 1024 | tf_op jit(solution)/shard_map/text_kv/pallas_call | solution.py:325
  13.4 0.0 collective-permute-done.9.turned
  13.4 0.1 forward.1
  13.5 2.7 %collective-permute-start.10 = (bf16[256,512]{1,0:T(8,128)(2,1)S(1)}, bf16[256,512]{1,0:T(8,128)(2,1)S(1)}, u32[]{:S(2)}, u32[]{:S(2)}) collective-permute-start(bf16[256,512]{1,0:T(8,128)(2,1)S(1)} %forward.1), channel_id=1, source_target_pairs={{0,2},{1,3},{2,0},{3,1},{4,6},{5,7},{6,4},{7,5},{8,10},{9,11},{10,... | collective-permute-start | bytes 786440 | tf_op jit(solution)/shard_map/ppermute | solution.py:342
  16.2 1.6 %collective-permute-start.11 = (bf16[256,512]{1,0:T(8,128)(2,1)S(1)}, bf16[256,512]{1,0:T(8,128)(2,1)S(1)}, u32[]{:S(2)}, u32[]{:S(2)}) collective-permute-start(bf16[256,512]{1,0:T(8,128)(2,1)S(1)} %get-tuple-element.64), channel_id=1, source_target_pairs={{0,1},{1,0},{2,3},{3,2},{4,5},{5,4},{6,7},{7,6},{8,9},{9,8},{10,11... | collective-permute-start | bytes 786440 | tf_op jit(solution)/shard_map/ppermute | solution.py:342
  17.8 0.0 collective-permute-done.2.refs_5_
  17.8 0.0 collective-permute-done.3.refs_6_
  17.8 2.2 %merge_rows.1 = (f32[32,2048]{1,0:T(8,128)S(1)}, bf16[32,2048]{1,0:T(8,128)(2,1)S(1)}, bf16[32,2048]{1,0:T(8,128)(2,1)S(1)}) custom-call(bf16[16,1792]{1,0:T(8,128)(2,1)S(1)} %get-tuple-element.36.refs_0_, bf16[16,1792]{1,0:T(8,128)(2,1)S(1)} %get-tuple-element.37.refs_1_, bf16[16,1792]{1,0:T(8,128)(2,1)S(1)} %get-tuple-element.38.refs_2_, ...), custom_call_target="tpu_custom_call" | custom-call | flops 1024 | bytes 1024 | tf_op jit(solution)/shard_map/merge_rows/pallas_call | solution.py:325
  20.0 0.1 collective-permute-start.4
  20.1 1.3 %collective-permute-done.4.refs_1_ = bf16[32,2048]{1,0:T(8,128)(2,1)S(1)} collective-permute-done((bf16[32,2048]{1,0:T(8,128)(2,1)S(1)}, bf16[32,2048]{1,0:T(8,128)(2,1)S(1)}, u32[]{:S(2)}, u32[]{:S(2)}) %collective-permute-start.4) | collective-permute-done | bytes 131104 | tf_op jit(solution)/shard_map/ppermute | solution.py:342
  21.4 0.0 collective-permute-done.5.refs_8_
  21.5 1.8 %slot_kv.1 = (bf16[32,2048]{1,0:T(8,128)(2,1)S(1)}, f32[256,512]{1,0:T(8,128)S(1)}, bf16[16,640]{1,0:T(8,128)(2,1)S(1)}, bf16[16,640]{1,0:T(8,128)(2,1)S(1)}, bf...) custom-call(f32[32,2048]{1,0:T(8,128)S(1)} %get-tuple-element.42.refs_0_, ...), custom_call_target="tpu_custom_call" | custom-call | flops 1024 | bytes 1024 | tf_op jit(solution)/shard_map/slot_kv/pallas_call | solution.py:325
  23.3 1.0 %collective-permute-start.6 = (bf16[16,640]{1,0:T(8,128)(2,1)S(1)}, bf16[16,640]{1,0:T(8,128)(2,1)S(1)}, u32[]{:S(2)}, u32[]{:S(2)}) collective-permute-start(bf16[16,640]{1,0:T(8,128)(2,1)S(1)} %get-tuple-element.57), channel_id=1, source_target_pairs={{0,1},{1,0},{2,3},{3,2},{4,5},{5,4},{6,7},{7,6},{8,9},{9,8},{10,11... | collective-permute-start | bytes 61448 | tf_op jit(solution)/shard_map/ppermute | solution.py:342
  24.3 0.7 %collective-permute-start.7 = (bf16[16,640]{1,0:T(8,128)(2,1)S(1)}, bf16[16,640]{1,0:T(8,128)(2,1)S(1)}, u32[]{:S(2)}, u32[]{:S(2)}) collective-permute-start(bf16[16,640]{1,0:T(8,128)(2,1)S(1)} %get-tuple-element.58), channel_id=1, source_target_pairs={{0,2},{1,3},{2,0},{3,1},{4,6},{5,7},{6,4},{7,5},{8,10},{9,11},{10,... | collective-permute-start | bytes 61448 | tf_op jit(solution)/shard_map/ppermute | solution.py:342
  25.0 2.7 %collective-permute-start.8 = (bf16[16,640]{1,0:T(8,128)(2,1)S(1)}, bf16[16,640]{1,0:T(8,128)(2,1)S(1)}, u32[]{:S(2)}, u32[]{:S(2)}) collective-permute-start(bf16[16,640]{1,0:T(8,128)(2,1)S(1)} %get-tuple-element.59), channel_id=1, source_target_pairs={{0,3},{1,2},{2,1},{3,0},{4,7},{5,6},{6,5},{7,4},{8,11},{9,10},{10,... | collective-permute-start | bytes 61448 | tf_op jit(solution)/shard_map/ppermute | solution.py:342
  27.7 2.8 %normed_grad.1 = (f32[272,2048]{1,0:T(8,128)S(1)}, bf16[256,2048]{1,0:T(8,128)(2,1)S(1)}) custom-call(bf16[256,2048]{1,0:T(8,128)(2,1)S(1)} %copy-done, bf16[32,2048]{1,0:T(8,128)(2,1)S(1)} %get-tuple-element.45.refs_5_.grad_rows, bf16[2048,2048]{1,0:T(8,128)(2,1)S(1)} %bitcast.5, f32[1,2048]{1,0:T(1,128)S(1)} %bitcast.10, ...), custom_call_target="tpu_custom_call" | custom-call | flops 1000000000 | bytes 1024 | tf_op jit(solution)/shard_map/normed_grad/pallas_call | solution.py:325
  30.5 0.0 collective-permute-done.7.refs_7_
  30.5 0.5 %collective-permute-done.8.refs_8_ = bf16[16,640]{1,0:T(8,128)(2,1)S(1)} collective-permute-done((bf16[16,640]{1,0:T(8,128)(2,1)S(1)}, bf16[16,640]{1,0:T(8,128)(2,1)S(1)}, u32[]{:S(2)}, u32[]{:S(2)}) %collective-permute-start.8) | collective-permute-done | bytes 20512 | tf_op jit(solution)/shard_map/ppermute | solution.py:342
  31.1 2.3 %outputs.1 = (bf16[256,512]{1,0:T(8,128)(2,1)}, bf16[256,2048]{1,0:T(8,128)(2,1)}, bf16[256,2048]{1,0:T(8,128)(2,1)}) custom-call(bf16[32,2048]{1,0:T(8,128)(2,1)S(1)} %get-tuple-element.51.rows.refs_0_, f32[272,2048]{1,0:T(8,128)S(1)} %get-tuple-element.53.refs_1_, bf16[256,2048]{1,0:T(8,128)(2,1)S(1)} %get-tuple-element.54.refs_2_, ...), custom_call_target="tpu_custom_call" | custom-call | flops 1024 | bytes 1024 | tf_op jit(solution)/shard_map/outputs/pallas_call | solution.py:325
  (20 shorter events, 0.0 us)
Async XLA Ops:
  0.6 5.9 %copy-start = (bf16[256,2048]{1,0:T(8,128)(2,1)S(1)}, bf16[256,2048]{1,0:T(8,128)(2,1)}, u32[]{:S(2)}) copy-start(bf16[256,2048]{1,0:T(8,128)(2,1)} %grad.1) | copy-start | bytes 3145732
  0.6 5.9 %copy-start.3 = (bf16[512,2560]{1,0:T(8,128)(2,1)S(1)}, bf16[512,2560]{1,0:T(8,128)(2,1)}, u32[]{:S(2)}) copy-start(bf16[512,2560]{1,0:T(8,128)(2,1)} %refs_4_.1) | copy-start | bytes 7864324
  0.7 10.6 %slice-start = ((s8[8388608]{0:T(1024)(128)(4,1)}), s8[4194304]{0:T(1024)(128)(4,1)S(1)}, s32[]{:S(2)}) async-start(s8[8388608]{0:T(1024)(128)(4,1)} %bitcast.4), calls=%async_computation | async-start | bytes 8388608
  3.2 3.3 %collective-permute-start = (s32[1,256]{1,0:T(1,128)S(1)}, s32[1,256]{1,0:T(1,128)S(1)}, u32[]{:S(2)}, u32[]{:S(2)}) collective-permute-start(s32[1,256]{1,0:T(1,128)S(1)} %get-tuple-element.34.refs_1_), channel_id=1, source_target_pairs={{0,4},{4,0},{1,5},{5,1},{2,6},{6,2},{3,7},{7,3},{8,12},{12,8},{9,1... | collective-permute-start | bytes 3080 | tf_op jit(solution)/shard_map/ppermute | solution.py:342
  3.7 9.7 %collective-permute-start.9 = (bf16[256,512]{1,0:T(8,128)(2,1)S(1)}, bf16[256,512]{1,0:T(8,128)(2,1)S(1)}, u32[]{:S(2)}, u32[]{:S(2)}) collective-permute-start(bf16[256,512]{1,0:T(8,128)(2,1)S(1)} %get-tuple-element.48.refs_4_), channel_id=1, source_target_pairs={{0,1},{1,0},{2,3},{3,2},{4,5},{5,4},{6,7},{7,6},{8,9},{9,8},{10,11... | collective-permute-start | bytes 786440 | tf_op jit(solution)/shard_map/ppermute | solution.py:342
  6.4 15.1 %collective-permute-start.5 = (bf16[256,512]{1,0:T(8,128)(2,1)S(1)}, bf16[256,512]{1,0:T(8,128)(2,1)S(1)}, u32[]{:S(2)}, u32[]{:S(2)}) collective-permute-start(bf16[256,512]{1,0:T(8,128)(2,1)S(1)} %get-tuple-element.48.refs_4_), channel_id=1, source_target_pairs={{0,4},{1,2},{2,1},{3,7},{4,0},{5,6},{6,5},{7,3},{8,12},{9,10},{10,... | collective-permute-start | bytes 786440 | tf_op jit(solution)/shard_map/ppermute | solution.py:385
  6.6 4.7 %slice-start.1 = ((s8[8388608]{0:T(1024)(128)(4,1)}), s8[4194304]{0:T(1024)(128)(4,1)S(1)}, s32[]{:S(2)}) async-start(s8[8388608]{0:T(1024)(128)(4,1)} %bitcast.4), calls=%async_computation.1 | async-start | bytes 8388608
  6.6 11.2 %slice-start.2 = ((s8[10485760]{0:T(1024)(128)(4,1)}), s8[4194304]{0:T(1024)(128)(4,1)S(1)}, s32[]{:S(2)}) async-start(s8[10485760]{0:T(1024)(128)(4,1)} %bitcast.6), calls=%async_computation.2 | async-start | bytes 8388608
  6.6 11.2 %slice-start.3 = ((s8[10485760]{0:T(1024)(128)(4,1)}), s8[4194304]{0:T(1024)(128)(4,1)S(1)}, s32[]{:S(2)}) async-start(s8[10485760]{0:T(1024)(128)(4,1)} %bitcast.6), calls=%async_computation.3 | async-start | bytes 8388608
  7.7 8.5 %collective-permute-start.1 = (bf16[16,1792]{1,0:T(8,128)(2,1)S(1)}, bf16[16,1792]{1,0:T(8,128)(2,1)S(1)}, u32[]{:S(2)}, u32[]{:S(2)}) collective-permute-start(bf16[16,1792]{1,0:T(8,128)(2,1)S(1)} %get-tuple-element.37.refs_1_), channel_id=1, source_target_pairs={{0,8},{8,0},{16,24},{24,16},{1,9},{9,1},{17,25},{25,17},{2,10},{10... | collective-permute-start | bytes 172040 | tf_op jit(solution)/shard_map/ppermute | solution.py:342
  9.2 8.6 %collective-permute-start.2 = (bf16[16,1792]{1,0:T(8,128)(2,1)S(1)}, bf16[16,1792]{1,0:T(8,128)(2,1)S(1)}, u32[]{:S(2)}, u32[]{:S(2)}) collective-permute-start(bf16[16,1792]{1,0:T(8,128)(2,1)S(1)} %get-tuple-element.38.refs_2_), channel_id=1, source_target_pairs={{0,16},{8,24},{16,0},{24,8},{1,17},{9,25},{17,1},{25,9},{2,18},{10... | collective-permute-start | bytes 172040 | tf_op jit(solution)/shard_map/ppermute | solution.py:342
  10.7 7.0 %collective-permute-start.3 = (bf16[16,1792]{1,0:T(8,128)(2,1)S(1)}, bf16[16,1792]{1,0:T(8,128)(2,1)S(1)}, u32[]{:S(2)}, u32[]{:S(2)}) collective-permute-start(bf16[16,1792]{1,0:T(8,128)(2,1)S(1)} %get-tuple-element.39.refs_3_), channel_id=1, source_target_pairs={{0,24},{8,16},{16,8},{24,0},{1,25},{9,17},{17,9},{25,1},{2,26},{10... | collective-permute-start | bytes 172040 | tf_op jit(solution)/shard_map/ppermute | solution.py:342
  11.2 6.6 %slice-start.4 = ((s8[10485760]{0:T(1024)(128)(4,1)}), s8[2097152]{0:T(1024)(128)(4,1)S(1)}, s32[]{:S(2)}) async-start(s8[10485760]{0:T(1024)(128)(4,1)} %bitcast.6), calls=%async_computation.4 | async-start | bytes 4194304
  13.4 8.1 %copy-start.1 = (f32[2048]{0:T(1024)S(1)}, f32[2048]{0:T(1024)}, u32[]{:S(2)}) copy-start(f32[2048]{0:T(1024)} %param.15) | copy-start | bytes 24580
  13.4 8.1 %copy-start.2 = (f32[2048]{0:T(1024)S(1)}, f32[2048]{0:T(1024)}, u32[]{:S(2)}) copy-start(f32[2048]{0:T(1024)} %param.11) | copy-start | bytes 24580
  13.5 17.6 %collective-permute-start.10 = (bf16[256,512]{1,0:T(8,128)(2,1)S(1)}, bf16[256,512]{1,0:T(8,128)(2,1)S(1)}, u32[]{:S(2)}, u32[]{:S(2)}) collective-permute-start(bf16[256,512]{1,0:T(8,128)(2,1)S(1)} %forward.1), channel_id=1, source_target_pairs={{0,2},{1,3},{2,0},{3,1},{4,6},{5,7},{6,4},{7,5},{8,10},{9,11},{10,... | collective-permute-start | bytes 786440 | tf_op jit(solution)/shard_map/ppermute | solution.py:342
  16.2 14.9 %collective-permute-start.11 = (bf16[256,512]{1,0:T(8,128)(2,1)S(1)}, bf16[256,512]{1,0:T(8,128)(2,1)S(1)}, u32[]{:S(2)}, u32[]{:S(2)}) collective-permute-start(bf16[256,512]{1,0:T(8,128)(2,1)S(1)} %get-tuple-element.64), channel_id=1, source_target_pairs={{0,1},{1,0},{2,3},{3,2},{4,5},{5,4},{6,7},{7,6},{8,9},{9,8},{10,11... | collective-permute-start | bytes 786440 | tf_op jit(solution)/shard_map/ppermute | solution.py:342
  20.0 1.4 %collective-permute-start.4 = (bf16[32,2048]{1,0:T(8,128)(2,1)S(1)}, bf16[32,2048]{1,0:T(8,128)(2,1)S(1)}, u32[]{:S(2)}, u32[]{:S(2)}) collective-permute-start(bf16[32,2048]{1,0:T(8,128)(2,1)S(1)} %get-tuple-element.43), channel_id=1, source_target_pairs={{0,4},{4,0},{1,5},{5,1},{2,6},{6,2},{3,7},{7,3},{8,12},{12,8},{9,1... | collective-permute-start | bytes 393224 | tf_op jit(solution)/shard_map/ppermute | solution.py:342
  23.3 7.3 %collective-permute-start.6 = (bf16[16,640]{1,0:T(8,128)(2,1)S(1)}, bf16[16,640]{1,0:T(8,128)(2,1)S(1)}, u32[]{:S(2)}, u32[]{:S(2)}) collective-permute-start(bf16[16,640]{1,0:T(8,128)(2,1)S(1)} %get-tuple-element.57), channel_id=1, source_target_pairs={{0,1},{1,0},{2,3},{3,2},{4,5},{5,4},{6,7},{7,6},{8,9},{9,8},{10,11... | collective-permute-start | bytes 61448 | tf_op jit(solution)/shard_map/ppermute | solution.py:342
  24.3 6.2 %collective-permute-start.7 = (bf16[16,640]{1,0:T(8,128)(2,1)S(1)}, bf16[16,640]{1,0:T(8,128)(2,1)S(1)}, u32[]{:S(2)}, u32[]{:S(2)}) collective-permute-start(bf16[16,640]{1,0:T(8,128)(2,1)S(1)} %get-tuple-element.58), channel_id=1, source_target_pairs={{0,2},{1,3},{2,0},{3,1},{4,6},{5,7},{6,4},{7,5},{8,10},{9,11},{10,... | collective-permute-start | bytes 61448 | tf_op jit(solution)/shard_map/ppermute | solution.py:342
  25.0 6.0 %collective-permute-start.8 = (bf16[16,640]{1,0:T(8,128)(2,1)S(1)}, bf16[16,640]{1,0:T(8,128)(2,1)S(1)}, u32[]{:S(2)}, u32[]{:S(2)}) collective-permute-start(bf16[16,640]{1,0:T(8,128)(2,1)S(1)} %get-tuple-element.59), channel_id=1, source_target_pairs={{0,3},{1,2},{2,1},{3,0},{4,7},{5,6},{6,5},{7,4},{8,11},{9,10},{10,... | collective-permute-start | bytes 61448 | tf_op jit(solution)/shard_map/ppermute | solution.py:342

commit v5 on v4

--- a/solution.py
+++ b/solution.py
@@ -432,7 +432,7 @@
         + [shape((slots, cols + 128), BF16)] * tp_count,
         cost=SLOT_COST,
     )
-    messages = [messages[0]] + [swap(messages[k], "tp", k) for k in range(1, tp_count)]
+    messages = [swap(messages[k], "tp", k) for k in range(tp_count - 1, 0, -1)] + [messages[0]]
 
     scaled_grad, stream = call(
         grad_kernel,

time: 33.5 us -> 33.1 us (0.988)
  waiting for transfers between devices: 1.89 us -> 1.48 us
    ppermute x11, waiting for transfers between devices: 1.89 us -> 1.47 us  [swap(): lax.ppermute(array, axis, [(i, i ^ k) for i in range(lax.axis_size(axis))])]
  transfers between devices with their start and end apart: 12 -> 12, of which waited for: 2 -> 2; matrix products, arithmetic and copies ran while one was open for 0% -> 0% of each run, Pallas kernels for 30% -> 31%
where the time goes in v5:
time: 33.1 us; the launch traced here: 33 us
  starting transfers between devices  15.7 us (47%)
  Pallas kernels  15 us (45%)
  waiting for transfers between devices  1.48 us (4%)
  between operations  0.78 us (2%)
    ppermute x11, starting transfers between devices, swap(): lax.ppermute(array, axis, [(i, i ^ k) for i in range(lax.axis_size(axis))])  15.5 us
    pallas_call x8, Pallas kernels, call(): pl.pallas_call(kernel, out_shape=outs, in_specs=in_specs, out_specs=out_s...  15 us
    ppermute x11, waiting for transfers between devices, swap(): lax.ppermute(array, axis, [(i, i ^ k) for i in range(lax.axis_size(axis))])  1.47 us
  transfers between devices with their start and end apart: 12, of which 2 were waited for; matrix products, arithmetic and copies ran while one was open for 0% of the time, Pallas kernels for 31%

profile of v5, /device:TPU:0, one launch (start us, length us, event | category | flops | bytes accessed | tf_op | source)
XLA Modules:
  0.0 33.0 jit_solution(11657937715696587199)
XLA Ops:
  0.7 0.0 slice-start
  0.7 2.5 %first_text_kv.1 = (bf16[256,512]{1,0:T(8,128)(2,1)S(1)}, bf16[256,2048]{1,0:T(8,128)(2,1)S(1)}, bf16[256,2048]{1,0:T(8,128)(2,1)S(1)}, s32[1,256]{1,0:T(1,128)S(1)}, s32[4,4]{1,0:T(4,128)S(1)}) custom-call(bf16[256,2048]{1,0:T(8,128)(2,1)} %refs_0_.1, f32[1,2048]{1,0:T(1,128)} %bitcast.8, bf16[2048,2048]{1,0:T(8,128)(2,1)} %weight, s32[1,256]{1,0:T(1,128)} %bitcast.13, ...), custom_call_target="tpu_custom_call" | custom-call | flops 1024 | bytes 1024 | tf_op jit(solution)/shard_map/first_text_kv/pallas_call | solution.py:325
  3.2 0.5 %collective-permute-start = (s32[1,256]{1,0:T(1,128)S(1)}, s32[1,256]{1,0:T(1,128)S(1)}, u32[]{:S(2)}, u32[]{:S(2)}) collective-permute-start(s32[1,256]{1,0:T(1,128)S(1)} %get-tuple-element.34.refs_1_), channel_id=1, source_target_pairs={{0,4},{4,0},{1,5},{5,1},{2,6},{6,2},{3,7},{7,3},{8,12},{12,8},{9,1... | collective-permute-start | bytes 3080 | tf_op jit(solution)/shard_map/ppermute | solution.py:342
  3.7 2.6 %collective-permute-start.9 = (bf16[256,512]{1,0:T(8,128)(2,1)S(1)}, bf16[256,512]{1,0:T(8,128)(2,1)S(1)}, u32[]{:S(2)}, u32[]{:S(2)}) collective-permute-start(bf16[256,512]{1,0:T(8,128)(2,1)S(1)} %get-tuple-element.48.refs_4_), channel_id=1, source_target_pairs={{0,1},{1,0},{2,3},{3,2},{4,5},{5,4},{6,7},{7,6},{8,9},{9,8},{10,11... | collective-permute-start | bytes 786440 | tf_op jit(solution)/shard_map/ppermute | solution.py:342
  6.4 0.2 collective-permute-start.5
  6.5 0.0 collective-permute-done.refs_0_
  6.6 0.0 slice-start.1
  6.6 0.0 slice-start.2
  6.6 0.0 slice-start.3
  6.6 1.1 %gather_rows.1 = (bf16[16,1792]{1,0:T(8,128)(2,1)S(1)}, bf16[16,1792]{1,0:T(8,128)(2,1)S(1)}, bf16[16,1792]{1,0:T(8,128)(2,1)S(1)}, bf16[16,1792]{1,0:T(8,128)(2...) custom-call(s32[1,256]{1,0:T(1,128)S(1)} %collective-permute-done.refs_0_, ...), custom_call_target="tpu_custom_call" | custom-call | flops 4000000000 | bytes 1024 | tf_op jit(solution)/shard_map/gather_rows/pallas_call | solution.py:325
  7.7 1.6 %collective-permute-start.1 = (bf16[16,1792]{1,0:T(8,128)(2,1)S(1)}, bf16[16,1792]{1,0:T(8,128)(2,1)S(1)}, u32[]{:S(2)}, u32[]{:S(2)}) collective-permute-start(bf16[16,1792]{1,0:T(8,128)(2,1)S(1)} %get-tuple-element.37.refs_1_), channel_id=1, source_target_pairs={{0,8},{8,0},{16,24},{24,16},{1,9},{9,1},{17,25},{25,17},{2,10},{10... | collective-permute-start | bytes 172040 | tf_op jit(solution)/shard_map/ppermute | solution.py:342
  9.2 1.5 %collective-permute-start.2 = (bf16[16,1792]{1,0:T(8,128)(2,1)S(1)}, bf16[16,1792]{1,0:T(8,128)(2,1)S(1)}, u32[]{:S(2)}, u32[]{:S(2)}) collective-permute-start(bf16[16,1792]{1,0:T(8,128)(2,1)S(1)} %get-tuple-element.38.refs_2_), channel_id=1, source_target_pairs={{0,16},{8,24},{16,0},{24,8},{1,17},{9,25},{17,1},{25,9},{2,18},{10... | collective-permute-start | bytes 172040 | tf_op jit(solution)/shard_map/ppermute | solution.py:342
  10.7 0.5 %collective-permute-start.3 = (bf16[16,1792]{1,0:T(8,128)(2,1)S(1)}, bf16[16,1792]{1,0:T(8,128)(2,1)S(1)}, u32[]{:S(2)}, u32[]{:S(2)}) collective-permute-start(bf16[16,1792]{1,0:T(8,128)(2,1)S(1)} %get-tuple-element.39.refs_3_), channel_id=1, source_target_pairs={{0,24},{8,16},{16,8},{24,0},{1,25},{9,17},{17,9},{25,1},{2,26},{10... | collective-permute-start | bytes 172040 | tf_op jit(solution)/shard_map/ppermute | solution.py:342
  11.2 2.1 %text_kv.1 = (bf16[256,512]{1,0:T(8,128)(2,1)S(1)}, bf16[256,512]{1,0:T(8,128)(2,1)S(1)}, f32[256,512]{1,0:T(8,128)S(1)}, f32[8,256]{1,0:T(8,128)S(1)}) custom-call(bf16[256,2048]{1,0:T(8,128)(2,1)S(1)} %get-tuple-element.46.refs_0_, bf16[2048,2048]{1,0:T(8,128)(2,1)S(1)} %bitcast.5, bf16[256,2048]{1,0:T(8,128)(2,1)S(1)} %copy-done, ...), custom_call_target="tpu_custom_call" | custom-call | flops 1024 | bytes 1024 | tf_op jit(solution)/shard_map/text_kv/pallas_call | solution.py:325
  13.4 0.0 collective-permute-done.9.turned
  13.4 0.1 forward.1
  13.5 2.7 %collective-permute-start.10 = (bf16[256,512]{1,0:T(8,128)(2,1)S(1)}, bf16[256,512]{1,0:T(8,128)(2,1)S(1)}, u32[]{:S(2)}, u32[]{:S(2)}) collective-permute-start(bf16[256,512]{1,0:T(8,128)(2,1)S(1)} %forward.1), channel_id=1, source_target_pairs={{0,2},{1,3},{2,0},{3,1},{4,6},{5,7},{6,4},{7,5},{8,10},{9,11},{10,... | collective-permute-start | bytes 786440 | tf_op jit(solution)/shard_map/ppermute | solution.py:342
  16.2 1.6 %collective-permute-start.11 = (bf16[256,512]{1,0:T(8,128)(2,1)S(1)}, bf16[256,512]{1,0:T(8,128)(2,1)S(1)}, u32[]{:S(2)}, u32[]{:S(2)}) collective-permute-start(bf16[256,512]{1,0:T(8,128)(2,1)S(1)} %get-tuple-element.64), channel_id=1, source_target_pairs={{0,1},{1,0},{2,3},{3,2},{4,5},{5,4},{6,7},{7,6},{8,9},{9,8},{10,11... | collective-permute-start | bytes 786440 | tf_op jit(solution)/shard_map/ppermute | solution.py:342
  17.8 0.0 collective-permute-done.2.refs_5_
  17.8 0.0 collective-permute-done.3.refs_6_
  17.8 2.2 %merge_rows.1 = (f32[32,2048]{1,0:T(8,128)S(1)}, bf16[32,2048]{1,0:T(8,128)(2,1)S(1)}, bf16[32,2048]{1,0:T(8,128)(2,1)S(1)}) custom-call(bf16[16,1792]{1,0:T(8,128)(2,1)S(1)} %get-tuple-element.36.refs_0_, bf16[16,1792]{1,0:T(8,128)(2,1)S(1)} %get-tuple-element.37.refs_1_, bf16[16,1792]{1,0:T(8,128)(2,1)S(1)} %get-tuple-element.38.refs_2_, ...), custom_call_target="tpu_custom_call" | custom-call | flops 1024 | bytes 1024 | tf_op jit(solution)/shard_map/merge_rows/pallas_call | solution.py:325
  20.0 0.1 collective-permute-start.4
  20.1 1.3 %collective-permute-done.4.refs_1_ = bf16[32,2048]{1,0:T(8,128)(2,1)S(1)} collective-permute-done((bf16[32,2048]{1,0:T(8,128)(2,1)S(1)}, bf16[32,2048]{1,0:T(8,128)(2,1)S(1)}, u32[]{:S(2)}, u32[]{:S(2)}) %collective-permute-start.4) | collective-permute-done | bytes 131104 | tf_op jit(solution)/shard_map/ppermute | solution.py:342
  21.4 0.0 collective-permute-done.5.refs_8_
  21.5 1.8 %slot_kv.1 = (bf16[32,2048]{1,0:T(8,128)(2,1)S(1)}, f32[256,512]{1,0:T(8,128)S(1)}, bf16[16,640]{1,0:T(8,128)(2,1)S(1)}, bf16[16,640]{1,0:T(8,128)(2,1)S(1)}, bf...) custom-call(f32[32,2048]{1,0:T(8,128)S(1)} %get-tuple-element.42.refs_0_, ...), custom_call_target="tpu_custom_call" | custom-call | flops 1024 | bytes 1024 | tf_op jit(solution)/shard_map/slot_kv/pallas_call | solution.py:325
  23.3 1.1 %collective-permute-start.6 = (bf16[16,640]{1,0:T(8,128)(2,1)S(1)}, bf16[16,640]{1,0:T(8,128)(2,1)S(1)}, u32[]{:S(2)}, u32[]{:S(2)}) collective-permute-start(bf16[16,640]{1,0:T(8,128)(2,1)S(1)} %get-tuple-element.56), channel_id=1, source_target_pairs={{0,3},{1,2},{2,1},{3,0},{4,7},{5,6},{6,5},{7,4},{8,11},{9,10},{10,... | collective-permute-start | bytes 61448 | tf_op jit(solution)/shard_map/ppermute | solution.py:342
  24.4 1.4 %collective-permute-start.7 = (bf16[16,640]{1,0:T(8,128)(2,1)S(1)}, bf16[16,640]{1,0:T(8,128)(2,1)S(1)}, u32[]{:S(2)}, u32[]{:S(2)}) collective-permute-start(bf16[16,640]{1,0:T(8,128)(2,1)S(1)} %get-tuple-element.57), channel_id=1, source_target_pairs={{0,2},{1,3},{2,0},{3,1},{4,6},{5,7},{6,4},{7,5},{8,10},{9,11},{10,... | collective-permute-start | bytes 61448 | tf_op jit(solution)/shard_map/ppermute | solution.py:342
  25.8 1.9 %collective-permute-start.8 = (bf16[16,640]{1,0:T(8,128)(2,1)S(1)}, bf16[16,640]{1,0:T(8,128)(2,1)S(1)}, u32[]{:S(2)}, u32[]{:S(2)}) collective-permute-start(bf16[16,640]{1,0:T(8,128)(2,1)S(1)} %get-tuple-element.58), channel_id=1, source_target_pairs={{0,1},{1,0},{2,3},{3,2},{4,5},{5,4},{6,7},{7,6},{8,9},{9,8},{10,11... | collective-permute-start | bytes 61448 | tf_op jit(solution)/shard_map/ppermute | solution.py:342
  27.7 2.8 %normed_grad.1 = (f32[272,2048]{1,0:T(8,128)S(1)}, bf16[256,2048]{1,0:T(8,128)(2,1)S(1)}) custom-call(bf16[256,2048]{1,0:T(8,128)(2,1)S(1)} %copy-done, bf16[32,2048]{1,0:T(8,128)(2,1)S(1)} %get-tuple-element.45.refs_5_.grad_rows, bf16[2048,2048]{1,0:T(8,128)(2,1)S(1)} %bitcast.5, f32[1,2048]{1,0:T(1,128)S(1)} %bitcast.10, ...), custom_call_target="tpu_custom_call" | custom-call | flops 1000000000 | bytes 1024 | tf_op jit(solution)/shard_map/normed_grad/pallas_call | solution.py:325
  30.5 0.1 collective-permute-done.6.refs_5_
  30.7 0.0 collective-permute-done.11.refs_11_
  30.7 2.3 %outputs.1 = (bf16[256,512]{1,0:T(8,128)(2,1)}, bf16[256,2048]{1,0:T(8,128)(2,1)}, bf16[256,2048]{1,0:T(8,128)(2,1)}) custom-call(bf16[32,2048]{1,0:T(8,128)(2,1)S(1)} %get-tuple-element.51.rows.refs_0_, f32[272,2048]{1,0:T(8,128)S(1)} %get-tuple-element.53.refs_1_, bf16[256,2048]{1,0:T(8,128)(2,1)S(1)} %get-tuple-element.54.refs_2_, ...), custom_call_target="tpu_custom_call" | custom-call | flops 1024 | bytes 1024 | tf_op jit(solution)/shard_map/outputs/pallas_call | solution.py:325
  (20 shorter events, 0.0 us)
Async XLA Ops:
  0.6 5.9 %copy-start = (bf16[256,2048]{1,0:T(8,128)(2,1)S(1)}, bf16[256,2048]{1,0:T(8,128)(2,1)}, u32[]{:S(2)}) copy-start(bf16[256,2048]{1,0:T(8,128)(2,1)} %grad.1) | copy-start | bytes 3145732
  0.6 5.9 %copy-start.3 = (bf16[512,2560]{1,0:T(8,128)(2,1)S(1)}, bf16[512,2560]{1,0:T(8,128)(2,1)}, u32[]{:S(2)}) copy-start(bf16[512,2560]{1,0:T(8,128)(2,1)} %refs_4_.1) | copy-start | bytes 7864324
  0.7 10.6 %slice-start = ((s8[8388608]{0:T(1024)(128)(4,1)}), s8[4194304]{0:T(1024)(128)(4,1)S(1)}, s32[]{:S(2)}) async-start(s8[8388608]{0:T(1024)(128)(4,1)} %bitcast.4), calls=%async_computation | async-start | bytes 8388608
  3.2 3.3 %collective-permute-start = (s32[1,256]{1,0:T(1,128)S(1)}, s32[1,256]{1,0:T(1,128)S(1)}, u32[]{:S(2)}, u32[]{:S(2)}) collective-permute-start(s32[1,256]{1,0:T(1,128)S(1)} %get-tuple-element.34.refs_1_), channel_id=1, source_target_pairs={{0,4},{4,0},{1,5},{5,1},{2,6},{6,2},{3,7},{7,3},{8,12},{12,8},{9,1... | collective-permute-start | bytes 3080 | tf_op jit(solution)/shard_map/ppermute | solution.py:342
  3.7 9.7 %collective-permute-start.9 = (bf16[256,512]{1,0:T(8,128)(2,1)S(1)}, bf16[256,512]{1,0:T(8,128)(2,1)S(1)}, u32[]{:S(2)}, u32[]{:S(2)}) collective-permute-start(bf16[256,512]{1,0:T(8,128)(2,1)S(1)} %get-tuple-element.48.refs_4_), channel_id=1, source_target_pairs={{0,1},{1,0},{2,3},{3,2},{4,5},{5,4},{6,7},{7,6},{8,9},{9,8},{10,11... | collective-permute-start | bytes 786440 | tf_op jit(solution)/shard_map/ppermute | solution.py:342
  6.4 15.1 %collective-permute-start.5 = (bf16[256,512]{1,0:T(8,128)(2,1)S(1)}, bf16[256,512]{1,0:T(8,128)(2,1)S(1)}, u32[]{:S(2)}, u32[]{:S(2)}) collective-permute-start(bf16[256,512]{1,0:T(8,128)(2,1)S(1)} %get-tuple-element.48.refs_4_), channel_id=1, source_target_pairs={{0,4},{1,2},{2,1},{3,7},{4,0},{5,6},{6,5},{7,3},{8,12},{9,10},{10,... | collective-permute-start | bytes 786440 | tf_op jit(solution)/shard_map/ppermute | solution.py:385
  6.6 4.7 %slice-start.1 = ((s8[8388608]{0:T(1024)(128)(4,1)}), s8[4194304]{0:T(1024)(128)(4,1)S(1)}, s32[]{:S(2)}) async-start(s8[8388608]{0:T(1024)(128)(4,1)} %bitcast.4), calls=%async_computation.1 | async-start | bytes 8388608
  6.6 11.2 %slice-start.2 = ((s8[10485760]{0:T(1024)(128)(4,1)}), s8[4194304]{0:T(1024)(128)(4,1)S(1)}, s32[]{:S(2)}) async-start(s8[10485760]{0:T(1024)(128)(4,1)} %bitcast.6), calls=%async_computation.2 | async-start | bytes 8388608
  6.6 11.2 %slice-start.3 = ((s8[10485760]{0:T(1024)(128)(4,1)}), s8[4194304]{0:T(1024)(128)(4,1)S(1)}, s32[]{:S(2)}) async-start(s8[10485760]{0:T(1024)(128)(4,1)} %bitcast.6), calls=%async_computation.3 | async-start | bytes 8388608
  7.7 8.5 %collective-permute-start.1 = (bf16[16,1792]{1,0:T(8,128)(2,1)S(1)}, bf16[16,1792]{1,0:T(8,128)(2,1)S(1)}, u32[]{:S(2)}, u32[]{:S(2)}) collective-permute-start(bf16[16,1792]{1,0:T(8,128)(2,1)S(1)} %get-tuple-element.37.refs_1_), channel_id=1, source_target_pairs={{0,8},{8,0},{16,24},{24,16},{1,9},{9,1},{17,25},{25,17},{2,10},{10... | collective-permute-start | bytes 172040 | tf_op jit(solution)/shard_map/ppermute | solution.py:342
  9.2 8.6 %collective-permute-start.2 = (bf16[16,1792]{1,0:T(8,128)(2,1)S(1)}, bf16[16,1792]{1,0:T(8,128)(2,1)S(1)}, u32[]{:S(2)}, u32[]{:S(2)}) collective-permute-start(bf16[16,1792]{1,0:T(8,128)(2,1)S(1)} %get-tuple-element.38.refs_2_), channel_id=1, source_target_pairs={{0,16},{8,24},{16,0},{24,8},{1,17},{9,25},{17,1},{25,9},{2,18},{10... | collective-permute-start | bytes 172040 | tf_op jit(solution)/shard_map/ppermute | solution.py:342
  10.7 7.0 %collective-permute-start.3 = (bf16[16,1792]{1,0:T(8,128)(2,1)S(1)}, bf16[16,1792]{1,0:T(8,128)(2,1)S(1)}, u32[]{:S(2)}, u32[]{:S(2)}) collective-permute-start(bf16[16,1792]{1,0:T(8,128)(2,1)S(1)} %get-tuple-element.39.refs_3_), channel_id=1, source_target_pairs={{0,24},{8,16},{16,8},{24,0},{1,25},{9,17},{17,9},{25,1},{2,26},{10... | collective-permute-start | bytes 172040 | tf_op jit(solution)/shard_map/ppermute | solution.py:342
  11.2 6.6 %slice-start.4 = ((s8[10485760]{0:T(1024)(128)(4,1)}), s8[2097152]{0:T(1024)(128)(4,1)S(1)}, s32[]{:S(2)}) async-start(s8[10485760]{0:T(1024)(128)(4,1)} %bitcast.6), calls=%async_computation.4 | async-start | bytes 4194304
  13.4 8.1 %copy-start.1 = (f32[2048]{0:T(1024)S(1)}, f32[2048]{0:T(1024)}, u32[]{:S(2)}) copy-start(f32[2048]{0:T(1024)} %param.15) | copy-start | bytes 24580
  13.4 8.1 %copy-start.2 = (f32[2048]{0:T(1024)S(1)}, f32[2048]{0:T(1024)}, u32[]{:S(2)}) copy-start(f32[2048]{0:T(1024)} %param.11) | copy-start | bytes 24580
  13.5 17.2 %collective-permute-start.10 = (bf16[256,512]{1,0:T(8,128)(2,1)S(1)}, bf16[256,512]{1,0:T(8,128)(2,1)S(1)}, u32[]{:S(2)}, u32[]{:S(2)}) collective-permute-start(bf16[256,512]{1,0:T(8,128)(2,1)S(1)} %forward.1), channel_id=1, source_target_pairs={{0,2},{1,3},{2,0},{3,1},{4,6},{5,7},{6,4},{7,5},{8,10},{9,11},{10,... | collective-permute-start | bytes 786440 | tf_op jit(solution)/shard_map/ppermute | solution.py:342
  16.2 14.5 %collective-permute-start.11 = (bf16[256,512]{1,0:T(8,128)(2,1)S(1)}, bf16[256,512]{1,0:T(8,128)(2,1)S(1)}, u32[]{:S(2)}, u32[]{:S(2)}) collective-permute-start(bf16[256,512]{1,0:T(8,128)(2,1)S(1)} %get-tuple-element.64), channel_id=1, source_target_pairs={{0,1},{1,0},{2,3},{3,2},{4,5},{5,4},{6,7},{7,6},{8,9},{9,8},{10,11... | collective-permute-start | bytes 786440 | tf_op jit(solution)/shard_map/ppermute | solution.py:342
  20.0 1.4 %collective-permute-start.4 = (bf16[32,2048]{1,0:T(8,128)(2,1)S(1)}, bf16[32,2048]{1,0:T(8,128)(2,1)S(1)}, u32[]{:S(2)}, u32[]{:S(2)}) collective-permute-start(bf16[32,2048]{1,0:T(8,128)(2,1)S(1)} %get-tuple-element.43), channel_id=1, source_target_pairs={{0,4},{4,0},{1,5},{5,1},{2,6},{6,2},{3,7},{7,3},{8,12},{12,8},{9,1... | collective-permute-start | bytes 393224 | tf_op jit(solution)/shard_map/ppermute | solution.py:342
  23.3 7.4 %collective-permute-start.6 = (bf16[16,640]{1,0:T(8,128)(2,1)S(1)}, bf16[16,640]{1,0:T(8,128)(2,1)S(1)}, u32[]{:S(2)}, u32[]{:S(2)}) collective-permute-start(bf16[16,640]{1,0:T(8,128)(2,1)S(1)} %get-tuple-element.56), channel_id=1, source_target_pairs={{0,3},{1,2},{2,1},{3,0},{4,7},{5,6},{6,5},{7,4},{8,11},{9,10},{10,... | collective-permute-start | bytes 61448 | tf_op jit(solution)/shard_map/ppermute | solution.py:342
  24.4 6.2 %collective-permute-start.7 = (bf16[16,640]{1,0:T(8,128)(2,1)S(1)}, bf16[16,640]{1,0:T(8,128)(2,1)S(1)}, u32[]{:S(2)}, u32[]{:S(2)}) collective-permute-start(bf16[16,640]{1,0:T(8,128)(2,1)S(1)} %get-tuple-element.57), channel_id=1, source_target_pairs={{0,2},{1,3},{2,0},{3,1},{4,6},{5,7},{6,4},{7,5},{8,10},{9,11},{10,... | collective-permute-start | bytes 61448 | tf_op jit(solution)/shard_map/ppermute | solution.py:342
  25.8 4.9 %collective-permute-start.8 = (bf16[16,640]{1,0:T(8,128)(2,1)S(1)}, bf16[16,640]{1,0:T(8,128)(2,1)S(1)}, u32[]{:S(2)}, u32[]{:S(2)}) collective-permute-start(bf16[16,640]{1,0:T(8,128)(2,1)S(1)} %get-tuple-element.58), channel_id=1, source_target_pairs={{0,1},{1,0},{2,3},{3,2},{4,5},{5,4},{6,7},{7,6},{8,9},{9,8},{10,11... | collective-permute-start | bytes 61448 | tf_op jit(solution)/shard_map/ppermute | solution.py:342

commit v6 on v5

--- a/solution.py
+++ b/solution.py
@@ -176,16 +176,18 @@
     got = jnp.concatenate([ref[...] for ref in got_refs], axis=0)
     sent = jnp.concatenate([ref[...] for ref in sent_refs], axis=0)
 
-    def unfold(table, first, step, cols):
-        pieces = [dot(picker(slots, rows, group, cap, i), table[:, cols]) for i in range(first, group, step)]
+    def unfold(table, firsts, step, cols):
+        pieces = []
+        for i in range(0, group, step):
+            picks = jnp.concatenate([picker(slots, rows, group, cap, first + i) for first in firsts], axis=0)
+            pieces.append(dot(picks, table[:, cols]))
         return jnp.concatenate(pieces, axis=1).astype(BF16)
 
     merged = slice(0, width)
-    picked = jnp.concatenate(
-        [unfold(table, first, 2 * cap, merged) for first in (0, cap) for table in (got, sent)], axis=0
-    )
-    grad_rows[:slots] = unfold(sent, 0, cap, slice(width, width + grad_width))
-    grad_rows[slots:] = unfold(got, 0, cap, slice(width, width + grad_width))
+    got_rows, sent_rows = unfold(got, (0, cap), 2 * cap, merged), unfold(sent, (0, cap), 2 * cap, merged)
+    picked = jnp.concatenate([got_rows[:slots], sent_rows[:slots], got_rows[slots:], sent_rows[slots:]], axis=0)
+    grad_rows[:slots] = unfold(sent, (0,), cap, slice(width, width + grad_width))
+    grad_rows[slots:] = unfold(got, (0,), cap, slice(width, width + grad_width))
     cols = weight.shape[1]
     step = min(512, cols)
     for c in range(0, cols, step):
@@ -309,7 +311,7 @@
 
 COST = cost_of(1024)
 CHUNKS = 4
-PIECES = 2
+PIECES = 1
 MERGE_COST = cost_of(1024)
 GRAD_COST = cost_of(1000000000)
 TEXT_COST = cost_of(1024)

time: 33.1 us -> 33 us (level)
  no operation moved by 1% of the time
where the time goes in v6:
time: 33 us; the launch traced here: 32.9 us
  starting transfers between devices  15.7 us (48%)
  Pallas kernels  14.8 us (45%)
  waiting for transfers between devices  1.54 us (5%)
  between operations  0.78 us (2%)
    ppermute x11, starting transfers between devices, swap(): lax.ppermute(array, axis, [(i, i ^ k) for i in range(lax.axis_size(axis))])  15.5 us
    pallas_call x8, Pallas kernels, call(): pl.pallas_call(kernel, out_shape=outs, in_specs=in_specs, out_specs=out_s...  14.8 us
    ppermute x11, waiting for transfers between devices, swap(): lax.ppermute(array, axis, [(i, i ^ k) for i in range(lax.axis_size(axis))])  1.54 us
  transfers between devices with their start and end apart: 12, of which 2 were waited for; matrix products, arithmetic and copies ran while one was open for 0% of the time, Pallas kernels for 31%

profile of v6, /device:TPU:0, one launch (start us, length us, event | category | flops | bytes accessed | tf_op | source)
XLA Modules:
  0.0 32.9 jit_solution(2913481550516800661)
XLA Ops:
  0.7 0.0 slice-start
  0.7 2.5 %first_text_kv.1 = (bf16[256,512]{1,0:T(8,128)(2,1)S(1)}, bf16[256,2048]{1,0:T(8,128)(2,1)S(1)}, bf16[256,2048]{1,0:T(8,128)(2,1)S(1)}, s32[1,256]{1,0:T(1,128)S(1)}, s32[4,4]{1,0:T(4,128)S(1)}) custom-call(bf16[256,2048]{1,0:T(8,128)(2,1)} %refs_0_.1, f32[1,2048]{1,0:T(1,128)} %bitcast.8, bf16[2048,2048]{1,0:T(8,128)(2,1)} %weight, s32[1,256]{1,0:T(1,128)} %bitcast.13, ...), custom_call_target="tpu_custom_call" | custom-call | flops 1024 | bytes 1024 | tf_op jit(solution)/shard_map/first_text_kv/pallas_call | solution.py:327
  3.2 0.5 %collective-permute-start = (s32[1,256]{1,0:T(1,128)S(1)}, s32[1,256]{1,0:T(1,128)S(1)}, u32[]{:S(2)}, u32[]{:S(2)}) collective-permute-start(s32[1,256]{1,0:T(1,128)S(1)} %get-tuple-element.34.refs_1_), channel_id=1, source_target_pairs={{0,4},{4,0},{1,5},{5,1},{2,6},{6,2},{3,7},{7,3},{8,12},{12,8},{9,1... | collective-permute-start | bytes 3080 | tf_op jit(solution)/shard_map/ppermute | solution.py:344
  3.7 2.6 %collective-permute-start.9 = (bf16[256,512]{1,0:T(8,128)(2,1)S(1)}, bf16[256,512]{1,0:T(8,128)(2,1)S(1)}, u32[]{:S(2)}, u32[]{:S(2)}) collective-permute-start(bf16[256,512]{1,0:T(8,128)(2,1)S(1)} %get-tuple-element.48.refs_4_), channel_id=1, source_target_pairs={{0,1},{1,0},{2,3},{3,2},{4,5},{5,4},{6,7},{7,6},{8,9},{9,8},{10,11... | collective-permute-start | bytes 786440 | tf_op jit(solution)/shard_map/ppermute | solution.py:344
  6.4 0.2 collective-permute-start.5
  6.5 0.0 collective-permute-done.refs_0_
  6.6 0.0 slice-start.1
  6.6 0.0 slice-start.2
  6.6 0.0 slice-start.3
  6.6 1.1 %gather_rows.1 = (bf16[16,1792]{1,0:T(8,128)(2,1)S(1)}, bf16[16,1792]{1,0:T(8,128)(2,1)S(1)}, bf16[16,1792]{1,0:T(8,128)(2,1)S(1)}, bf16[16,1792]{1,0:T(8,128)(2...) custom-call(s32[1,256]{1,0:T(1,128)S(1)} %collective-permute-done.refs_0_, ...), custom_call_target="tpu_custom_call" | custom-call | flops 4000000000 | bytes 1024 | tf_op jit(solution)/shard_map/gather_rows/pallas_call | solution.py:327
  7.7 1.6 %collective-permute-start.1 = (bf16[16,1792]{1,0:T(8,128)(2,1)S(1)}, bf16[16,1792]{1,0:T(8,128)(2,1)S(1)}, u32[]{:S(2)}, u32[]{:S(2)}) collective-permute-start(bf16[16,1792]{1,0:T(8,128)(2,1)S(1)} %get-tuple-element.37.refs_1_), channel_id=1, source_target_pairs={{0,8},{8,0},{16,24},{24,16},{1,9},{9,1},{17,25},{25,17},{2,10},{10... | collective-permute-start | bytes 172040 | tf_op jit(solution)/shard_map/ppermute | solution.py:344
  9.2 1.5 %collective-permute-start.2 = (bf16[16,1792]{1,0:T(8,128)(2,1)S(1)}, bf16[16,1792]{1,0:T(8,128)(2,1)S(1)}, u32[]{:S(2)}, u32[]{:S(2)}) collective-permute-start(bf16[16,1792]{1,0:T(8,128)(2,1)S(1)} %get-tuple-element.38.refs_2_), channel_id=1, source_target_pairs={{0,16},{8,24},{16,0},{24,8},{1,17},{9,25},{17,1},{25,9},{2,18},{10... | collective-permute-start | bytes 172040 | tf_op jit(solution)/shard_map/ppermute | solution.py:344
  10.7 0.5 %collective-permute-start.3 = (bf16[16,1792]{1,0:T(8,128)(2,1)S(1)}, bf16[16,1792]{1,0:T(8,128)(2,1)S(1)}, u32[]{:S(2)}, u32[]{:S(2)}) collective-permute-start(bf16[16,1792]{1,0:T(8,128)(2,1)S(1)} %get-tuple-element.39.refs_3_), channel_id=1, source_target_pairs={{0,24},{8,16},{16,8},{24,0},{1,25},{9,17},{17,9},{25,1},{2,26},{10... | collective-permute-start | bytes 172040 | tf_op jit(solution)/shard_map/ppermute | solution.py:344
  11.2 2.1 %text_kv.1 = (bf16[256,512]{1,0:T(8,128)(2,1)S(1)}, bf16[256,512]{1,0:T(8,128)(2,1)S(1)}, f32[256,512]{1,0:T(8,128)S(1)}, f32[8,256]{1,0:T(8,128)S(1)}) custom-call(bf16[256,2048]{1,0:T(8,128)(2,1)S(1)} %get-tuple-element.46.refs_0_, bf16[2048,2048]{1,0:T(8,128)(2,1)S(1)} %bitcast.5, bf16[256,2048]{1,0:T(8,128)(2,1)S(1)} %copy-done, ...), custom_call_target="tpu_custom_call" | custom-call | flops 1024 | bytes 1024 | tf_op jit(solution)/shard_map/text_kv/pallas_call | solution.py:327
  13.4 0.1 forward.1
  13.5 2.7 %collective-permute-start.10 = (bf16[256,512]{1,0:T(8,128)(2,1)S(1)}, bf16[256,512]{1,0:T(8,128)(2,1)S(1)}, u32[]{:S(2)}, u32[]{:S(2)}) collective-permute-start(bf16[256,512]{1,0:T(8,128)(2,1)S(1)} %forward.1), channel_id=1, source_target_pairs={{0,2},{1,3},{2,0},{3,1},{4,6},{5,7},{6,4},{7,5},{8,10},{9,11},{10,... | collective-permute-start | bytes 786440 | tf_op jit(solution)/shard_map/ppermute | solution.py:344
  16.2 0.0 collective-permute-done.1.refs_4_
  16.2 1.6 %collective-permute-start.11 = (bf16[256,512]{1,0:T(8,128)(2,1)S(1)}, bf16[256,512]{1,0:T(8,128)(2,1)S(1)}, u32[]{:S(2)}, u32[]{:S(2)}) collective-permute-start(bf16[256,512]{1,0:T(8,128)(2,1)S(1)} %get-tuple-element.64), channel_id=1, source_target_pairs={{0,1},{1,0},{2,3},{3,2},{4,5},{5,4},{6,7},{7,6},{8,9},{9,8},{10,11... | collective-permute-start | bytes 786440 | tf_op jit(solution)/shard_map/ppermute | solution.py:344
  17.8 2.1 %merge_rows.1 = (f32[32,2048]{1,0:T(8,128)S(1)}, bf16[32,2048]{1,0:T(8,128)(2,1)S(1)}, bf16[32,2048]{1,0:T(8,128)(2,1)S(1)}) custom-call(bf16[16,1792]{1,0:T(8,128)(2,1)S(1)} %get-tuple-element.36.refs_0_, bf16[16,1792]{1,0:T(8,128)(2,1)S(1)} %get-tuple-element.37.refs_1_, bf16[16,1792]{1,0:T(8,128)(2,1)S(1)} %get-tuple-element.38.refs_2_, ...), custom_call_target="tpu_custom_call" | custom-call | flops 1024 | bytes 1024 | tf_op jit(solution)/shard_map/merge_rows/pallas_call | solution.py:327
  20.0 0.1 collective-permute-start.4
  20.0 1.3 %collective-permute-done.4.refs_1_ = bf16[32,2048]{1,0:T(8,128)(2,1)S(1)} collective-permute-done((bf16[32,2048]{1,0:T(8,128)(2,1)S(1)}, bf16[32,2048]{1,0:T(8,128)(2,1)S(1)}, u32[]{:S(2)}, u32[]{:S(2)}) %collective-permute-start.4) | collective-permute-done | bytes 131104 | tf_op jit(solution)/shard_map/ppermute | solution.py:344
  21.4 0.0 collective-permute-done.5.refs_8_
  21.4 1.8 %slot_kv.1 = (bf16[32,2048]{1,0:T(8,128)(2,1)S(1)}, f32[256,512]{1,0:T(8,128)S(1)}, bf16[16,640]{1,0:T(8,128)(2,1)S(1)}, bf16[16,640]{1,0:T(8,128)(2,1)S(1)}, bf...) custom-call(f32[32,2048]{1,0:T(8,128)S(1)} %get-tuple-element.42.refs_0_, ...), custom_call_target="tpu_custom_call" | custom-call | flops 1024 | bytes 1024 | tf_op jit(solution)/shard_map/slot_kv/pallas_call | solution.py:327
  23.2 1.1 %collective-permute-start.6 = (bf16[16,640]{1,0:T(8,128)(2,1)S(1)}, bf16[16,640]{1,0:T(8,128)(2,1)S(1)}, u32[]{:S(2)}, u32[]{:S(2)}) collective-permute-start(bf16[16,640]{1,0:T(8,128)(2,1)S(1)} %get-tuple-element.56), channel_id=1, source_target_pairs={{0,3},{1,2},{2,1},{3,0},{4,7},{5,6},{6,5},{7,4},{8,11},{9,10},{10,... | collective-permute-start | bytes 61448 | tf_op jit(solution)/shard_map/ppermute | solution.py:344
  24.4 1.4 %collective-permute-start.7 = (bf16[16,640]{1,0:T(8,128)(2,1)S(1)}, bf16[16,640]{1,0:T(8,128)(2,1)S(1)}, u32[]{:S(2)}, u32[]{:S(2)}) collective-permute-start(bf16[16,640]{1,0:T(8,128)(2,1)S(1)} %get-tuple-element.57), channel_id=1, source_target_pairs={{0,2},{1,3},{2,0},{3,1},{4,6},{5,7},{6,4},{7,5},{8,10},{9,11},{10,... | collective-permute-start | bytes 61448 | tf_op jit(solution)/shard_map/ppermute | solution.py:344
  25.7 1.9 %collective-permute-start.8 = (bf16[16,640]{1,0:T(8,128)(2,1)S(1)}, bf16[16,640]{1,0:T(8,128)(2,1)S(1)}, u32[]{:S(2)}, u32[]{:S(2)}) collective-permute-start(bf16[16,640]{1,0:T(8,128)(2,1)S(1)} %get-tuple-element.58), channel_id=1, source_target_pairs={{0,1},{1,0},{2,3},{3,2},{4,5},{5,4},{6,7},{7,6},{8,9},{9,8},{10,11... | collective-permute-start | bytes 61448 | tf_op jit(solution)/shard_map/ppermute | solution.py:344
  27.6 2.8 %normed_grad.1 = (f32[272,2048]{1,0:T(8,128)S(1)}, bf16[256,2048]{1,0:T(8,128)(2,1)S(1)}) custom-call(bf16[256,2048]{1,0:T(8,128)(2,1)S(1)} %copy-done, bf16[32,2048]{1,0:T(8,128)(2,1)S(1)} %get-tuple-element.45.refs_5_.grad_rows, bf16[2048,2048]{1,0:T(8,128)(2,1)S(1)} %bitcast.5, f32[1,2048]{1,0:T(1,128)S(1)} %bitcast.10, ...), custom_call_target="tpu_custom_call" | custom-call | flops 1000000000 | bytes 1024 | tf_op jit(solution)/shard_map/normed_grad/pallas_call | solution.py:327
  30.5 0.2 collective-permute-done.6.refs_5_
  30.6 0.0 collective-permute-done.7.refs_6_
  30.6 0.0 collective-permute-done.8.refs_7_
  30.6 0.0 collective-permute-done.10.refs_10_
  30.7 2.2 %outputs.1 = (bf16[256,512]{1,0:T(8,128)(2,1)}, bf16[256,2048]{1,0:T(8,128)(2,1)}, bf16[256,2048]{1,0:T(8,128)(2,1)}) custom-call(bf16[32,2048]{1,0:T(8,128)(2,1)S(1)} %get-tuple-element.51.rows.refs_0_, f32[272,2048]{1,0:T(8,128)S(1)} %get-tuple-element.53.refs_1_, bf16[256,2048]{1,0:T(8,128)(2,1)S(1)} %get-tuple-element.54.refs_2_, ...), custom_call_target="tpu_custom_call" | custom-call | flops 1024 | bytes 1024 | tf_op jit(solution)/shard_map/outputs/pallas_call | solution.py:327
  (20 shorter events, 0.0 us)
Async XLA Ops:
  0.6 5.9 %copy-start = (bf16[256,2048]{1,0:T(8,128)(2,1)S(1)}, bf16[256,2048]{1,0:T(8,128)(2,1)}, u32[]{:S(2)}) copy-start(bf16[256,2048]{1,0:T(8,128)(2,1)} %grad.1) | copy-start | bytes 3145732
  0.6 5.9 %copy-start.3 = (bf16[512,2560]{1,0:T(8,128)(2,1)S(1)}, bf16[512,2560]{1,0:T(8,128)(2,1)}, u32[]{:S(2)}) copy-start(bf16[512,2560]{1,0:T(8,128)(2,1)} %refs_4_.1) | copy-start | bytes 7864324
  0.7 10.6 %slice-start = ((s8[8388608]{0:T(1024)(128)(4,1)}), s8[4194304]{0:T(1024)(128)(4,1)S(1)}, s32[]{:S(2)}) async-start(s8[8388608]{0:T(1024)(128)(4,1)} %bitcast.4), calls=%async_computation | async-start | bytes 8388608
  3.2 3.3 %collective-permute-start = (s32[1,256]{1,0:T(1,128)S(1)}, s32[1,256]{1,0:T(1,128)S(1)}, u32[]{:S(2)}, u32[]{:S(2)}) collective-permute-start(s32[1,256]{1,0:T(1,128)S(1)} %get-tuple-element.34.refs_1_), channel_id=1, source_target_pairs={{0,4},{4,0},{1,5},{5,1},{2,6},{6,2},{3,7},{7,3},{8,12},{12,8},{9,1... | collective-permute-start | bytes 3080 | tf_op jit(solution)/shard_map/ppermute | solution.py:344
  3.7 9.7 %collective-permute-start.9 = (bf16[256,512]{1,0:T(8,128)(2,1)S(1)}, bf16[256,512]{1,0:T(8,128)(2,1)S(1)}, u32[]{:S(2)}, u32[]{:S(2)}) collective-permute-start(bf16[256,512]{1,0:T(8,128)(2,1)S(1)} %get-tuple-element.48.refs_4_), channel_id=1, source_target_pairs={{0,1},{1,0},{2,3},{3,2},{4,5},{5,4},{6,7},{7,6},{8,9},{9,8},{10,11... | collective-permute-start | bytes 786440 | tf_op jit(solution)/shard_map/ppermute | solution.py:344
  6.4 15.0 %collective-permute-start.5 = (bf16[256,512]{1,0:T(8,128)(2,1)S(1)}, bf16[256,512]{1,0:T(8,128)(2,1)S(1)}, u32[]{:S(2)}, u32[]{:S(2)}) collective-permute-start(bf16[256,512]{1,0:T(8,128)(2,1)S(1)} %get-tuple-element.48.refs_4_), channel_id=1, source_target_pairs={{0,4},{1,2},{2,1},{3,7},{4,0},{5,6},{6,5},{7,3},{8,12},{9,10},{10,... | collective-permute-start | bytes 786440 | tf_op jit(solution)/shard_map/ppermute | solution.py:387
  6.6 4.7 %slice-start.1 = ((s8[8388608]{0:T(1024)(128)(4,1)}), s8[4194304]{0:T(1024)(128)(4,1)S(1)}, s32[]{:S(2)}) async-start(s8[8388608]{0:T(1024)(128)(4,1)} %bitcast.4), calls=%async_computation.1 | async-start | bytes 8388608
  6.6 11.2 %slice-start.2 = ((s8[10485760]{0:T(1024)(128)(4,1)}), s8[4194304]{0:T(1024)(128)(4,1)S(1)}, s32[]{:S(2)}) async-start(s8[10485760]{0:T(1024)(128)(4,1)} %bitcast.6), calls=%async_computation.2 | async-start | bytes 8388608
  6.6 11.2 %slice-start.3 = ((s8[10485760]{0:T(1024)(128)(4,1)}), s8[4194304]{0:T(1024)(128)(4,1)S(1)}, s32[]{:S(2)}) async-start(s8[10485760]{0:T(1024)(128)(4,1)} %bitcast.6), calls=%async_computation.3 | async-start | bytes 8388608
  7.7 8.5 %collective-permute-start.1 = (bf16[16,1792]{1,0:T(8,128)(2,1)S(1)}, bf16[16,1792]{1,0:T(8,128)(2,1)S(1)}, u32[]{:S(2)}, u32[]{:S(2)}) collective-permute-start(bf16[16,1792]{1,0:T(8,128)(2,1)S(1)} %get-tuple-element.37.refs_1_), channel_id=1, source_target_pairs={{0,8},{8,0},{16,24},{24,16},{1,9},{9,1},{17,25},{25,17},{2,10},{10... | collective-permute-start | bytes 172040 | tf_op jit(solution)/shard_map/ppermute | solution.py:344
  9.2 8.6 %collective-permute-start.2 = (bf16[16,1792]{1,0:T(8,128)(2,1)S(1)}, bf16[16,1792]{1,0:T(8,128)(2,1)S(1)}, u32[]{:S(2)}, u32[]{:S(2)}) collective-permute-start(bf16[16,1792]{1,0:T(8,128)(2,1)S(1)} %get-tuple-element.38.refs_2_), channel_id=1, source_target_pairs={{0,16},{8,24},{16,0},{24,8},{1,17},{9,25},{17,1},{25,9},{2,18},{10... | collective-permute-start | bytes 172040 | tf_op jit(solution)/shard_map/ppermute | solution.py:344
  10.7 7.0 %collective-permute-start.3 = (bf16[16,1792]{1,0:T(8,128)(2,1)S(1)}, bf16[16,1792]{1,0:T(8,128)(2,1)S(1)}, u32[]{:S(2)}, u32[]{:S(2)}) collective-permute-start(bf16[16,1792]{1,0:T(8,128)(2,1)S(1)} %get-tuple-element.39.refs_3_), channel_id=1, source_target_pairs={{0,24},{8,16},{16,8},{24,0},{1,25},{9,17},{17,9},{25,1},{2,26},{10... | collective-permute-start | bytes 172040 | tf_op jit(solution)/shard_map/ppermute | solution.py:344
  11.2 6.6 %slice-start.4 = ((s8[10485760]{0:T(1024)(128)(4,1)}), s8[2097152]{0:T(1024)(128)(4,1)S(1)}, s32[]{:S(2)}) async-start(s8[10485760]{0:T(1024)(128)(4,1)} %bitcast.6), calls=%async_computation.4 | async-start | bytes 4194304
  13.4 8.0 %copy-start.1 = (f32[2048]{0:T(1024)S(1)}, f32[2048]{0:T(1024)}, u32[]{:S(2)}) copy-start(f32[2048]{0:T(1024)} %param.15) | copy-start | bytes 24580
  13.4 8.0 %copy-start.2 = (f32[2048]{0:T(1024)S(1)}, f32[2048]{0:T(1024)}, u32[]{:S(2)}) copy-start(f32[2048]{0:T(1024)} %param.11) | copy-start | bytes 24580
  13.5 17.2 %collective-permute-start.10 = (bf16[256,512]{1,0:T(8,128)(2,1)S(1)}, bf16[256,512]{1,0:T(8,128)(2,1)S(1)}, u32[]{:S(2)}, u32[]{:S(2)}) collective-permute-start(bf16[256,512]{1,0:T(8,128)(2,1)S(1)} %forward.1), channel_id=1, source_target_pairs={{0,2},{1,3},{2,0},{3,1},{4,6},{5,7},{6,4},{7,5},{8,10},{9,11},{10,... | collective-permute-start | bytes 786440 | tf_op jit(solution)/shard_map/ppermute | solution.py:344
  16.2 14.5 %collective-permute-start.11 = (bf16[256,512]{1,0:T(8,128)(2,1)S(1)}, bf16[256,512]{1,0:T(8,128)(2,1)S(1)}, u32[]{:S(2)}, u32[]{:S(2)}) collective-permute-start(bf16[256,512]{1,0:T(8,128)(2,1)S(1)} %get-tuple-element.64), channel_id=1, source_target_pairs={{0,1},{1,0},{2,3},{3,2},{4,5},{5,4},{6,7},{7,6},{8,9},{9,8},{10,11... | collective-permute-start | bytes 786440 | tf_op jit(solution)/shard_map/ppermute | solution.py:344
  20.0 1.4 %collective-permute-start.4 = (bf16[32,2048]{1,0:T(8,128)(2,1)S(1)}, bf16[32,2048]{1,0:T(8,128)(2,1)S(1)}, u32[]{:S(2)}, u32[]{:S(2)}) collective-permute-start(bf16[32,2048]{1,0:T(8,128)(2,1)S(1)} %get-tuple-element.43), channel_id=1, source_target_pairs={{0,4},{4,0},{1,5},{5,1},{2,6},{6,2},{3,7},{7,3},{8,12},{12,8},{9,1... | collective-permute-start | bytes 393224 | tf_op jit(solution)/shard_map/ppermute | solution.py:344
  23.2 7.4 %collective-permute-start.6 = (bf16[16,640]{1,0:T(8,128)(2,1)S(1)}, bf16[16,640]{1,0:T(8,128)(2,1)S(1)}, u32[]{:S(2)}, u32[]{:S(2)}) collective-permute-start(bf16[16,640]{1,0:T(8,128)(2,1)S(1)} %get-tuple-element.56), channel_id=1, source_target_pairs={{0,3},{1,2},{2,1},{3,0},{4,7},{5,6},{6,5},{7,4},{8,11},{9,10},{10,... | collective-permute-start | bytes 61448 | tf_op jit(solution)/shard_map/ppermute | solution.py:344
  24.4 6.3 %collective-permute-start.7 = (bf16[16,640]{1,0:T(8,128)(2,1)S(1)}, bf16[16,640]{1,0:T(8,128)(2,1)S(1)}, u32[]{:S(2)}, u32[]{:S(2)}) collective-permute-start(bf16[16,640]{1,0:T(8,128)(2,1)S(1)} %get-tuple-element.57), channel_id=1, source_target_pairs={{0,2},{1,3},{2,0},{3,1},{4,6},{5,7},{6,4},{7,5},{8,10},{9,11},{10,... | collective-permute-start | bytes 61448 | tf_op jit(solution)/shard_map/ppermute | solution.py:344
  25.7 4.9 %collective-permute-start.8 = (bf16[16,640]{1,0:T(8,128)(2,1)S(1)}, bf16[16,640]{1,0:T(8,128)(2,1)S(1)}, u32[]{:S(2)}, u32[]{:S(2)}) collective-permute-start(bf16[16,640]{1,0:T(8,128)(2,1)S(1)} %get-tuple-element.58), channel_id=1, source_target_pairs={{0,1},{1,0},{2,3},{3,2},{4,5},{5,4},{6,7},{7,6},{8,9},{9,8},{10,11... | collective-permute-start | bytes 61448 | tf_op jit(solution)/shard_map/ppermute | solution.py:344

commit v7 on v6

--- a/solution.py
+++ b/solution.py
@@ -434,7 +434,8 @@
         + [shape((slots, cols + 128), BF16)] * tp_count,
         cost=SLOT_COST,
     )
-    messages = [swap(messages[k], "tp", k) for k in range(tp_count - 1, 0, -1)] + [messages[0]]
+    farthest_first = [tp_count - 1] + list(range(1, tp_count - 1))
+    messages = [swap(messages[k], "tp", k) for k in farthest_first] + [messages[0]]
 
     scaled_grad, stream = call(
         grad_kernel,

time: 33 us -> 33 us (level)
  no operation moved by 1% of the time
where the time goes in v7:
time: 33 us; the launch traced here: 32.9 us
  starting transfers between devices  15.7 us (48%)
  Pallas kernels  14.8 us (45%)
  waiting for transfers between devices  1.54 us (5%)
  between operations  0.78 us (2%)
    ppermute x11, starting transfers between devices, swap(): lax.ppermute(array, axis, [(i, i ^ k) for i in range(lax.axis_size(axis))])  15.5 us
    pallas_call x8, Pallas kernels, call(): pl.pallas_call(kernel, out_shape=outs, in_specs=in_specs, out_specs=out_s...  14.8 us
    ppermute x11, waiting for transfers between devices, swap(): lax.ppermute(array, axis, [(i, i ^ k) for i in range(lax.axis_size(axis))])  1.54 us
  transfers between devices with their start and end apart: 12, of which 2 were waited for; matrix products, arithmetic and copies ran while one was open for 0% of the time, Pallas kernels for 31%

profile of v7, /device:TPU:0, one launch (start us, length us, event | category | flops | bytes accessed | tf_op | source)
XLA Modules:
  0.0 32.9 jit_solution(2558294576812534236)
XLA Ops:
  0.7 0.0 slice-start
  0.7 2.5 %first_text_kv.1 = (bf16[256,512]{1,0:T(8,128)(2,1)S(1)}, bf16[256,2048]{1,0:T(8,128)(2,1)S(1)}, bf16[256,2048]{1,0:T(8,128)(2,1)S(1)}, s32[1,256]{1,0:T(1,128)S(1)}, s32[4,4]{1,0:T(4,128)S(1)}) custom-call(bf16[256,2048]{1,0:T(8,128)(2,1)} %refs_0_.1, f32[1,2048]{1,0:T(1,128)} %bitcast.8, bf16[2048,2048]{1,0:T(8,128)(2,1)} %weight, s32[1,256]{1,0:T(1,128)} %bitcast.13, ...), custom_call_target="tpu_custom_call" | custom-call | flops 1024 | bytes 1024 | tf_op jit(solution)/shard_map/first_text_kv/pallas_call | solution.py:327
  3.2 0.5 %collective-permute-start = (s32[1,256]{1,0:T(1,128)S(1)}, s32[1,256]{1,0:T(1,128)S(1)}, u32[]{:S(2)}, u32[]{:S(2)}) collective-permute-start(s32[1,256]{1,0:T(1,128)S(1)} %get-tuple-element.34.refs_1_), channel_id=1, source_target_pairs={{0,4},{4,0},{1,5},{5,1},{2,6},{6,2},{3,7},{7,3},{8,12},{12,8},{9,1... | collective-permute-start | bytes 3080 | tf_op jit(solution)/shard_map/ppermute | solution.py:344
  3.7 2.6 %collective-permute-start.9 = (bf16[256,512]{1,0:T(8,128)(2,1)S(1)}, bf16[256,512]{1,0:T(8,128)(2,1)S(1)}, u32[]{:S(2)}, u32[]{:S(2)}) collective-permute-start(bf16[256,512]{1,0:T(8,128)(2,1)S(1)} %get-tuple-element.48.refs_4_), channel_id=1, source_target_pairs={{0,1},{1,0},{2,3},{3,2},{4,5},{5,4},{6,7},{7,6},{8,9},{9,8},{10,11... | collective-permute-start | bytes 786440 | tf_op jit(solution)/shard_map/ppermute | solution.py:344
  6.4 0.2 collective-permute-start.5
  6.6 0.0 slice-start.1
  6.6 0.0 slice-start.2
  6.6 0.0 slice-start.3
  6.6 1.1 %gather_rows.1 = (bf16[16,1792]{1,0:T(8,128)(2,1)S(1)}, bf16[16,1792]{1,0:T(8,128)(2,1)S(1)}, bf16[16,1792]{1,0:T(8,128)(2,1)S(1)}, bf16[16,1792]{1,0:T(8,128)(2...) custom-call(s32[1,256]{1,0:T(1,128)S(1)} %collective-permute-done.refs_0_, ...), custom_call_target="tpu_custom_call" | custom-call | flops 4000000000 | bytes 1024 | tf_op jit(solution)/shard_map/gather_rows/pallas_call | solution.py:327
  7.7 1.6 %collective-permute-start.1 = (bf16[16,1792]{1,0:T(8,128)(2,1)S(1)}, bf16[16,1792]{1,0:T(8,128)(2,1)S(1)}, u32[]{:S(2)}, u32[]{:S(2)}) collective-permute-start(bf16[16,1792]{1,0:T(8,128)(2,1)S(1)} %get-tuple-element.37.refs_1_), channel_id=1, source_target_pairs={{0,8},{8,0},{16,24},{24,16},{1,9},{9,1},{17,25},{25,17},{2,10},{10... | collective-permute-start | bytes 172040 | tf_op jit(solution)/shard_map/ppermute | solution.py:344
  9.2 1.5 %collective-permute-start.2 = (bf16[16,1792]{1,0:T(8,128)(2,1)S(1)}, bf16[16,1792]{1,0:T(8,128)(2,1)S(1)}, u32[]{:S(2)}, u32[]{:S(2)}) collective-permute-start(bf16[16,1792]{1,0:T(8,128)(2,1)S(1)} %get-tuple-element.38.refs_2_), channel_id=1, source_target_pairs={{0,16},{8,24},{16,0},{24,8},{1,17},{9,25},{17,1},{25,9},{2,18},{10... | collective-permute-start | bytes 172040 | tf_op jit(solution)/shard_map/ppermute | solution.py:344
  10.7 0.5 %collective-permute-start.3 = (bf16[16,1792]{1,0:T(8,128)(2,1)S(1)}, bf16[16,1792]{1,0:T(8,128)(2,1)S(1)}, u32[]{:S(2)}, u32[]{:S(2)}) collective-permute-start(bf16[16,1792]{1,0:T(8,128)(2,1)S(1)} %get-tuple-element.39.refs_3_), channel_id=1, source_target_pairs={{0,24},{8,16},{16,8},{24,0},{1,25},{9,17},{17,9},{25,1},{2,26},{10... | collective-permute-start | bytes 172040 | tf_op jit(solution)/shard_map/ppermute | solution.py:344
  11.2 2.1 %text_kv.1 = (bf16[256,512]{1,0:T(8,128)(2,1)S(1)}, bf16[256,512]{1,0:T(8,128)(2,1)S(1)}, f32[256,512]{1,0:T(8,128)S(1)}, f32[8,256]{1,0:T(8,128)S(1)}) custom-call(bf16[256,2048]{1,0:T(8,128)(2,1)S(1)} %get-tuple-element.46.refs_0_, bf16[2048,2048]{1,0:T(8,128)(2,1)S(1)} %bitcast.5, bf16[256,2048]{1,0:T(8,128)(2,1)S(1)} %copy-done, ...), custom_call_target="tpu_custom_call" | custom-call | flops 1024 | bytes 1024 | tf_op jit(solution)/shard_map/text_kv/pallas_call | solution.py:327
  13.4 0.1 forward.1
  13.5 2.7 %collective-permute-start.10 = (bf16[256,512]{1,0:T(8,128)(2,1)S(1)}, bf16[256,512]{1,0:T(8,128)(2,1)S(1)}, u32[]{:S(2)}, u32[]{:S(2)}) collective-permute-start(bf16[256,512]{1,0:T(8,128)(2,1)S(1)} %forward.1), channel_id=1, source_target_pairs={{0,2},{1,3},{2,0},{3,1},{4,6},{5,7},{6,4},{7,5},{8,10},{9,11},{10,... | collective-permute-start | bytes 786440 | tf_op jit(solution)/shard_map/ppermute | solution.py:344
  16.2 0.0 collective-permute-done.1.refs_4_
  16.2 1.6 %collective-permute-start.11 = (bf16[256,512]{1,0:T(8,128)(2,1)S(1)}, bf16[256,512]{1,0:T(8,128)(2,1)S(1)}, u32[]{:S(2)}, u32[]{:S(2)}) collective-permute-start(bf16[256,512]{1,0:T(8,128)(2,1)S(1)} %get-tuple-element.64), channel_id=1, source_target_pairs={{0,1},{1,0},{2,3},{3,2},{4,5},{5,4},{6,7},{7,6},{8,9},{9,8},{10,11... | collective-permute-start | bytes 786440 | tf_op jit(solution)/shard_map/ppermute | solution.py:344
  17.8 2.1 %merge_rows.1 = (f32[32,2048]{1,0:T(8,128)S(1)}, bf16[32,2048]{1,0:T(8,128)(2,1)S(1)}, bf16[32,2048]{1,0:T(8,128)(2,1)S(1)}) custom-call(bf16[16,1792]{1,0:T(8,128)(2,1)S(1)} %get-tuple-element.36.refs_0_, bf16[16,1792]{1,0:T(8,128)(2,1)S(1)} %get-tuple-element.37.refs_1_, bf16[16,1792]{1,0:T(8,128)(2,1)S(1)} %get-tuple-element.38.refs_2_, ...), custom_call_target="tpu_custom_call" | custom-call | flops 1024 | bytes 1024 | tf_op jit(solution)/shard_map/merge_rows/pallas_call | solution.py:327
  20.0 0.1 collective-permute-start.4
  20.0 1.3 %collective-permute-done.4.refs_1_ = bf16[32,2048]{1,0:T(8,128)(2,1)S(1)} collective-permute-done((bf16[32,2048]{1,0:T(8,128)(2,1)S(1)}, bf16[32,2048]{1,0:T(8,128)(2,1)S(1)}, u32[]{:S(2)}, u32[]{:S(2)}) %collective-permute-start.4) | collective-permute-done | bytes 131104 | tf_op jit(solution)/shard_map/ppermute | solution.py:344
  21.4 0.0 collective-permute-done.5.refs_8_
  21.4 1.8 %slot_kv.1 = (bf16[32,2048]{1,0:T(8,128)(2,1)S(1)}, f32[256,512]{1,0:T(8,128)S(1)}, bf16[16,640]{1,0:T(8,128)(2,1)S(1)}, bf16[16,640]{1,0:T(8,128)(2,1)S(1)}, bf...) custom-call(f32[32,2048]{1,0:T(8,128)S(1)} %get-tuple-element.42.refs_0_, ...), custom_call_target="tpu_custom_call" | custom-call | flops 1024 | bytes 1024 | tf_op jit(solution)/shard_map/slot_kv/pallas_call | solution.py:327
  23.2 1.1 %collective-permute-start.6 = (bf16[16,640]{1,0:T(8,128)(2,1)S(1)}, bf16[16,640]{1,0:T(8,128)(2,1)S(1)}, u32[]{:S(2)}, u32[]{:S(2)}) collective-permute-start(bf16[16,640]{1,0:T(8,128)(2,1)S(1)} %get-tuple-element.56), channel_id=1, source_target_pairs={{0,3},{1,2},{2,1},{3,0},{4,7},{5,6},{6,5},{7,4},{8,11},{9,10},{10,... | collective-permute-start | bytes 61448 | tf_op jit(solution)/shard_map/ppermute | solution.py:344
  24.4 1.1 %collective-permute-start.7 = (bf16[16,640]{1,0:T(8,128)(2,1)S(1)}, bf16[16,640]{1,0:T(8,128)(2,1)S(1)}, u32[]{:S(2)}, u32[]{:S(2)}) collective-permute-start(bf16[16,640]{1,0:T(8,128)(2,1)S(1)} %get-tuple-element.57), channel_id=1, source_target_pairs={{0,1},{1,0},{2,3},{3,2},{4,5},{5,4},{6,7},{7,6},{8,9},{9,8},{10,11... | collective-permute-start | bytes 61448 | tf_op jit(solution)/shard_map/ppermute | solution.py:344
  25.5 2.2 %collective-permute-start.8 = (bf16[16,640]{1,0:T(8,128)(2,1)S(1)}, bf16[16,640]{1,0:T(8,128)(2,1)S(1)}, u32[]{:S(2)}, u32[]{:S(2)}) collective-permute-start(bf16[16,640]{1,0:T(8,128)(2,1)S(1)} %get-tuple-element.58), channel_id=1, source_target_pairs={{0,2},{1,3},{2,0},{3,1},{4,6},{5,7},{6,4},{7,5},{8,10},{9,11},{10,... | collective-permute-start | bytes 61448 | tf_op jit(solution)/shard_map/ppermute | solution.py:344
  27.6 2.8 %normed_grad.1 = (f32[272,2048]{1,0:T(8,128)S(1)}, bf16[256,2048]{1,0:T(8,128)(2,1)S(1)}) custom-call(bf16[256,2048]{1,0:T(8,128)(2,1)S(1)} %copy-done, bf16[32,2048]{1,0:T(8,128)(2,1)S(1)} %get-tuple-element.45.refs_5_.grad_rows, bf16[2048,2048]{1,0:T(8,128)(2,1)S(1)} %bitcast.5, f32[1,2048]{1,0:T(1,128)S(1)} %bitcast.10, ...), custom_call_target="tpu_custom_call" | custom-call | flops 1000000000 | bytes 1024 | tf_op jit(solution)/shard_map/normed_grad/pallas_call | solution.py:327
  30.5 0.2 collective-permute-done.6.refs_5_
  30.6 0.0 collective-permute-done.7.refs_6_
  30.6 0.0 collective-permute-done.8.refs_7_
  30.6 0.0 collective-permute-done.10.refs_10_
  30.7 0.0 collective-permute-done.11.refs_11_
  30.7 2.2 %outputs.1 = (bf16[256,512]{1,0:T(8,128)(2,1)}, bf16[256,2048]{1,0:T(8,128)(2,1)}, bf16[256,2048]{1,0:T(8,128)(2,1)}) custom-call(bf16[32,2048]{1,0:T(8,128)(2,1)S(1)} %get-tuple-element.51.rows.refs_0_, f32[272,2048]{1,0:T(8,128)S(1)} %get-tuple-element.53.refs_1_, bf16[256,2048]{1,0:T(8,128)(2,1)S(1)} %get-tuple-element.54.refs_2_, ...), custom_call_target="tpu_custom_call" | custom-call | flops 1024 | bytes 1024 | tf_op jit(solution)/shard_map/outputs/pallas_call | solution.py:327
  (20 shorter events, 0.0 us)
Async XLA Ops:
  0.6 5.9 %copy-start = (bf16[256,2048]{1,0:T(8,128)(2,1)S(1)}, bf16[256,2048]{1,0:T(8,128)(2,1)}, u32[]{:S(2)}) copy-start(bf16[256,2048]{1,0:T(8,128)(2,1)} %grad.1) | copy-start | bytes 3145732
  0.6 5.9 %copy-start.3 = (bf16[512,2560]{1,0:T(8,128)(2,1)S(1)}, bf16[512,2560]{1,0:T(8,128)(2,1)}, u32[]{:S(2)}) copy-start(bf16[512,2560]{1,0:T(8,128)(2,1)} %refs_4_.1) | copy-start | bytes 7864324
  0.7 10.6 %slice-start = ((s8[8388608]{0:T(1024)(128)(4,1)}), s8[4194304]{0:T(1024)(128)(4,1)S(1)}, s32[]{:S(2)}) async-start(s8[8388608]{0:T(1024)(128)(4,1)} %bitcast.4), calls=%async_computation | async-start | bytes 8388608
  3.2 3.3 %collective-permute-start = (s32[1,256]{1,0:T(1,128)S(1)}, s32[1,256]{1,0:T(1,128)S(1)}, u32[]{:S(2)}, u32[]{:S(2)}) collective-permute-start(s32[1,256]{1,0:T(1,128)S(1)} %get-tuple-element.34.refs_1_), channel_id=1, source_target_pairs={{0,4},{4,0},{1,5},{5,1},{2,6},{6,2},{3,7},{7,3},{8,12},{12,8},{9,1... | collective-permute-start | bytes 3080 | tf_op jit(solution)/shard_map/ppermute | solution.py:344
  3.7 9.7 %collective-permute-start.9 = (bf16[256,512]{1,0:T(8,128)(2,1)S(1)}, bf16[256,512]{1,0:T(8,128)(2,1)S(1)}, u32[]{:S(2)}, u32[]{:S(2)}) collective-permute-start(bf16[256,512]{1,0:T(8,128)(2,1)S(1)} %get-tuple-element.48.refs_4_), channel_id=1, source_target_pairs={{0,1},{1,0},{2,3},{3,2},{4,5},{5,4},{6,7},{7,6},{8,9},{9,8},{10,11... | collective-permute-start | bytes 786440 | tf_op jit(solution)/shard_map/ppermute | solution.py:344
  6.4 15.0 %collective-permute-start.5 = (bf16[256,512]{1,0:T(8,128)(2,1)S(1)}, bf16[256,512]{1,0:T(8,128)(2,1)S(1)}, u32[]{:S(2)}, u32[]{:S(2)}) collective-permute-start(bf16[256,512]{1,0:T(8,128)(2,1)S(1)} %get-tuple-element.48.refs_4_), channel_id=1, source_target_pairs={{0,4},{1,2},{2,1},{3,7},{4,0},{5,6},{6,5},{7,3},{8,12},{9,10},{10,... | collective-permute-start | bytes 786440 | tf_op jit(solution)/shard_map/ppermute | solution.py:387
  6.6 4.7 %slice-start.1 = ((s8[8388608]{0:T(1024)(128)(4,1)}), s8[4194304]{0:T(1024)(128)(4,1)S(1)}, s32[]{:S(2)}) async-start(s8[8388608]{0:T(1024)(128)(4,1)} %bitcast.4), calls=%async_computation.1 | async-start | bytes 8388608
  6.6 11.2 %slice-start.2 = ((s8[10485760]{0:T(1024)(128)(4,1)}), s8[4194304]{0:T(1024)(128)(4,1)S(1)}, s32[]{:S(2)}) async-start(s8[10485760]{0:T(1024)(128)(4,1)} %bitcast.6), calls=%async_computation.2 | async-start | bytes 8388608
  6.6 11.2 %slice-start.3 = ((s8[10485760]{0:T(1024)(128)(4,1)}), s8[4194304]{0:T(1024)(128)(4,1)S(1)}, s32[]{:S(2)}) async-start(s8[10485760]{0:T(1024)(128)(4,1)} %bitcast.6), calls=%async_computation.3 | async-start | bytes 8388608
  7.7 8.5 %collective-permute-start.1 = (bf16[16,1792]{1,0:T(8,128)(2,1)S(1)}, bf16[16,1792]{1,0:T(8,128)(2,1)S(1)}, u32[]{:S(2)}, u32[]{:S(2)}) collective-permute-start(bf16[16,1792]{1,0:T(8,128)(2,1)S(1)} %get-tuple-element.37.refs_1_), channel_id=1, source_target_pairs={{0,8},{8,0},{16,24},{24,16},{1,9},{9,1},{17,25},{25,17},{2,10},{10... | collective-permute-start | bytes 172040 | tf_op jit(solution)/shard_map/ppermute | solution.py:344
  9.2 8.6 %collective-permute-start.2 = (bf16[16,1792]{1,0:T(8,128)(2,1)S(1)}, bf16[16,1792]{1,0:T(8,128)(2,1)S(1)}, u32[]{:S(2)}, u32[]{:S(2)}) collective-permute-start(bf16[16,1792]{1,0:T(8,128)(2,1)S(1)} %get-tuple-element.38.refs_2_), channel_id=1, source_target_pairs={{0,16},{8,24},{16,0},{24,8},{1,17},{9,25},{17,1},{25,9},{2,18},{10... | collective-permute-start | bytes 172040 | tf_op jit(solution)/shard_map/ppermute | solution.py:344
  10.7 7.0 %collective-permute-start.3 = (bf16[16,1792]{1,0:T(8,128)(2,1)S(1)}, bf16[16,1792]{1,0:T(8,128)(2,1)S(1)}, u32[]{:S(2)}, u32[]{:S(2)}) collective-permute-start(bf16[16,1792]{1,0:T(8,128)(2,1)S(1)} %get-tuple-element.39.refs_3_), channel_id=1, source_target_pairs={{0,24},{8,16},{16,8},{24,0},{1,25},{9,17},{17,9},{25,1},{2,26},{10... | collective-permute-start | bytes 172040 | tf_op jit(solution)/shard_map/ppermute | solution.py:344
  11.2 6.6 %slice-start.4 = ((s8[10485760]{0:T(1024)(128)(4,1)}), s8[2097152]{0:T(1024)(128)(4,1)S(1)}, s32[]{:S(2)}) async-start(s8[10485760]{0:T(1024)(128)(4,1)} %bitcast.6), calls=%async_computation.4 | async-start | bytes 4194304
  13.4 8.0 %copy-start.1 = (f32[2048]{0:T(1024)S(1)}, f32[2048]{0:T(1024)}, u32[]{:S(2)}) copy-start(f32[2048]{0:T(1024)} %param.15) | copy-start | bytes 24580
  13.4 8.0 %copy-start.2 = (f32[2048]{0:T(1024)S(1)}, f32[2048]{0:T(1024)}, u32[]{:S(2)}) copy-start(f32[2048]{0:T(1024)} %param.11) | copy-start | bytes 24580
  13.5 17.2 %collective-permute-start.10 = (bf16[256,512]{1,0:T(8,128)(2,1)S(1)}, bf16[256,512]{1,0:T(8,128)(2,1)S(1)}, u32[]{:S(2)}, u32[]{:S(2)}) collective-permute-start(bf16[256,512]{1,0:T(8,128)(2,1)S(1)} %forward.1), channel_id=1, source_target_pairs={{0,2},{1,3},{2,0},{3,1},{4,6},{5,7},{6,4},{7,5},{8,10},{9,11},{10,... | collective-permute-start | bytes 786440 | tf_op jit(solution)/shard_map/ppermute | solution.py:344
  16.2 14.5 %collective-permute-start.11 = (bf16[256,512]{1,0:T(8,128)(2,1)S(1)}, bf16[256,512]{1,0:T(8,128)(2,1)S(1)}, u32[]{:S(2)}, u32[]{:S(2)}) collective-permute-start(bf16[256,512]{1,0:T(8,128)(2,1)S(1)} %get-tuple-element.64), channel_id=1, source_target_pairs={{0,1},{1,0},{2,3},{3,2},{4,5},{5,4},{6,7},{7,6},{8,9},{9,8},{10,11... | collective-permute-start | bytes 786440 | tf_op jit(solution)/shard_map/ppermute | solution.py:344
  20.0 1.4 %collective-permute-start.4 = (bf16[32,2048]{1,0:T(8,128)(2,1)S(1)}, bf16[32,2048]{1,0:T(8,128)(2,1)S(1)}, u32[]{:S(2)}, u32[]{:S(2)}) collective-permute-start(bf16[32,2048]{1,0:T(8,128)(2,1)S(1)} %get-tuple-element.43), channel_id=1, source_target_pairs={{0,4},{4,0},{1,5},{5,1},{2,6},{6,2},{3,7},{7,3},{8,12},{12,8},{9,1... | collective-permute-start | bytes 393224 | tf_op jit(solution)/shard_map/ppermute | solution.py:344
  23.2 7.4 %collective-permute-start.6 = (bf16[16,640]{1,0:T(8,128)(2,1)S(1)}, bf16[16,640]{1,0:T(8,128)(2,1)S(1)}, u32[]{:S(2)}, u32[]{:S(2)}) collective-permute-start(bf16[16,640]{1,0:T(8,128)(2,1)S(1)} %get-tuple-element.56), channel_id=1, source_target_pairs={{0,3},{1,2},{2,1},{3,0},{4,7},{5,6},{6,5},{7,4},{8,11},{9,10},{10,... | collective-permute-start | bytes 61448 | tf_op jit(solution)/shard_map/ppermute | solution.py:344
  24.4 6.3 %collective-permute-start.7 = (bf16[16,640]{1,0:T(8,128)(2,1)S(1)}, bf16[16,640]{1,0:T(8,128)(2,1)S(1)}, u32[]{:S(2)}, u32[]{:S(2)}) collective-permute-start(bf16[16,640]{1,0:T(8,128)(2,1)S(1)} %get-tuple-element.57), channel_id=1, source_target_pairs={{0,1},{1,0},{2,3},{3,2},{4,5},{5,4},{6,7},{7,6},{8,9},{9,8},{10,11... | collective-permute-start | bytes 61448 | tf_op jit(solution)/shard_map/ppermute | solution.py:344
  25.5 5.2 %collective-permute-start.8 = (bf16[16,640]{1,0:T(8,128)(2,1)S(1)}, bf16[16,640]{1,0:T(8,128)(2,1)S(1)}, u32[]{:S(2)}, u32[]{:S(2)}) collective-permute-start(bf16[16,640]{1,0:T(8,128)(2,1)S(1)} %get-tuple-element.58), channel_id=1, source_target_pairs={{0,2},{1,3},{2,0},{3,1},{4,6},{5,7},{6,4},{7,5},{8,10},{9,11},{10,... | collective-permute-start | bytes 61448 | tf_op jit(solution)/shard_map/ppermute | solution.py:344

commit v8 on v7

--- a/solution.py
+++ b/solution.py
@@ -67,7 +67,7 @@
             pltpu.make_async_copy(text_hbm.at[:, cut], text.at[:, cut], sem.at[2 * i + 1]),
             pltpu.make_async_copy(weight_hbm.at[cut, span], weight.at[cut], sem.at[2 * i + 2]),
         )
-        for copy in pair:
+        for copy in pair[::-1]:
             copy.start()
         copies.append(pair)
         if i == 0:

time: 33 us -> 33 us (level)
  no operation moved by 1% of the time
where the time goes in v8:
time: 33 us; the launch traced here: 32.9 us
  starting transfers between devices  15.7 us (48%)
  Pallas kernels  14.9 us (45%)
  waiting for transfers between devices  1.54 us (5%)
  between operations  0.78 us (2%)
    ppermute x11, starting transfers between devices, swap(): lax.ppermute(array, axis, [(i, i ^ k) for i in range(lax.axis_size(axis))])  15.5 us
    pallas_call x8, Pallas kernels, call(): pl.pallas_call(kernel, out_shape=outs, in_specs=in_specs, out_specs=out_s...  14.9 us
    ppermute x11, waiting for transfers between devices, swap(): lax.ppermute(array, axis, [(i, i ^ k) for i in range(lax.axis_size(axis))])  1.54 us
  transfers between devices with their start and end apart: 12, of which 2 were waited for; matrix products, arithmetic and copies ran while one was open for 0% of the time, Pallas kernels for 31%

profile of v8, /device:TPU:0, one launch (start us, length us, event | category | flops | bytes accessed | tf_op | source)
XLA Modules:
  0.0 32.9 jit_solution(11240598719114440608)
XLA Ops:
  0.7 0.0 slice-start
  0.7 2.6 %first_text_kv.1 = (bf16[256,512]{1,0:T(8,128)(2,1)S(1)}, bf16[256,2048]{1,0:T(8,128)(2,1)S(1)}, bf16[256,2048]{1,0:T(8,128)(2,1)S(1)}, s32[1,256]{1,0:T(1,128)S(1)}, s32[4,4]{1,0:T(4,128)S(1)}) custom-call(bf16[256,2048]{1,0:T(8,128)(2,1)} %refs_0_.1, f32[1,2048]{1,0:T(1,128)} %bitcast.8, bf16[2048,2048]{1,0:T(8,128)(2,1)} %weight, s32[1,256]{1,0:T(1,128)} %bitcast.13, ...), custom_call_target="tpu_custom_call" | custom-call | flops 1024 | bytes 1024 | tf_op jit(solution)/shard_map/first_text_kv/pallas_call | solution.py:327
  3.3 0.5 %collective-permute-start = (s32[1,256]{1,0:T(1,128)S(1)}, s32[1,256]{1,0:T(1,128)S(1)}, u32[]{:S(2)}, u32[]{:S(2)}) collective-permute-start(s32[1,256]{1,0:T(1,128)S(1)} %get-tuple-element.34.refs_1_), channel_id=1, source_target_pairs={{0,4},{4,0},{1,5},{5,1},{2,6},{6,2},{3,7},{7,3},{8,12},{12,8},{9,1... | collective-permute-start | bytes 3080 | tf_op jit(solution)/shard_map/ppermute | solution.py:344
  3.8 2.6 %collective-permute-start.9 = (bf16[256,512]{1,0:T(8,128)(2,1)S(1)}, bf16[256,512]{1,0:T(8,128)(2,1)S(1)}, u32[]{:S(2)}, u32[]{:S(2)}) collective-permute-start(bf16[256,512]{1,0:T(8,128)(2,1)S(1)} %get-tuple-element.48.refs_4_), channel_id=1, source_target_pairs={{0,1},{1,0},{2,3},{3,2},{4,5},{5,4},{6,7},{7,6},{8,9},{9,8},{10,11... | collective-permute-start | bytes 786440 | tf_op jit(solution)/shard_map/ppermute | solution.py:344
  6.4 0.2 collective-permute-start.5
  6.6 0.0 slice-start.1
  6.6 0.0 slice-start.2
  6.6 0.0 slice-start.3
  6.6 1.1 %gather_rows.1 = (bf16[16,1792]{1,0:T(8,128)(2,1)S(1)}, bf16[16,1792]{1,0:T(8,128)(2,1)S(1)}, bf16[16,1792]{1,0:T(8,128)(2,1)S(1)}, bf16[16,1792]{1,0:T(8,128)(2...) custom-call(s32[1,256]{1,0:T(1,128)S(1)} %collective-permute-done.refs_0_, ...), custom_call_target="tpu_custom_call" | custom-call | flops 4000000000 | bytes 1024 | tf_op jit(solution)/shard_map/gather_rows/pallas_call | solution.py:327
  7.7 1.5 %collective-permute-start.1 = (bf16[16,1792]{1,0:T(8,128)(2,1)S(1)}, bf16[16,1792]{1,0:T(8,128)(2,1)S(1)}, u32[]{:S(2)}, u32[]{:S(2)}) collective-permute-start(bf16[16,1792]{1,0:T(8,128)(2,1)S(1)} %get-tuple-element.37.refs_1_), channel_id=1, source_target_pairs={{0,8},{8,0},{16,24},{24,16},{1,9},{9,1},{17,25},{25,17},{2,10},{10... | collective-permute-start | bytes 172040 | tf_op jit(solution)/shard_map/ppermute | solution.py:344
  9.3 1.5 %collective-permute-start.2 = (bf16[16,1792]{1,0:T(8,128)(2,1)S(1)}, bf16[16,1792]{1,0:T(8,128)(2,1)S(1)}, u32[]{:S(2)}, u32[]{:S(2)}) collective-permute-start(bf16[16,1792]{1,0:T(8,128)(2,1)S(1)} %get-tuple-element.38.refs_2_), channel_id=1, source_target_pairs={{0,16},{8,24},{16,0},{24,8},{1,17},{9,25},{17,1},{25,9},{2,18},{10... | collective-permute-start | bytes 172040 | tf_op jit(solution)/shard_map/ppermute | solution.py:344
  10.8 0.5 %collective-permute-start.3 = (bf16[16,1792]{1,0:T(8,128)(2,1)S(1)}, bf16[16,1792]{1,0:T(8,128)(2,1)S(1)}, u32[]{:S(2)}, u32[]{:S(2)}) collective-permute-start(bf16[16,1792]{1,0:T(8,128)(2,1)S(1)} %get-tuple-element.39.refs_3_), channel_id=1, source_target_pairs={{0,24},{8,16},{16,8},{24,0},{1,25},{9,17},{17,9},{25,1},{2,26},{10... | collective-permute-start | bytes 172040 | tf_op jit(solution)/shard_map/ppermute | solution.py:344
  11.3 2.1 %text_kv.1 = (bf16[256,512]{1,0:T(8,128)(2,1)S(1)}, bf16[256,512]{1,0:T(8,128)(2,1)S(1)}, f32[256,512]{1,0:T(8,128)S(1)}, f32[8,256]{1,0:T(8,128)S(1)}) custom-call(bf16[256,2048]{1,0:T(8,128)(2,1)S(1)} %get-tuple-element.46.refs_0_, bf16[2048,2048]{1,0:T(8,128)(2,1)S(1)} %bitcast.5, bf16[256,2048]{1,0:T(8,128)(2,1)S(1)} %copy-done, ...), custom_call_target="tpu_custom_call" | custom-call | flops 1024 | bytes 1024 | tf_op jit(solution)/shard_map/text_kv/pallas_call | solution.py:327
  13.4 0.0 collective-permute-done.9.turned
  13.4 0.1 forward.1
  13.5 2.7 %collective-permute-start.10 = (bf16[256,512]{1,0:T(8,128)(2,1)S(1)}, bf16[256,512]{1,0:T(8,128)(2,1)S(1)}, u32[]{:S(2)}, u32[]{:S(2)}) collective-permute-start(bf16[256,512]{1,0:T(8,128)(2,1)S(1)} %forward.1), channel_id=1, source_target_pairs={{0,2},{1,3},{2,0},{3,1},{4,6},{5,7},{6,4},{7,5},{8,10},{9,11},{10,... | collective-permute-start | bytes 786440 | tf_op jit(solution)/shard_map/ppermute | solution.py:344
  16.2 0.0 collective-permute-done.1.refs_4_
  16.2 1.6 %collective-permute-start.11 = (bf16[256,512]{1,0:T(8,128)(2,1)S(1)}, bf16[256,512]{1,0:T(8,128)(2,1)S(1)}, u32[]{:S(2)}, u32[]{:S(2)}) collective-permute-start(bf16[256,512]{1,0:T(8,128)(2,1)S(1)} %get-tuple-element.64), channel_id=1, source_target_pairs={{0,1},{1,0},{2,3},{3,2},{4,5},{5,4},{6,7},{7,6},{8,9},{9,8},{10,11... | collective-permute-start | bytes 786440 | tf_op jit(solution)/shard_map/ppermute | solution.py:344
  17.8 0.0 collective-permute-done.2.refs_5_
  17.8 0.0 collective-permute-done.3.refs_6_
  17.9 2.1 %merge_rows.1 = (f32[32,2048]{1,0:T(8,128)S(1)}, bf16[32,2048]{1,0:T(8,128)(2,1)S(1)}, bf16[32,2048]{1,0:T(8,128)(2,1)S(1)}) custom-call(bf16[16,1792]{1,0:T(8,128)(2,1)S(1)} %get-tuple-element.36.refs_0_, bf16[16,1792]{1,0:T(8,128)(2,1)S(1)} %get-tuple-element.37.refs_1_, bf16[16,1792]{1,0:T(8,128)(2,1)S(1)} %get-tuple-element.38.refs_2_, ...), custom_call_target="tpu_custom_call" | custom-call | flops 1024 | bytes 1024 | tf_op jit(solution)/shard_map/merge_rows/pallas_call | solution.py:327
  20.0 0.1 collective-permute-start.4
  20.1 1.3 %collective-permute-done.4.refs_1_ = bf16[32,2048]{1,0:T(8,128)(2,1)S(1)} collective-permute-done((bf16[32,2048]{1,0:T(8,128)(2,1)S(1)}, bf16[32,2048]{1,0:T(8,128)(2,1)S(1)}, u32[]{:S(2)}, u32[]{:S(2)}) %collective-permute-start.4) | collective-permute-done | bytes 131104 | tf_op jit(solution)/shard_map/ppermute | solution.py:344
  21.4 0.0 collective-permute-done.5.refs_8_
  21.4 1.8 %slot_kv.1 = (bf16[32,2048]{1,0:T(8,128)(2,1)S(1)}, f32[256,512]{1,0:T(8,128)S(1)}, bf16[16,640]{1,0:T(8,128)(2,1)S(1)}, bf16[16,640]{1,0:T(8,128)(2,1)S(1)}, bf...) custom-call(f32[32,2048]{1,0:T(8,128)S(1)} %get-tuple-element.42.refs_0_, ...), custom_call_target="tpu_custom_call" | custom-call | flops 1024 | bytes 1024 | tf_op jit(solution)/shard_map/slot_kv/pallas_call | solution.py:327
  23.3 1.1 %collective-permute-start.6 = (bf16[16,640]{1,0:T(8,128)(2,1)S(1)}, bf16[16,640]{1,0:T(8,128)(2,1)S(1)}, u32[]{:S(2)}, u32[]{:S(2)}) collective-permute-start(bf16[16,640]{1,0:T(8,128)(2,1)S(1)} %get-tuple-element.56), channel_id=1, source_target_pairs={{0,3},{1,2},{2,1},{3,0},{4,7},{5,6},{6,5},{7,4},{8,11},{9,10},{10,... | collective-permute-start | bytes 61448 | tf_op jit(solution)/shard_map/ppermute | solution.py:344
  24.4 1.1 %collective-permute-start.7 = (bf16[16,640]{1,0:T(8,128)(2,1)S(1)}, bf16[16,640]{1,0:T(8,128)(2,1)S(1)}, u32[]{:S(2)}, u32[]{:S(2)}) collective-permute-start(bf16[16,640]{1,0:T(8,128)(2,1)S(1)} %get-tuple-element.57), channel_id=1, source_target_pairs={{0,1},{1,0},{2,3},{3,2},{4,5},{5,4},{6,7},{7,6},{8,9},{9,8},{10,11... | collective-permute-start | bytes 61448 | tf_op jit(solution)/shard_map/ppermute | solution.py:344
  25.5 2.2 %collective-permute-start.8 = (bf16[16,640]{1,0:T(8,128)(2,1)S(1)}, bf16[16,640]{1,0:T(8,128)(2,1)S(1)}, u32[]{:S(2)}, u32[]{:S(2)}) collective-permute-start(bf16[16,640]{1,0:T(8,128)(2,1)S(1)} %get-tuple-element.58), channel_id=1, source_target_pairs={{0,2},{1,3},{2,0},{3,1},{4,6},{5,7},{6,4},{7,5},{8,10},{9,11},{10,... | collective-permute-start | bytes 61448 | tf_op jit(solution)/shard_map/ppermute | solution.py:344
  27.7 2.8 %normed_grad.1 = (f32[272,2048]{1,0:T(8,128)S(1)}, bf16[256,2048]{1,0:T(8,128)(2,1)S(1)}) custom-call(bf16[256,2048]{1,0:T(8,128)(2,1)S(1)} %copy-done, bf16[32,2048]{1,0:T(8,128)(2,1)S(1)} %get-tuple-element.45.refs_5_.grad_rows, bf16[2048,2048]{1,0:T(8,128)(2,1)S(1)} %bitcast.5, f32[1,2048]{1,0:T(1,128)S(1)} %bitcast.10, ...), custom_call_target="tpu_custom_call" | custom-call | flops 1000000000 | bytes 1024 | tf_op jit(solution)/shard_map/normed_grad/pallas_call | solution.py:327
  30.5 0.2 collective-permute-done.6.refs_5_
  30.7 0.0 collective-permute-done.7.refs_6_
  30.7 2.2 %outputs.1 = (bf16[256,512]{1,0:T(8,128)(2,1)}, bf16[256,2048]{1,0:T(8,128)(2,1)}, bf16[256,2048]{1,0:T(8,128)(2,1)}) custom-call(bf16[32,2048]{1,0:T(8,128)(2,1)S(1)} %get-tuple-element.51.rows.refs_0_, f32[272,2048]{1,0:T(8,128)S(1)} %get-tuple-element.53.refs_1_, bf16[256,2048]{1,0:T(8,128)(2,1)S(1)} %get-tuple-element.54.refs_2_, ...), custom_call_target="tpu_custom_call" | custom-call | flops 1024 | bytes 1024 | tf_op jit(solution)/shard_map/outputs/pallas_call | solution.py:327
  (20 shorter events, 0.0 us)
Async XLA Ops:
  0.6 6.0 %copy-start = (bf16[256,2048]{1,0:T(8,128)(2,1)S(1)}, bf16[256,2048]{1,0:T(8,128)(2,1)}, u32[]{:S(2)}) copy-start(bf16[256,2048]{1,0:T(8,128)(2,1)} %grad.1) | copy-start | bytes 3145732
  0.6 6.0 %copy-start.3 = (bf16[512,2560]{1,0:T(8,128)(2,1)S(1)}, bf16[512,2560]{1,0:T(8,128)(2,1)}, u32[]{:S(2)}) copy-start(bf16[512,2560]{1,0:T(8,128)(2,1)} %refs_4_.1) | copy-start | bytes 7864324
  0.7 10.6 %slice-start = ((s8[8388608]{0:T(1024)(128)(4,1)}), s8[4194304]{0:T(1024)(128)(4,1)S(1)}, s32[]{:S(2)}) async-start(s8[8388608]{0:T(1024)(128)(4,1)} %bitcast.4), calls=%async_computation | async-start | bytes 8388608
  3.3 3.3 %collective-permute-start = (s32[1,256]{1,0:T(1,128)S(1)}, s32[1,256]{1,0:T(1,128)S(1)}, u32[]{:S(2)}, u32[]{:S(2)}) collective-permute-start(s32[1,256]{1,0:T(1,128)S(1)} %get-tuple-element.34.refs_1_), channel_id=1, source_target_pairs={{0,4},{4,0},{1,5},{5,1},{2,6},{6,2},{3,7},{7,3},{8,12},{12,8},{9,1... | collective-permute-start | bytes 3080 | tf_op jit(solution)/shard_map/ppermute | solution.py:344
  3.8 9.7 %collective-permute-start.9 = (bf16[256,512]{1,0:T(8,128)(2,1)S(1)}, bf16[256,512]{1,0:T(8,128)(2,1)S(1)}, u32[]{:S(2)}, u32[]{:S(2)}) collective-permute-start(bf16[256,512]{1,0:T(8,128)(2,1)S(1)} %get-tuple-element.48.refs_4_), channel_id=1, source_target_pairs={{0,1},{1,0},{2,3},{3,2},{4,5},{5,4},{6,7},{7,6},{8,9},{9,8},{10,11... | collective-permute-start | bytes 786440 | tf_op jit(solution)/shard_map/ppermute | solution.py:344
  6.4 15.0 %collective-permute-start.5 = (bf16[256,512]{1,0:T(8,128)(2,1)S(1)}, bf16[256,512]{1,0:T(8,128)(2,1)S(1)}, u32[]{:S(2)}, u32[]{:S(2)}) collective-permute-start(bf16[256,512]{1,0:T(8,128)(2,1)S(1)} %get-tuple-element.48.refs_4_), channel_id=1, source_target_pairs={{0,4},{1,2},{2,1},{3,7},{4,0},{5,6},{6,5},{7,3},{8,12},{9,10},{10,... | collective-permute-start | bytes 786440 | tf_op jit(solution)/shard_map/ppermute | solution.py:387
  6.6 4.7 %slice-start.1 = ((s8[8388608]{0:T(1024)(128)(4,1)}), s8[4194304]{0:T(1024)(128)(4,1)S(1)}, s32[]{:S(2)}) async-start(s8[8388608]{0:T(1024)(128)(4,1)} %bitcast.4), calls=%async_computation.1 | async-start | bytes 8388608
  6.6 11.2 %slice-start.2 = ((s8[10485760]{0:T(1024)(128)(4,1)}), s8[4194304]{0:T(1024)(128)(4,1)S(1)}, s32[]{:S(2)}) async-start(s8[10485760]{0:T(1024)(128)(4,1)} %bitcast.6), calls=%async_computation.2 | async-start | bytes 8388608
  6.6 11.2 %slice-start.3 = ((s8[10485760]{0:T(1024)(128)(4,1)}), s8[4194304]{0:T(1024)(128)(4,1)S(1)}, s32[]{:S(2)}) async-start(s8[10485760]{0:T(1024)(128)(4,1)} %bitcast.6), calls=%async_computation.3 | async-start | bytes 8388608
  7.7 8.5 %collective-permute-start.1 = (bf16[16,1792]{1,0:T(8,128)(2,1)S(1)}, bf16[16,1792]{1,0:T(8,128)(2,1)S(1)}, u32[]{:S(2)}, u32[]{:S(2)}) collective-permute-start(bf16[16,1792]{1,0:T(8,128)(2,1)S(1)} %get-tuple-element.37.refs_1_), channel_id=1, source_target_pairs={{0,8},{8,0},{16,24},{24,16},{1,9},{9,1},{17,25},{25,17},{2,10},{10... | collective-permute-start | bytes 172040 | tf_op jit(solution)/shard_map/ppermute | solution.py:344
  9.3 8.6 %collective-permute-start.2 = (bf16[16,1792]{1,0:T(8,128)(2,1)S(1)}, bf16[16,1792]{1,0:T(8,128)(2,1)S(1)}, u32[]{:S(2)}, u32[]{:S(2)}) collective-permute-start(bf16[16,1792]{1,0:T(8,128)(2,1)S(1)} %get-tuple-element.38.refs_2_), channel_id=1, source_target_pairs={{0,16},{8,24},{16,0},{24,8},{1,17},{9,25},{17,1},{25,9},{2,18},{10... | collective-permute-start | bytes 172040 | tf_op jit(solution)/shard_map/ppermute | solution.py:344
  10.8 7.0 %collective-permute-start.3 = (bf16[16,1792]{1,0:T(8,128)(2,1)S(1)}, bf16[16,1792]{1,0:T(8,128)(2,1)S(1)}, u32[]{:S(2)}, u32[]{:S(2)}) collective-permute-start(bf16[16,1792]{1,0:T(8,128)(2,1)S(1)} %get-tuple-element.39.refs_3_), channel_id=1, source_target_pairs={{0,24},{8,16},{16,8},{24,0},{1,25},{9,17},{17,9},{25,1},{2,26},{10... | collective-permute-start | bytes 172040 | tf_op jit(solution)/shard_map/ppermute | solution.py:344
  11.3 6.6 %slice-start.4 = ((s8[10485760]{0:T(1024)(128)(4,1)}), s8[2097152]{0:T(1024)(128)(4,1)S(1)}, s32[]{:S(2)}) async-start(s8[10485760]{0:T(1024)(128)(4,1)} %bitcast.6), calls=%async_computation.4 | async-start | bytes 4194304
  13.4 8.0 %copy-start.1 = (f32[2048]{0:T(1024)S(1)}, f32[2048]{0:T(1024)}, u32[]{:S(2)}) copy-start(f32[2048]{0:T(1024)} %param.15) | copy-start | bytes 24580
  13.4 8.0 %copy-start.2 = (f32[2048]{0:T(1024)S(1)}, f32[2048]{0:T(1024)}, u32[]{:S(2)}) copy-start(f32[2048]{0:T(1024)} %param.11) | copy-start | bytes 24580
  13.5 17.2 %collective-permute-start.10 = (bf16[256,512]{1,0:T(8,128)(2,1)S(1)}, bf16[256,512]{1,0:T(8,128)(2,1)S(1)}, u32[]{:S(2)}, u32[]{:S(2)}) collective-permute-start(bf16[256,512]{1,0:T(8,128)(2,1)S(1)} %forward.1), channel_id=1, source_target_pairs={{0,2},{1,3},{2,0},{3,1},{4,6},{5,7},{6,4},{7,5},{8,10},{9,11},{10,... | collective-permute-start | bytes 786440 | tf_op jit(solution)/shard_map/ppermute | solution.py:344
  16.2 14.5 %collective-permute-start.11 = (bf16[256,512]{1,0:T(8,128)(2,1)S(1)}, bf16[256,512]{1,0:T(8,128)(2,1)S(1)}, u32[]{:S(2)}, u32[]{:S(2)}) collective-permute-start(bf16[256,512]{1,0:T(8,128)(2,1)S(1)} %get-tuple-element.64), channel_id=1, source_target_pairs={{0,1},{1,0},{2,3},{3,2},{4,5},{5,4},{6,7},{7,6},{8,9},{9,8},{10,11... | collective-permute-start | bytes 786440 | tf_op jit(solution)/shard_map/ppermute | solution.py:344
  20.0 1.4 %collective-permute-start.4 = (bf16[32,2048]{1,0:T(8,128)(2,1)S(1)}, bf16[32,2048]{1,0:T(8,128)(2,1)S(1)}, u32[]{:S(2)}, u32[]{:S(2)}) collective-permute-start(bf16[32,2048]{1,0:T(8,128)(2,1)S(1)} %get-tuple-element.43), channel_id=1, source_target_pairs={{0,4},{4,0},{1,5},{5,1},{2,6},{6,2},{3,7},{7,3},{8,12},{12,8},{9,1... | collective-permute-start | bytes 393224 | tf_op jit(solution)/shard_map/ppermute | solution.py:344
  23.3 7.4 %collective-permute-start.6 = (bf16[16,640]{1,0:T(8,128)(2,1)S(1)}, bf16[16,640]{1,0:T(8,128)(2,1)S(1)}, u32[]{:S(2)}, u32[]{:S(2)}) collective-permute-start(bf16[16,640]{1,0:T(8,128)(2,1)S(1)} %get-tuple-element.56), channel_id=1, source_target_pairs={{0,3},{1,2},{2,1},{3,0},{4,7},{5,6},{6,5},{7,4},{8,11},{9,10},{10,... | collective-permute-start | bytes 61448 | tf_op jit(solution)/shard_map/ppermute | solution.py:344
  24.4 6.3 %collective-permute-start.7 = (bf16[16,640]{1,0:T(8,128)(2,1)S(1)}, bf16[16,640]{1,0:T(8,128)(2,1)S(1)}, u32[]{:S(2)}, u32[]{:S(2)}) collective-permute-start(bf16[16,640]{1,0:T(8,128)(2,1)S(1)} %get-tuple-element.57), channel_id=1, source_target_pairs={{0,1},{1,0},{2,3},{3,2},{4,5},{5,4},{6,7},{7,6},{8,9},{9,8},{10,11... | collective-permute-start | bytes 61448 | tf_op jit(solution)/shard_map/ppermute | solution.py:344
  25.5 5.2 %collective-permute-start.8 = (bf16[16,640]{1,0:T(8,128)(2,1)S(1)}, bf16[16,640]{1,0:T(8,128)(2,1)S(1)}, u32[]{:S(2)}, u32[]{:S(2)}) collective-permute-start(bf16[16,640]{1,0:T(8,128)(2,1)S(1)} %get-tuple-element.58), channel_id=1, source_target_pairs={{0,2},{1,3},{2,0},{3,1},{4,6},{5,7},{6,4},{7,5},{8,10},{9,11},{10,... | collective-permute-start | bytes 61448 | tf_op jit(solution)/shard_map/ppermute | solution.py:344
